TPU v7x, 32 devices: a whole 2x2x4 slice. The times are simulated.
32 devices in a mesh: dp: 8 (over y, x, core), tensor: 4 (over z).
Axes of the slice: x: 2, y: 2, z: 4, core: 2. Of those that a mesh axis runs over, the one named last changes fastest.
Arguments:
- tokens: bfloat16 [64, 128, 1024], P('dp', 'tensor'), may hold values from -6 to 6
- enc_states: bfloat16 [64, 256, 1024], P('dp', 'tensor'), may hold values from -6 to 6
- cotangent: bfloat16 [64, 128, 1024], P('dp', 'tensor'), may hold values from -6 to 6
- tok_len: int32 [64], replicated, may hold values from 16 to 128, as said below
- enc_len: int32 [64], replicated, may hold values from 128 to 256, as said below
- deal: int32 [64], replicated, may hold values from 0 to 63, as said below
- w_q_self: bfloat16 [1024, 1024], P(None, 'tensor'), may hold values from -0.1875 to 0.1875
- w_k_self: bfloat16 [1024, 1024], P(None, 'tensor'), may hold values from -0.1875 to 0.1875
- w_v_self: bfloat16 [1024, 1024], P(None, 'tensor'), may hold values from -0.1875 to 0.1875
- w_o_self: bfloat16 [1024, 1024], P('tensor'), may hold values from -1 to 1
- w_q_cross: bfloat16 [1024, 1024], P(None, 'tensor'), may hold values from -0.1875 to 0.1875
- w_k_cross: bfloat16 [1024, 1024], P(None, 'tensor'), may hold values from -0.1875 to 0.1875
- w_v_cross: bfloat16 [1024, 1024], P(None, 'tensor'), may hold values from -0.1875 to 0.1875
- w_o_cross: bfloat16 [1024, 1024], P('tensor'), may hold values from -2 to 2
- w_in: bfloat16 [1024, 4096], P(None, 'tensor'), may hold values from -0.1875 to 0.1875
- w_out: bfloat16 [4096, 1024], P('tensor'), may hold values from -0.09375 to 0.09375
- norm_gain: float32 [3, 1024], replicated, may hold values from 0.5 to 1.5
- norm_bias: float32 [3, 1024], replicated, may hold values from -1.75 to 1.75
Outputs:
- result: bfloat16 [64, 128, 1024], P('dp', 'tensor')
- d_tokens: bfloat16 [64, 128, 1024], P('dp', 'tensor')
- encoder_state_gradient: bfloat16 [64, 256, 1024], P('dp', 'tensor')
- d_w_q_self: float32 [1024, 1024], P('dp', 'tensor')
- d_w_k_self: float32 [1024, 1024], P('dp', 'tensor')
- d_w_v_self: float32 [1024, 1024], P('dp', 'tensor')
- d_w_o_self: float32 [1024, 1024], P('tensor', 'dp')
- d_w_q_cross: float32 [1024, 1024], P('dp', 'tensor')
- d_w_k_cross: float32 [1024, 1024], P('dp', 'tensor')
- d_w_v_cross: float32 [1024, 1024], P('dp', 'tensor')
- d_w_o_cross: float32 [1024, 1024], P('tensor', 'dp')
- d_w_in: float32 [1024, 4096], P('dp', 'tensor')
- d_w_out: float32 [4096, 1024], P('tensor', 'dp')
- d_norm_gain: float32 [3, 1024], replicated
- d_norm_bias: float32 [3, 1024], replicated
Inputs may be any that keep to these rules, and one draw needn't show every extreme that they name: `tok_len`: some sequence has exactly 128 tokens. `enc_len`: some sequence has exactly 256 encoder states. deal is a permutation; deal[p] % 8 == p % 8; the 8 dealt positions of one index of dp hold sequences of 8 different indices of dp.
All inputs are finite; a program needn't handle non-finite values.
Results may differ from a plain program's by a relative error of at most 0.02.
Values may be sent and summed in bfloat16 or wider, within the bound.
A program may use at most 128 MiB of HBM per device.

v0:
```python
import math

import jax
import jax.numpy as jnp
from jax import lax
from jax.sharding import PartitionSpec as P

HEAD_DIM = 64


MASKED = -1e30
EPSILON = 1e-05


def select_rows(lookup, positions):
    matches = positions[:, None] == jnp.arange(lookup.shape[0], dtype=jnp.int32)[None, :]
    return jnp.sum(jnp.where(matches, lookup[None, :], 0), axis=1)


def route_rows(selector, value_entries):
    return jnp.einsum(
        "kj,jrd->krd", selector, value_entries, preferred_element_type=jnp.float32
    ).astype(jnp.bfloat16)


def project(value_entries, weight_matrix):
    return jnp.einsum(
        "nrw,wk->nrk", value_entries, weight_matrix, preferred_element_type=jnp.float32
    )


def project_back(value_entries, weight_matrix):
    return jnp.einsum(
        "azp,jp->azj", value_entries, weight_matrix, preferred_element_type=jnp.float32
    )


def weight_grad(left_operand, right_operand):
    return jnp.einsum(
        "jrm,jrw->mw", left_operand, right_operand, preferred_element_type=jnp.float32
    )


def silu_slope(pre_act):
    sigmoid_value = jax.nn.sigmoid(pre_act)
    return sigmoid_value * (1.0 + pre_act * (1.0 - sigmoid_value))


def norm_forward(value_entries, gain_row, bias_row):
    row_mean = jnp.mean(value_entries, axis=-1, keepdims=True)
    variance = jnp.mean(value_entries * value_entries, axis=-1, keepdims=True) - row_mean * row_mean
    inverse_std = lax.rsqrt(variance + EPSILON)
    normed = (value_entries - row_mean) * inverse_std
    return (normed * gain_row + bias_row, normed, inverse_std)


def norm_backward(grad_out, normed, inverse_std, gain_row):
    scaled = grad_out * gain_row
    grad_in = inverse_std * (
        scaled
        - jnp.mean(scaled, axis=-1, keepdims=True)
        - normed * jnp.mean(scaled * normed, axis=-1, keepdims=True)
    )
    return (grad_in, jnp.sum(grad_out * normed, axis=(0, 1)), jnp.sum(grad_out, axis=(0, 1)))


def block_allowed(row_start, block_rows, key_total, key_limit, causal):
    key_pos = jnp.arange(key_total, dtype=jnp.int32)
    allowed = jnp.broadcast_to(key_pos[None, :] < key_limit, (block_rows, key_total))
    if causal:
        row_pos = row_start + jnp.arange(block_rows, dtype=jnp.int32)
        allowed = allowed & (key_pos[None, :] <= row_pos[:, None])
    return allowed


def split_heads(value_entries):
    return value_entries.reshape(
        value_entries.shape[0], value_entries.shape[1] // HEAD_DIM, HEAD_DIM
    )


def attend_forward(queries, key_rows, value_rows, key_limit, causal):
    score_scale = 1.0 / math.sqrt(HEAD_DIM)
    seq_rows = queries.shape[0]
    block_rows = min(512, seq_rows)
    key_heads = split_heads(key_rows)
    value_heads = split_heads(value_rows)
    outputs = []
    totals = []
    for row_start in range(0, seq_rows, block_rows):
        query_heads = split_heads(queries[row_start : row_start + block_rows])
        allowed = block_allowed(row_start, block_rows, key_rows.shape[0], key_limit, causal)
        raw_scores = jnp.einsum(
            "qhd,khd->hqk", query_heads, key_heads, preferred_element_type=jnp.float32
        )
        scores = jnp.where(allowed[None], raw_scores * score_scale, MASKED)
        row_max = jnp.max(scores, axis=-1, keepdims=True)
        shifted = jnp.exp(scores - row_max)
        row_total = jnp.sum(shifted, axis=-1, keepdims=True)
        weights = (shifted / row_total).astype(jnp.bfloat16)
        output = jnp.einsum(
            "hqk,khd->qhd", weights, value_heads, preferred_element_type=jnp.float32
        )
        outputs.append(output.reshape(block_rows, -1).astype(jnp.bfloat16))
        totals.append((row_max + jnp.log(row_total))[:, :, 0])
    return (jnp.concatenate(outputs, axis=0), jnp.concatenate(totals, axis=1))


def attend_backward(queries, key_rows, value_rows, grad_out, log_total, key_limit, causal):
    score_scale = 1.0 / math.sqrt(HEAD_DIM)
    seq_rows = queries.shape[0]
    block_rows = min(512, seq_rows)
    key_heads = split_heads(key_rows)
    value_heads = split_heads(value_rows)
    key_grad = jnp.zeros(key_heads.shape, jnp.float32)
    value_grad = jnp.zeros(value_heads.shape, jnp.float32)
    query_grads = []
    for row_start in range(0, seq_rows, block_rows):
        query_heads = split_heads(queries[row_start : row_start + block_rows])
        grad_heads = split_heads(grad_out[row_start : row_start + block_rows])
        allowed = block_allowed(row_start, block_rows, key_rows.shape[0], key_limit, causal)
        raw_scores = jnp.einsum(
            "qhd,khd->hqk", query_heads, key_heads, preferred_element_type=jnp.float32
        )
        scores = jnp.where(allowed[None], raw_scores * score_scale, MASKED)
        weights = jnp.exp(scores - log_total[:, row_start : row_start + block_rows, None])
        grad_weights = jnp.einsum(
            "qhd,khd->hqk", grad_heads, value_heads, preferred_element_type=jnp.float32
        )
        row_delta = jnp.sum(weights * grad_weights, axis=-1, keepdims=True)
        grad_scores = (weights * (grad_weights - row_delta) * score_scale).astype(jnp.bfloat16)
        query_grad = jnp.einsum(
            "hqk,khd->qhd", grad_scores, key_heads, preferred_element_type=jnp.float32
        )
        query_grads.append(query_grad.reshape(block_rows, -1).astype(jnp.bfloat16))
        key_grad = key_grad + jnp.einsum(
            "hqk,qhd->khd", grad_scores, query_heads, preferred_element_type=jnp.float32
        )
        value_grad = value_grad + jnp.einsum(
            "hqk,qhd->khd",
            weights.astype(jnp.bfloat16),
            grad_heads,
            preferred_element_type=jnp.float32,
        )
    key_shape = key_rows.shape
    return (
        jnp.concatenate(query_grads, axis=0),
        key_grad.reshape(key_shape).astype(jnp.bfloat16),
        value_grad.reshape(key_shape).astype(jnp.bfloat16),
    )


def attend_all(queries, key_rows, value_rows, limits, causal):
    return lax.map(
        lambda operands: attend_forward(*operands, causal), (queries, key_rows, value_rows, limits)
    )


def back_all(queries, key_rows, value_rows, grad_out, log_total, limits, causal):
    return lax.map(
        lambda operands: attend_backward(*operands, causal),
        (queries, key_rows, value_rows, grad_out, log_total, limits),
    )


def widen_rows(value_entries):
    return lax.all_gather(value_entries, "tensor", axis=1, tiled=True)


def narrow_rows(value_entries):
    return lax.psum_scatter(value_entries, "tensor", scatter_dimension=1, tiled=True)


def widen_grads(value_entries):
    return lax.all_gather(value_entries, "tensor", axis=1, tiled=True)


def narrow_grads(value_entries):
    return lax.psum_scatter(value_entries, "tensor", scatter_dimension=1, tiled=True)


def per_device(
    tokens,
    enc_states,
    cotangent,
    tok_len,
    enc_len,
    deal,
    w_q_self,
    w_k_self,
    w_v_self,
    w_o_self,
    w_q_cross,
    w_k_cross,
    w_v_cross,
    w_o_cross,
    w_in,
    w_out,
    norm_gain,
    norm_bias,
):
    dp_size = lax.axis_size("dp")
    dp_index = lax.axis_index("dp")
    tensor_index = lax.axis_index("tensor")
    seq_count = tokens.shape[0]
    local_rows = tokens.shape[1]
    all_seqs = jnp.arange(deal.shape[0], dtype=jnp.int32)
    my_slots = dp_index * seq_count + jnp.arange(seq_count, dtype=jnp.int32)
    sources = select_rows(deal, my_slots)
    targets = jnp.sum(jnp.where(deal[None, :] == my_slots[:, None], all_seqs[None, :], 0), axis=1)
    peer_ids = jnp.arange(dp_size, dtype=jnp.int32)
    outward = (targets[None, :] // seq_count == peer_ids[:, None]).astype(jnp.bfloat16)
    inward = (sources[:, None] // seq_count == peer_ids[None, :]).astype(jnp.bfloat16)
    got_tokens, received_states = (
        lax.all_to_all(route_rows(outward, tokens), "dp", split_axis=0, concat_axis=0, tiled=True),
        lax.all_to_all(
            route_rows(outward, enc_states), "dp", split_axis=0, concat_axis=0, tiled=True
        ),
    )
    tokens_here = route_rows(inward, got_tokens)
    states_here = route_rows(inward, received_states)
    sequence_lengths = select_rows(tok_len, sources)
    limits = select_rows(enc_len, sources)
    positions = tensor_index * local_rows + jnp.arange(local_rows, dtype=jnp.int32)
    row_mask = (positions[None, :] < sequence_lengths[:, None]).astype(jnp.float32)[:, :, None]
    tokens_wide = tokens_here.astype(jnp.float32)
    normed_one, unit_one, scale_one = norm_forward(tokens_wide, norm_gain[0], norm_bias[0])
    full_one = widen_rows(normed_one.astype(jnp.bfloat16))
    query_one = project(full_one, w_q_self).astype(jnp.bfloat16)
    key_one = project(full_one, w_k_self).astype(jnp.bfloat16)
    value_one = project(full_one, w_v_self).astype(jnp.bfloat16)
    attended_one, totals_one = attend_all(query_one, key_one, value_one, sequence_lengths, True)
    hidden_one = tokens_wide + narrow_rows(project(attended_one, w_o_self))
    normed_two, unit_two, second_scale = norm_forward(hidden_one, norm_gain[1], norm_bias[1])
    full_two = widen_rows(normed_two.astype(jnp.bfloat16))
    states_full = widen_rows(states_here)
    query_two = project(full_two, w_q_cross).astype(jnp.bfloat16)
    key_two = project(states_full, w_k_cross).astype(jnp.bfloat16)
    value_two = project(states_full, w_v_cross).astype(jnp.bfloat16)
    attended_two, totals_two = attend_all(query_two, key_two, value_two, limits, False)
    hidden_two = hidden_one + narrow_rows(project(attended_two, w_o_cross))
    normed_three, unit_three, scale_three = norm_forward(hidden_two, norm_gain[2], norm_bias[2])
    full_three = widen_rows(normed_three.astype(jnp.bfloat16))
    pre_act = project(full_three, w_in)
    activated = jax.nn.silu(pre_act).astype(jnp.bfloat16)
    branch_out = narrow_rows(project(activated, w_out))
    result = ((hidden_two + branch_out) * row_mask).astype(jnp.bfloat16)
    grad_out = cotangent.astype(jnp.float32) * row_mask
    grad_low = grad_out.astype(jnp.bfloat16)
    grad_full = widen_grads(grad_low)
    grad_act = project_back(grad_full, w_out)
    grad_pre = (grad_act * silu_slope(pre_act)).astype(jnp.bfloat16)
    grad_w_out = weight_grad(activated, grad_full)
    grad_w_in = weight_grad(full_three, grad_pre)
    grad_three = narrow_grads(project_back(grad_pre, w_in))
    grad_norm_three, gain_three, bias_three = norm_backward(
        grad_three, unit_three, scale_three, norm_gain[2]
    )
    grad_hidden_two = grad_out + grad_norm_three
    grad_two_full = widen_grads(grad_hidden_two.astype(jnp.bfloat16))
    grad_w_o_cross = weight_grad(attended_two, grad_two_full)
    grad_attended_two = project_back(grad_two_full, w_o_cross).astype(jnp.bfloat16)
    grad_query_two, grad_key_two, grad_value_two = back_all(
        query_two, key_two, value_two, grad_attended_two, totals_two, limits, False
    )
    grad_w_q_cross = weight_grad(full_two, grad_query_two)
    grad_w_k_cross = weight_grad(states_full, grad_key_two)
    grad_w_v_cross = weight_grad(states_full, grad_value_two)
    grad_states = narrow_grads(
        project_back(grad_key_two, w_k_cross) + project_back(grad_value_two, w_v_cross)
    )
    grad_norm_two_in = narrow_grads(project_back(grad_query_two, w_q_cross))
    grad_norm_two, gain_two, bias_two = norm_backward(
        grad_norm_two_in, unit_two, second_scale, norm_gain[1]
    )
    grad_hidden_one = grad_hidden_two + grad_norm_two
    grad_one_full = widen_grads(grad_hidden_one.astype(jnp.bfloat16))
    grad_w_o_self = weight_grad(attended_one, grad_one_full)
    grad_attended_one = project_back(grad_one_full, w_o_self).astype(jnp.bfloat16)
    grad_query_one, grad_key_one, grad_value_one = back_all(
        query_one, key_one, value_one, grad_attended_one, totals_one, sequence_lengths, True
    )
    grad_w_q_self = weight_grad(full_one, grad_query_one)
    grad_w_k_self = weight_grad(full_one, grad_key_one)
    grad_w_v_self = weight_grad(full_one, grad_value_one)
    grad_norm_one_in = narrow_grads(
        project_back(grad_query_one, w_q_self)
        + project_back(grad_key_one, w_k_self)
        + project_back(grad_value_one, w_v_self)
    )
    grad_norm_one, gain_one, bias_one = norm_backward(
        grad_norm_one_in, unit_one, scale_one, norm_gain[0]
    )
    grad_tokens_here = grad_hidden_one + grad_norm_one
    back_tokens, back_states = (
        lax.all_to_all(
            route_rows(inward.T, grad_tokens_here.astype(jnp.bfloat16)),
            "dp",
            split_axis=0,
            concat_axis=0,
            tiled=True,
        ),
        lax.all_to_all(
            route_rows(inward.T, grad_states.astype(jnp.bfloat16)),
            "dp",
            split_axis=0,
            concat_axis=0,
            tiled=True,
        ),
    )
    d_tokens = route_rows(outward.T, back_tokens)
    d_states = route_rows(outward.T, back_states)
    gain_sum, bias_sum = lax.psum(
        (jnp.stack([gain_one, gain_two, gain_three]), jnp.stack([bias_one, bias_two, bias_three])),
        ("dp", "tensor"),
    )
    (
        sum_q_self,
        sum_k_self,
        sum_v_self,
        sum_o_self,
        sum_q_cross,
        sum_k_cross,
        sum_v_cross,
        sum_o_cross,
        sum_in,
        sum_out,
    ) = (
        lax.psum_scatter(
            grad_w_q_self.astype(jnp.bfloat16), "dp", scatter_dimension=0, tiled=True
        ).astype(jnp.float32),
        lax.psum_scatter(
            grad_w_k_self.astype(jnp.bfloat16), "dp", scatter_dimension=0, tiled=True
        ).astype(jnp.float32),
        lax.psum_scatter(
            grad_w_v_self.astype(jnp.bfloat16), "dp", scatter_dimension=0, tiled=True
        ).astype(jnp.float32),
        lax.psum_scatter(
            grad_w_o_self.astype(jnp.bfloat16), "dp", scatter_dimension=1, tiled=True
        ).astype(jnp.float32),
        lax.psum_scatter(
            grad_w_q_cross.astype(jnp.bfloat16), "dp", scatter_dimension=0, tiled=True
        ).astype(jnp.float32),
        lax.psum_scatter(
            grad_w_k_cross.astype(jnp.bfloat16), "dp", scatter_dimension=0, tiled=True
        ).astype(jnp.float32),
        lax.psum_scatter(
            grad_w_v_cross.astype(jnp.bfloat16), "dp", scatter_dimension=0, tiled=True
        ).astype(jnp.float32),
        lax.psum_scatter(
            grad_w_o_cross.astype(jnp.bfloat16), "dp", scatter_dimension=1, tiled=True
        ).astype(jnp.float32),
        lax.psum_scatter(
            grad_w_in.astype(jnp.bfloat16), "dp", scatter_dimension=0, tiled=True
        ).astype(jnp.float32),
        lax.psum_scatter(
            grad_w_out.astype(jnp.bfloat16), "dp", scatter_dimension=1, tiled=True
        ).astype(jnp.float32),
    )
    return (
        result,
        d_tokens,
        d_states,
        sum_q_self,
        sum_k_self,
        sum_v_self,
        sum_o_self,
        sum_q_cross,
        sum_k_cross,
        sum_v_cross,
        sum_o_cross,
        sum_in,
        sum_out,
        gain_sum,
        bias_sum,
    )


def solution(mesh):
    placed = (
        P("dp", "tensor", None),
        P("dp", "tensor", None),
        P("dp", "tensor", None),
        P(),
        P(),
        P(),
        P(None, "tensor"),
        P(None, "tensor"),
        P(None, "tensor"),
        P("tensor", None),
        P(None, "tensor"),
        P(None, "tensor"),
        P(None, "tensor"),
        P("tensor", None),
        P(None, "tensor"),
        P("tensor", None),
        P(),
        P(),
    )
    return jax.shard_map(
        per_device,
        mesh=mesh,
        in_specs=placed,
        out_specs=(
            P("dp", "tensor", None),
            P("dp", "tensor", None),
            P("dp", "tensor", None),
            P("dp", "tensor"),
            P("dp", "tensor"),
            P("dp", "tensor"),
            P("tensor", "dp"),
            P("dp", "tensor"),
            P("dp", "tensor"),
            P("dp", "tensor"),
            P("tensor", "dp"),
            P("dp", "tensor"),
            P("tensor", "dp"),
            P(),
            P(),
        ),
        check_vma=False,
    )
```

profile of v0, /device:TPU:0, one launch (start us, length us, event | category | flops | bytes accessed | tf_op | source)
XLA Modules:
  0.0 1676.6 jit_solution(1027753458709127056)
XLA Ops:
  10.9 5.3 all-to-all-start
  16.3 9.6 all-to-all-done
  28.6 45.2 %all-gather.8.cloned.1.call-done = bf16[8,128,1024]{2,0,1:T(8,128)(2,1)} async-done(((bf16[8,32,1024]{2,0,1:T(8,128)(2,1)}), bf16[8,128,1024]{2,0,1:T(8,128)(2,1)}) %all-gather.8.cloned.1.call-update) | async-done | bytes 2097168 | tf_op jit(solution)/shard_map/all_gather | solution.py:167
  73.8 4.8 fusion.100
  79.9 4.0 fusion.103
  85.0 4.8 fusion.97
  92.0 26.9 %while.52 = (s32[]{:T(128)}, bf16[8,128,256]{1,2,0:T(8,128)(2,1)}, f32[8,4,128]{2,1,0:T(4,128)S(1)}, bf16[8,128,256]{1,2,0:T(8,128)(2,1)S(1)}, s32[8]{0:T(128)S(...) while((s32[]{:T(128)}, bf16[8,128,256]{1,2,0:T(8,128)(2,1)}, ...), condition=%wide.region_8.9_spmd, body=%wide.region_5.8_spmd.sunk | while | flops 17366656 | bytes 1622397 | solution.py:154
  118.9 2.6 copy.318
  121.5 3.9 fusion.153
  128.0 18.8 %all_to_all.20 = bf16[8,64,1024]{2,1,0:T(8,128)(2,1)S(1)} all-to-all(bf16[8,64,1024]{2,1,0:T(8,128)(2,1)S(1)} %copy.256), channel_id=1, replica_groups=mesh['dp'=8,'tensor'=4] {'dp'}, dimensions={0} | all-to-all | bytes 2097152 | tf_op jit(solution)/shard_map/all_to_all | solution.py:216
  148.6 52.5 %reduce-scatter.24.cloned.1.call-done = f32[8,32,1024]{2,0,1:T(8,128)} async-done(((f32[8,128,1024]{2,0,1:T(8,128)}), f32[8,32,1024]{2,0,1:T(8,128)}) %reduce-scatter.24.cloned.1.call-update) | async-done | bytes 1048592 | tf_op jit(solution)/shard_map/reduce_scatter | solution.py:171
  203.8 80.8 %all-gather.10.cloned.1.call-done = bf16[8,256,1024]{2,0,1:T(8,128)(2,1)} async-done(((bf16[8,64,1024]{2,0,1:T(8,128)(2,1)}), bf16[8,256,1024]{2,0,1:T(8,128)(2,1)}) %all-gather.10.cloned.1.call-update) | async-done | bytes 4194320 | tf_op jit(solution)/shard_map/all_gather | solution.py:167
  284.6 8.0 fusion.82
  292.6 2.7 copy.264
  295.3 8.0 fusion.79
  305.6 25.6 %all-gather.12.cloned.1.call-done = bf16[8,128,1024]{2,0,1:T(8,128)(2,1)} async-done(((bf16[8,32,1024]{2,0,1:T(8,128)(2,1)}), bf16[8,128,1024]{2,0,1:T(8,128)(2,1)}) %all-gather.12.cloned.1.call-update) | async-done | bytes 2097168 | tf_op jit(solution)/shard_map/all_gather | solution.py:167
  331.2 4.8 fusion.112
  338.9 37.7 %while.53 = (s32[]{:T(128)}, bf16[8,128,256]{1,2,0:T(8,128)(2,1)}, f32[8,4,128]{2,1,0:T(4,128)S(1)}, bf16[8,256,256]{1,2,0:T(8,128)(2,1)}, s32[8]{0:T(128)S(1)},...) while((s32[]{:T(128)}, bf16[8,128,256]{1,2,0:T(8,128)(2,1)}, ...), condition=%wide.region_16.17_spmd, body=%wide.region_13.16_spmd.sunk | while | flops 34635520 | bytes 2769533 | solution.py:154
  378.9 3.9 fusion.142
  382.8 75.5 %reduce-scatter.26.cloned.1.call-done = f32[8,32,1024]{2,0,1:T(8,128)} async-done(((f32[8,128,1024]{2,0,1:T(8,128)}), f32[8,32,1024]{2,0,1:T(8,128)}) %reduce-scatter.26.cloned.1.call-update) | async-done | bytes 1048592 | tf_op jit(solution)/shard_map/reduce_scatter | solution.py:171
  464.5 44.0 %all-gather.14.cloned.1.call-done = bf16[8,128,1024]{2,0,1:T(8,128)(2,1)} async-done(((bf16[8,32,1024]{2,0,1:T(8,128)(2,1)}), bf16[8,128,1024]{2,0,1:T(8,128)(2,1)}) %all-gather.14.cloned.1.call-update) | async-done | bytes 2097168 | tf_op jit(solution)/shard_map/all_gather | solution.py:167
  508.5 8.3 multiply_convert_fusion.1
  516.9 37.9 %all-gather.16.cloned.1.call-done = bf16[8,128,1024]{2,0,1:T(8,128)(2,1)} async-done(((bf16[8,32,1024]{2,0,1:T(8,128)(2,1)}), bf16[8,128,1024]{2,0,1:T(8,128)(2,1)}) %all-gather.16.cloned.1.call-update) | async-done | bytes 2097168 | tf_op jit(solution)/shard_map/all_gather | solution.py:175
  554.8 7.9 multiply_convert_fusion
  564.0 4.6 fusion.53
  568.7 75.6 %reduce-scatter.30.cloned.1.call-done = f32[8,32,1024]{2,0,1:T(8,128)} async-done(((f32[8,128,1024]{2,0,1:T(8,128)}), f32[8,32,1024]{2,0,1:T(8,128)}) %reduce-scatter.30.cloned.1.call-update) | async-done | bytes 1048592 | tf_op jit(solution)/shard_map/reduce_scatter | solution.py:179
  649.4 46.3 %all-gather.18.cloned.1.call-done = bf16[8,128,1024]{2,0,1:T(8,128)(2,1)} async-done(((bf16[8,32,1024]{2,0,1:T(8,128)(2,1)}), bf16[8,128,1024]{2,0,1:T(8,128)(2,1)}) %all-gather.18.cloned.1.call-update) | async-done | bytes 2097168 | tf_op jit(solution)/shard_map/all_gather | solution.py:175
  695.7 4.9 fusion.106
  701.4 87.3 %while.54 = (s32[]{:T(128)}, bf16[8,128,256]{1,2,0:T(8,128)(2,1)}, bf16[8,256,256]{1,2,0:T(8,128)(2,1)}, bf16[8,256,256]{1,2,0:T(8,128)(2,1)}, bf16[8,256,256]{1...) while((s32[]{:T(128)}, bf16[8,128,256]{1,2,0:T(8,128)(2,1)}, ...), condition=%wide.region_26.27_spmd, body=%wide.region_24.26_spmd.sunk | while | flops 85886720 | bytes 6232737 | solution.py:160
  790.2 3.9 fusion.147
  794.2 6.8 fusion.51
  801.1 68.7 %reduce-scatter.32.cloned.1.call-done = f32[8,32,1024]{2,0,1:T(8,128)} async-done(((f32[8,128,1024]{2,0,1:T(8,128)}), f32[8,32,1024]{2,0,1:T(8,128)}) %reduce-scatter.32.cloned.1.call-update) | async-done | bytes 1048592 | tf_op jit(solution)/shard_map/reduce_scatter | solution.py:179
  872.1 77.3 %reduce-scatter.28.cloned.1.call-done = f32[8,32,1024]{2,0,1:T(8,128)} async-done(((f32[8,128,1024]{2,0,1:T(8,128)}), f32[8,32,1024]{2,0,1:T(8,128)}) %reduce-scatter.28.cloned.1.call-update) | async-done | bytes 1048592 | tf_op jit(solution)/shard_map/reduce_scatter | solution.py:171
  949.4 4.0 fusion.192
  953.9 6.1 bitcast_convert_fusion
  960.0 2.6 copy.352
  964.2 5.5 bitcast_convert_fusion.1
  970.8 4.1 fusion.94
  976.0 3.4 fusion.120
  980.7 4.9 fusion.116
  986.6 4.8 fusion.115
  991.5 8.5 all-gather.20.cloned.1.call-done
  1000.0 4.8 fusion.109
  1005.8 58.8 %while.55 = (s32[]{:T(128)}, bf16[8,128,256]{1,2,0:T(8,128)(2,1)}, bf16[8,128,256]{1,2,0:T(8,128)(2,1)S(1)}, bf16[8,128,256]{1,2,0:T(8,128)(2,1)S(1)}, bf16[8,12...) while((s32[]{:T(128)}, bf16[8,128,256]{1,2,0:T(8,128)(2,1)}, ...), condition=%wide.region_32.33_spmd, body=%wide.region_30.32_spmd.sunk | while | flops 42993024 | bytes 3578273 | solution.py:160
  1064.7 4.5 fusion.91
  1070.7 3.4 fusion.118
  1074.7 3.4 fusion.117
  1078.6 3.5 fusion.119
  1082.1 2.5 fusion.144
  1084.6 4.6 convolution_add_fusion
  1092.2 2.8 add_add_fusion
  1098.9 26.7 %reduce-scatter.54.cloned.1.call-done = bf16[128,256]{1,0:T(8,128)(2,1)} async-done(((bf16[1024,256]{1,0:T(8,128)(2,1)}), bf16[128,256]{1,0:T(8,128)(2,1)}) %reduce-scatter.54.cloned.1.call-update) | async-done | bytes 65552
  1127.2 35.5 %reduce-scatter.44.cloned.1.call-done = bf16[128,256]{1,0:T(8,128)(2,1)} async-done(((bf16[1024,256]{1,0:T(8,128)(2,1)}), bf16[128,256]{1,0:T(8,128)(2,1)}) %reduce-scatter.44.cloned.1.call-update) | async-done | bytes 65552 | tf_op jit(solution)/shard_map/reduce_scatter | solution.py:341
  1164.1 35.9 %reduce-scatter.48.cloned.1.call-done = bf16[128,256]{1,0:T(8,128)(2,1)} async-done(((bf16[1024,256]{1,0:T(8,128)(2,1)}), bf16[128,256]{1,0:T(8,128)(2,1)}) %reduce-scatter.48.cloned.1.call-update) | async-done | bytes 65552 | tf_op jit(solution)/shard_map/reduce_scatter | solution.py:347
  1201.5 35.6 %reduce-scatter.46.cloned.1.call-done = bf16[128,256]{1,0:T(8,128)(2,1)} async-done(((bf16[1024,256]{1,0:T(8,128)(2,1)}), bf16[128,256]{1,0:T(8,128)(2,1)}) %reduce-scatter.46.cloned.1.call-update) | async-done | bytes 65552 | tf_op jit(solution)/shard_map/reduce_scatter | solution.py:344
  1239.7 35.0 %reduce-scatter.52.cloned.1.call-done = bf16[128,256]{1,0:T(8,128)(2,1)} async-done(((bf16[1024,256]{1,0:T(8,128)(2,1)}), bf16[128,256]{1,0:T(8,128)(2,1)}) %reduce-scatter.52.cloned.1.call-update) | async-done | bytes 65552
  1276.3 36.0 %reduce-scatter.40.cloned.1.call-done = bf16[128,256]{1,0:T(8,128)(2,1)} async-done(((bf16[1024,256]{1,0:T(8,128)(2,1)}), bf16[128,256]{1,0:T(8,128)(2,1)}) %reduce-scatter.40.cloned.1.call-update) | async-done | bytes 65552 | tf_op jit(solution)/shard_map/reduce_scatter | solution.py:332
  1313.8 36.6 %reduce-scatter.38.cloned.1.call-done = bf16[128,256]{1,0:T(8,128)(2,1)} async-done(((bf16[1024,256]{1,0:T(8,128)(2,1)}), bf16[128,256]{1,0:T(8,128)(2,1)}) %reduce-scatter.38.cloned.1.call-update) | async-done | bytes 65552 | tf_op jit(solution)/shard_map/reduce_scatter | solution.py:329
  1351.9 35.7 %reduce-scatter.42.cloned.1.call-done = bf16[128,256]{1,0:T(8,128)(2,1)} async-done(((bf16[1024,256]{1,0:T(8,128)(2,1)}), bf16[128,256]{1,0:T(8,128)(2,1)}) %reduce-scatter.42.cloned.1.call-update) | async-done | bytes 65552 | tf_op jit(solution)/shard_map/reduce_scatter | solution.py:335
  1389.2 145.5 %reduce-scatter.36.cloned.1.call-done = f32[8,64,1024]{2,1,0:T(8,128)} async-done(((f32[8,256,1024]{2,1,0:T(8,128)}), f32[8,64,1024]{2,1,0:T(8,128)}) %reduce-scatter.36.cloned.1.call-update) | async-done | bytes 2097168 | tf_op jit(solution)/shard_map/reduce_scatter | solution.py:179
  1538.7 3.8 all-to-all-start.3
  1542.5 71.9 %reduce-scatter.34.cloned.1.call-done = f32[8,32,1024]{2,0,1:T(8,128)} async-done(((f32[8,128,1024]{2,0,1:T(8,128)}), f32[8,32,1024]{2,0,1:T(8,128)}) %reduce-scatter.34.cloned.1.call-update) | async-done | bytes 1048592 | tf_op jit(solution)/shard_map/reduce_scatter | solution.py:179
  1617.9 4.4 all-to-all-start.2
  1624.7 42.0 %all-reduce = (f32[3,1024]{1,0:T(4,128)}, f32[3,1024]{1,0:T(4,128)}) all-reduce(f32[3,1024]{1,0:T(4,128)S(1)} %pad_maximum_fusion, f32[3,1024]{1,0:T(4,128)S(1)} %pad_maximum_fusion.1), channel_id=1, replica_groups=mesh['dp'=8,'tensor'=4] {'dp','tensor'}, use_global_device_ids=true, to_apply=%region_50.51 | all-reduce | flops 6144 | bytes 49152 | tf_op jit(solution)/shard_map/psum | solution.py:313
  (645 shorter events, 294.6 us)
Async XLA Ops:
  7.2 501.3 %copy-start = (bf16[1024,1024]{1,0:T(8,128)(2,1)S(1)}, bf16[1024,1024]{1,0:T(8,128)(2,1)}, u32[]{:S(2)}) copy-start(bf16[1024,1024]{1,0:T(8,128)(2,1)} %param.40) | copy-start | bytes 6291460
  7.2 9.1 copy-start.42
  7.2 9.1 copy-start.43
  8.3 117.4 %copy-start.44 = (s32[8]{0:T(128)}, s32[8]{0:T(128)S(1)}, u32[]{:S(2)}) copy-start(s32[8]{0:T(128)S(1)} %and_select_fusion) | copy-start | bytes 100
  10.9 17.5 %copy-start.50 = (s32[64]{0:T(128)S(1)}, s32[64]{0:T(128)}, u32[]{:S(2)}) copy-start(s32[64]{0:T(128)} %param.30) | copy-start | bytes 772
  10.9 17.5 %copy-start.51 = (s32[64]{0:T(128)S(1)}, s32[64]{0:T(128)}, u32[]{:S(2)}) copy-start(s32[64]{0:T(128)} %param.29) | copy-start | bytes 772
  10.9 62.9 %copy-start.27 = (bf16[1024,256]{1,0:T(8,128)(2,1)S(1)}, bf16[1024,256]{1,0:T(8,128)(2,1)}, u32[]{:S(2)}) copy-start(bf16[1024,256]{1,0:T(8,128)(2,1)} %param.32) | copy-start | bytes 1572868
  10.9 15.0 all-to-all-start
  16.2 57.6 %all-gather.8.cloned.1.call-start = ((), (), s32[]{:S(2)}) async-start(), calls=%async_computation.21 | async-start | bytes 2621440 | tf_op jit(solution)/shard_map/all_gather | solution.py:167
  16.3 130.5 %copy-start.46 = (s32[8]{0:T(128)}, s32[8]{0:T(128)S(1)}, u32[]{:S(2)}) copy-start(s32[8]{0:T(128)S(1)} %and_select_fusion.1) | copy-start | bytes 100
  16.3 62.3 %copy-start.35 = (f32[1,1024]{1,0:T(1,128)}, f32[1,1024]{1,0:T(1,128)S(1)}, u32[]{:S(2)}) copy-start(f32[1,1024]{1,0:T(1,128)S(1)} %get-tuple-element.517) | copy-start | bytes 12292
  28.4 172.7 %reduce-scatter.24.cloned.1.call-start = ((), (), s32[]{:S(2)}) async-start(), calls=%async_computation.22 | async-start | bytes 5242880 | tf_op jit(solution)/shard_map/reduce_scatter | solution.py:171
  118.9 6.5 copy-start.13
  118.9 6.5 copy-start.14
  118.9 6.5 copy-start.37
  118.9 343.1 %copy-start.48 = (s32[8]{0:T(128)}, s32[8]{0:T(128)S(1)}, u32[]{:S(2)}) copy-start(s32[8]{0:T(128)S(1)} %get-tuple-element.975) | copy-start | bytes 100
  125.4 159.2 %all-gather.10.cloned.1.call-start = ((), (), s32[]{:S(2)}) async-start(), calls=%async_computation.23 | async-start | bytes 5242880 | tf_op jit(solution)/shard_map/all_gather | solution.py:167
  148.5 182.6 %all-gather.12.cloned.1.call-start = ((), (), s32[]{:S(2)}) async-start(), calls=%async_computation.24 | async-start | bytes 2621440 | tf_op jit(solution)/shard_map/all_gather | solution.py:167
  203.7 254.6 %reduce-scatter.26.cloned.1.call-start = ((), (), s32[]{:S(2)}) async-start(), calls=%async_computation.25 | async-start | bytes 5242880 | tf_op jit(solution)/shard_map/reduce_scatter | solution.py:171
  382.8 125.7 %all-gather.14.cloned.1.call-start = ((), (), s32[]{:S(2)}) async-start(), calls=%async_computation.26 | async-start | bytes 2621440 | tf_op jit(solution)/shard_map/all_gather | solution.py:167
  461.9 92.9 %all-gather.16.cloned.1.call-start = ((), (), s32[]{:S(2)}) async-start(), calls=%async_computation.28 | async-start | bytes 2621440 | tf_op jit(solution)/shard_map/all_gather | solution.py:175
  464.3 179.9 %reduce-scatter.30.cloned.1.call-start = ((), (), s32[]{:S(2)}) async-start(), calls=%async_computation.29 | async-start | bytes 5242880 | tf_op jit(solution)/shard_map/reduce_scatter | solution.py:179
  568.6 75.7 %copy-start.3 = (f32[8,32,1024]{2,0,1:T(8,128)S(1)}, f32[8,32,1024]{2,0,1:T(8,128)}, u32[]{:S(2)}) copy-start(f32[8,32,1024]{2,0,1:T(8,128)} %copy-done.2) | copy-start | bytes 3145732
  568.6 127.1 %all-gather.18.cloned.1.call-start = ((), (), s32[]{:S(2)}) async-start(), calls=%async_computation.30 | async-start | bytes 2621440 | tf_op jit(solution)/shard_map/all_gather | solution.py:175
  644.2 2.4 copy-start.4
  649.1 220.7 %reduce-scatter.32.cloned.1.call-start = ((), (), s32[]{:S(2)}) async-start(), calls=%async_computation.31 | async-start | bytes 5242880 | tf_op jit(solution)/shard_map/reduce_scatter | solution.py:179
  790.2 4.0 copy-start.16
  794.1 155.2 %reduce-scatter.28.cloned.1.call-start = ((), (), s32[]{:S(2)}) async-start(), calls=%async_computation.27 | async-start | bytes 5242880 | tf_op jit(solution)/shard_map/reduce_scatter | solution.py:171
  801.0 148.4 %copy-start.5 = (f32[8,32,1024]{2,0,1:T(8,128)S(1)}, f32[8,32,1024]{2,0,1:T(8,128)}, u32[]{:S(2)}) copy-start(f32[8,32,1024]{2,0,1:T(8,128)} %reduce-scatter.30.cloned.1.call-done) | copy-start | bytes 3145732
  801.0 199.0 %all-gather.20.cloned.1.call-start = ((), (), s32[]{:S(2)}) async-start(), calls=%async_computation.32 | async-start | bytes 2621440 | tf_op jit(solution)/shard_map/all_gather | solution.py:175
  953.4 141.6 %reduce-scatter.56.cloned.1.call-start = ((), (), s32[]{:S(2)}) async-start(), calls=%async_computation.44 | async-start | bytes 2359296
  962.6 134.4 %reduce-scatter.50.cloned.1.call-start = ((), (), s32[]{:S(2)}) async-start(), calls=%async_computation.41 | async-start | bytes 2359296 | tf_op jit(solution)/shard_map/reduce_scatter | solution.py:353
  969.7 6.2 copy-start.17
  969.7 155.8 %reduce-scatter.54.cloned.1.call-start = ((), (), s32[]{:S(2)}) async-start(), calls=%async_computation.43 | async-start | bytes 589824
  975.9 3.5 copy-start.8
  975.9 186.7 %reduce-scatter.44.cloned.1.call-start = ((), (), s32[]{:S(2)}) async-start(), calls=%async_computation.38 | async-start | bytes 589824 | tf_op jit(solution)/shard_map/reduce_scatter | solution.py:341
  980.4 5.1 copy-start.10
  980.4 219.6 %reduce-scatter.48.cloned.1.call-start = ((), (), s32[]{:S(2)}) async-start(), calls=%async_computation.40 | async-start | bytes 589824 | tf_op jit(solution)/shard_map/reduce_scatter | solution.py:347
  986.6 13.5 copy-start.25
  986.6 250.5 %reduce-scatter.46.cloned.1.call-start = ((), (), s32[]{:S(2)}) async-start(), calls=%async_computation.39 | async-start | bytes 589824 | tf_op jit(solution)/shard_map/reduce_scatter | solution.py:344
  991.5 14.3 copy-start.49
  991.5 283.2 %reduce-scatter.52.cloned.1.call-start = ((), (), s32[]{:S(2)}) async-start(), calls=%async_computation.42 | async-start | bytes 589824
  1064.6 4.5 copy-start.18
  1070.6 3.4 copy-start.20
  1070.6 241.7 %reduce-scatter.40.cloned.1.call-start = ((), (), s32[]{:S(2)}) async-start(), calls=%async_computation.36 | async-start | bytes 589824 | tf_op jit(solution)/shard_map/reduce_scatter | solution.py:332
  1074.5 3.6 copy-start.19
  1074.5 276.0 %reduce-scatter.38.cloned.1.call-start = ((), (), s32[]{:S(2)}) async-start(), calls=%async_computation.35 | async-start | bytes 589824 | tf_op jit(solution)/shard_map/reduce_scatter | solution.py:329
  1078.5 3.6 copy-start.22
  1078.5 309.1 %reduce-scatter.42.cloned.1.call-start = ((), (), s32[]{:S(2)}) async-start(), calls=%async_computation.37 | async-start | bytes 589824 | tf_op jit(solution)/shard_map/reduce_scatter | solution.py:335
  1082.1 2.5 copy-start.9
  1082.1 452.5 %reduce-scatter.36.cloned.1.call-start = ((), (), s32[]{:S(2)}) async-start(), calls=%async_computation.34 | async-start | bytes 10485760 | tf_op jit(solution)/shard_map/reduce_scatter | solution.py:179
  1082.1 2.5 copy-start.26
  1089.2 525.2 %reduce-scatter.34.cloned.1.call-start = ((), (), s32[]{:S(2)}) async-start(), calls=%async_computation.33 | async-start | bytes 5242880 | tf_op jit(solution)/shard_map/reduce_scatter | solution.py:179
  1095.0 143.6 %copy-start.15 = (bf16[8,32,1024]{2,0,1:T(8,128)(2,1)S(1)}, bf16[8,32,1024]{2,0,1:T(8,128)(2,1)}, u32[]{:S(2)}) copy-start(bf16[8,32,1024]{2,0,1:T(8,128)(2,1)} %get-tuple-element.513) | copy-start | bytes 1572868
  1239.7 296.7 %copy-start.47 = (s32[8]{0:T(128)S(1)}, s32[8]{0:T(128)}, u32[]{:S(2)}) copy-start(s32[8]{0:T(128)} %copy-done.46) | copy-start | bytes 100
  1537.1 77.3 %copy-start.7 = (bf16[8,32,1024]{2,0,1:T(8,128)(2,1)S(1)}, bf16[8,32,1024]{2,0,1:T(8,128)(2,1)}, u32[]{:S(2)}) copy-start(bf16[8,32,1024]{2,0,1:T(8,128)(2,1)} %copy-done.6) | copy-start | bytes 1572868
  1537.1 77.3 %copy-start.32 = (f32[8,32]{0,1:T(8,128)S(1)}, f32[8,32]{0,1:T(8,128)}, u32[]{:S(2)}) copy-start(f32[8,32]{0,1:T(8,128)} %copy-done.31) | copy-start | bytes 3076
  1537.1 77.3 %copy-start.34 = (f32[8,32]{0,1:T(8,128)S(1)}, f32[8,32]{0,1:T(8,128)}, u32[]{:S(2)}) copy-start(f32[8,32]{0,1:T(8,128)} %copy-done.33) | copy-start | bytes 3076
  1537.1 77.3 %copy-start.36 = (f32[1,1024]{1,0:T(1,128)S(1)}, f32[1,1024]{1,0:T(1,128)}, u32[]{:S(2)}) copy-start(f32[1,1024]{1,0:T(1,128)} %copy-done.35) | copy-start | bytes 12292
  1538.7 77.6 %copy-start.11 = (f32[8,32,1024]{2,0,1:T(8,128)S(1)}, f32[8,32,1024]{2,0,1:T(8,128)}, u32[]{:S(2)}) copy-start(f32[8,32,1024]{2,0,1:T(8,128)} %get-tuple-element.498) | copy-start | bytes 3145732
  1538.7 79.2 %all-to-all-start.3 = ((bf16[8,64,1024]{2,1,0:T(8,128)(2,1)}), bf16[8,64,1024]{2,1,0:T(8,128)(2,1)S(1)}, u32[]{:S(2)}, u32[]{:S(2)}) async-start(bf16[8,64,1024]{2,1,0:T(8,128)(2,1)} %copy.296), calls=%async_computation.10 | async-start | bytes 2097152 | tf_op jit(solution)/shard_map/all_to_all | solution.py:303
  1616.3 6.0 copy-start.45
  1617.9 48.9 %all-to-all-start.2 = ((bf16[8,32,1024]{2,1,0:T(8,128)(2,1)}), bf16[8,32,1024]{2,1,0:T(8,128)(2,1)}, u32[]{:S(2)}, u32[]{:S(2)}) async-start(bf16[8,32,1024]{2,1,0:T(8,128)(2,1)} %copy.291), calls=%async_computation.8 | async-start | bytes 1048576 | tf_op jit(solution)/shard_map/all_to_all | solution.py:296
  1622.4 47.0 %copy-start.1 = (bf16[1024,1024]{1,0:T(8,128)(2,1)S(1)}, bf16[1024,1024]{1,0:T(8,128)(2,1)}, u32[]{:S(2)}) copy-start(bf16[1024,1024]{1,0:T(8,128)(2,1)} %param.40) | copy-start | bytes 6291460
  (17 other events, 24.8 us)
Sparse Core Ops, SparseCore 0:
  28.5 45.2 all-gather.7
  125.5 75.4 reduce-scatter.23
  203.3 81.2 all-gather.9
  286.7 44.4 all-gather.11
  382.9 75.4 reduce-scatter.25
  462.0 46.4 all-gather.13
  510.1 44.6 all-gather.15
  568.7 75.4 reduce-scatter.29
  649.2 46.4 all-gather.17
  794.3 75.4 reduce-scatter.31
  872.1 77.2 reduce-scatter.27
  953.5 46.4 all-gather.19
  1003.7 40.0 reduce-scatter.55
  1046.9 41.1 reduce-scatter.49
  1091.3 34.1 reduce-scatter.53
  1128.5 34.1 reduce-scatter.43
  1165.8 34.1 reduce-scatter.47
  1202.9 34.1 reduce-scatter.45
  1240.5 34.1 reduce-scatter.51
  1278.2 34.1 reduce-scatter.39
  1316.3 34.1 reduce-scatter.37
  1353.5 34.1 reduce-scatter.41
  1390.1 144.4 reduce-scatter.35
  1536.9 77.4 reduce-scatter.33
where the time goes:
time: 1690 us; the launch traced here: 1680 us
  waiting for transfers between devices  1140 us (67%)
  matrix products  201 us (12%)
  local copies, waits for them, and re-layouts  177 us (10%)
  other arithmetic  62.4 us (4%)
  blocking collectives  60.8 us (4%)
    reduce_scatter x4, waiting for transfers between devices, narrow_grads(): lax.psum_scatter(value_entries, 'tensor', scatter_dimension=1, tiled=True)  362 us
    reduce_scatter x3, waiting for transfers between devices, narrow_rows(): lax.psum_scatter(value_entries, 'tensor', scatter_dimension=1, tiled=True)  205 us
    all_gather x4, waiting for transfers between devices, widen_rows(): return lax.all_gather(value_entries, 'tensor', axis=1, tiled=True)  196 us
    dynamic_slice x144, local copies, waits for them, and re-layouts, attend_all(): lax.map(lambda operands: attend_forward(*operands, causal), (queries, key...  97.5 us
    all_gather x3, waiting for transfers between devices, widen_grads(): return lax.all_gather(value_entries, 'tensor', axis=1, tiled=True)  92.7 us
    unnamed x27, waiting for transfers between devices  62.1 us
    dot_general x10, matrix products, project(): jnp.einsum('nrw,wk->nrk', value_entries, weight_matrix, preferred_element...  57.4 us
    dot_general x10, matrix products, weight_grad(): jnp.einsum('jrm,jrw->mw', left_operand, right_operand, preferred_element_...  43.5 us
  transfers between devices with their start and end apart: 27, of which 23 were waited for; matrix products, arithmetic and copies ran while one was open for 12% of the time, Pallas kernels for 0%

commit v1 on v0

v1 whole, which is shorter than its diff:
```python
import functools

import jax
import jax.numpy as jnp
from jax import lax
from jax.experimental import pallas as pl
from jax.experimental.pallas import tpu as pltpu
from jax.sharding import PartitionSpec as P

HEAD_DIM = 64
SCALE = 0.125
MASKED = -1e30
EPSILON = 1e-05
MESH = pl.DeviceIdType.MESH
VMEM_LIMIT = 60 * 1024 * 1024
BF16 = jnp.bfloat16
F32 = jnp.float32


def dot_nn(a, b):
    return lax.dot_general(a, b, (((1,), (0,)), ((), ())), preferred_element_type=F32)


def dot_nt(a, b):
    return lax.dot_general(a, b, (((1,), (1,)), ((), ())), preferred_element_type=F32)


def dot_tn(a, b):
    return lax.dot_general(a, b, (((0,), (0,)), ((), ())), preferred_element_type=F32)


def norm_parts(v):
    mu = jnp.mean(v, axis=-1, keepdims=True)
    var = jnp.mean(v * v, axis=-1, keepdims=True) - mu * mu
    rstd = lax.rsqrt(var + EPSILON)
    return (v - mu) * rstd, rstd


def norm_back(dn, nh, rstd, gain):
    c = dn * gain
    return rstd * (
        c - jnp.mean(c, axis=-1, keepdims=True) - nh * jnp.mean(c * nh, axis=-1, keepdims=True)
    )


def head_stack(a, heads):
    lane = lax.broadcasted_iota(jnp.int32, a.shape, 1) // HEAD_DIM
    zero = jnp.zeros_like(a)
    return jnp.concatenate([jnp.where(lane == h, a, zero) for h in range(heads)], axis=0)


def attn_probs(q, k, limit, causal):
    heads = q.shape[1] // HEAD_DIM
    qs = head_stack(q, heads)
    s = dot_nt(qs, k) * SCALE
    key = lax.broadcasted_iota(jnp.int32, s.shape, 1)
    allowed = key < limit
    if causal:
        row = lax.rem(lax.broadcasted_iota(jnp.int32, s.shape, 0), q.shape[0])
        allowed = allowed & (key <= row)
    s = jnp.where(allowed, s, MASKED)
    e = jnp.exp(s - jnp.max(s, axis=-1, keepdims=True))
    return qs, e / jnp.sum(e, axis=-1, keepdims=True)


def lane_stack(a, heads):
    rows = a.shape[0] // heads
    return jnp.concatenate([a[h * rows : (h + 1) * rows] for h in range(heads)], axis=1)


def attn_fwd(q, k, v, limit, causal):
    heads = q.shape[1] // HEAD_DIM
    _, p = attn_probs(q, k, limit, causal)
    return dot_nn(lane_stack(p.astype(BF16), heads), head_stack(v, heads)).astype(BF16)


def attn_bwd(q, k, v, do, limit, causal):
    heads = q.shape[1] // HEAD_DIM
    qs, p = attn_probs(q, k, limit, causal)
    dos = head_stack(do, heads)
    dp = dot_nt(dos, v)
    delta = jnp.sum(p * dp, axis=-1, keepdims=True)
    ds = (p * (dp - delta) * SCALE).astype(BF16)
    dq = dot_nn(lane_stack(ds, heads), head_stack(k, heads)).astype(BF16)
    dk = dot_tn(ds, qs).astype(BF16)
    dv = dot_tn(p.astype(BF16), dos).astype(BF16)
    return dq, dk, dv


def params(steps):
    return pltpu.CompilerParams(
        dimension_semantics=("arbitrary",) * steps, vmem_limit_bytes=VMEM_LIMIT
    )


def whole(shape):
    return pl.BlockSpec(shape, lambda *_: (0,) * len(shape))


SMEM = pl.BlockSpec(memory_space=pltpu.SMEM)


def self_fwd_kernel(spd, lens, x_ref, gain, bias, w_ref, n1_ref, q_ref, k_ref, v_ref, o_ref, h_ref):
    j = pl.program_id(0)
    seq = x_ref.shape[0] // spd
    hc = q_ref.shape[2]

    @pl.when(j == 0)
    def _():
        x = x_ref[...].astype(F32)
        nh, _ = norm_parts(x)
        n1_ref[...] = (nh * gain[0:1] + bias[0:1]).astype(BF16)
        h_ref[...] = x

    w = w_ref.at[0, 0]
    qkv = dot_nn(n1_ref[...], w[:, : 3 * hc]).astype(BF16)
    q_ref[0] = qkv[:, :hc]
    k_ref[0] = qkv[:, hc : 2 * hc]
    v_ref[0] = qkv[:, 2 * hc :]
    for i in range(spd):
        rows = slice(i * seq, (i + 1) * seq)
        o_ref[0, rows] = attn_fwd(
            q_ref[0, rows], k_ref[0, rows], v_ref[0, rows], lens[i], True
        )
    h_ref[...] += dot_nt(o_ref[0], w[:, 3 * hc :])


def self_fwd(lens, x, gain, bias, wg, spd, nt):
    n, dim = x.shape
    hc = wg.shape[3] // 4
    part = pl.BlockSpec((1, n, hc), lambda j: (j, 0, 0))
    shaped = jax.ShapeDtypeStruct((nt, n, hc), BF16)
    return pl.pallas_call(
        functools.partial(self_fwd_kernel, spd),
        grid=(nt,),
        in_specs=[
            SMEM,
            whole((n, dim)),
            whole(gain.shape),
            whole(bias.shape),
            pl.BlockSpec((1, 1, dim, 4 * hc), lambda j: (j, 0, 0, 0)),
        ],
        out_specs=[whole((n, dim)), part, part, part, part, whole((n, dim))],
        out_shape=[
            jax.ShapeDtypeStruct((n, dim), BF16),
            shaped,
            shaped,
            shaped,
            shaped,
            jax.ShapeDtypeStruct((n, dim), F32),
        ],
        compiler_params=params(1),
        name="self_fwd",
    )(lens, x, gain, bias, wg)


def cross_fwd_kernel(
    spd, lens, h1_ref, ed_ref, gain, bias, w_ref, n2_ref, q_ref, k_ref, v_ref, o_ref, h_ref
):
    j = pl.program_id(0)
    seq = h1_ref.shape[0] // spd
    enc = ed_ref.shape[0] // spd
    hc = q_ref.shape[2]

    @pl.when(j == 0)
    def _():
        h = h1_ref[...]
        nh, _ = norm_parts(h)
        n2_ref[...] = (nh * gain[1:2] + bias[1:2]).astype(BF16)
        h_ref[...] = h

    w = w_ref.at[0, 0]
    q_ref[0] = dot_nn(n2_ref[...], w[:, :hc]).astype(BF16)
    kv = dot_nn(ed_ref[...], w[:, hc : 3 * hc]).astype(BF16)
    k_ref[0] = kv[:, :hc]
    v_ref[0] = kv[:, hc:]
    for i in range(spd):
        rows = slice(i * seq, (i + 1) * seq)
        keys = slice(i * enc, (i + 1) * enc)
        o_ref[0, rows] = attn_fwd(
            q_ref[0, rows], k_ref[0, keys], v_ref[0, keys], lens[i], False
        )
    h_ref[...] += dot_nt(o_ref[0], w[:, 3 * hc :])


def cross_fwd(lens, h1, ed, gain, bias, wg, spd, nt):
    n, dim = h1.shape
    m = ed.shape[0]
    hc = wg.shape[3] // 4
    part = pl.BlockSpec((1, n, hc), lambda j: (j, 0, 0))
    keys = pl.BlockSpec((1, m, hc), lambda j: (j, 0, 0))
    shaped = jax.ShapeDtypeStruct((nt, n, hc), BF16)
    long = jax.ShapeDtypeStruct((nt, m, hc), BF16)
    return pl.pallas_call(
        functools.partial(cross_fwd_kernel, spd),
        grid=(nt,),
        in_specs=[
            SMEM,
            whole((n, dim)),
            whole((m, dim)),
            whole(gain.shape),
            whole(bias.shape),
            pl.BlockSpec((1, 1, dim, 4 * hc), lambda j: (j, 1, 0, 0)),
        ],
        out_specs=[whole((n, dim)), part, keys, keys, part, whole((n, dim))],
        out_shape=[
            jax.ShapeDtypeStruct((n, dim), BF16),
            shaped,
            long,
            long,
            shaped,
            jax.ShapeDtypeStruct((n, dim), F32),
        ],
        compiler_params=params(1),
        name="cross_fwd",
    )(lens, h1, ed, gain, bias, wg)


def row_valid(lens, spd, n):
    row = lax.broadcasted_iota(jnp.int32, (n, 1), 0)
    seq = n // spd
    end = jnp.full((n, 1), lens[0], jnp.int32)
    for i in range(1, spd):
        end = jnp.where(row >= i * seq, i * seq + lens[i], end)
    return row < end


def feed_kernel(
    spd,
    lens,
    h2_ref,
    cot_ref,
    gain,
    bias,
    win_ref,
    wout_ref,
    res_ref,
    dh_ref,
    sums_ref,
    dw_in_ref,
    dw_out_ref,
    n3,
    n3t,
    g3,
    g3t,
    out_acc,
    dn_acc,
):
    step = pl.program_id(0) * pl.num_programs(1) + pl.program_id(1)
    last = pl.num_programs(0) * pl.num_programs(1) - 1
    n = h2_ref.shape[0]

    @pl.when(step == 0)
    def _():
        nh, _ = norm_parts(h2_ref[...])
        low = nh * gain[2:3] + bias[2:3]
        n3[...] = low.astype(BF16)
        n3t[...] = low.T.astype(BF16)
        keep = row_valid(lens, spd, n)
        dh = jnp.where(keep, cot_ref[...].astype(F32), 0.0)
        g3[...] = dh.astype(BF16)
        g3t[...] = dh.T.astype(BF16)
        out_acc[...] = jnp.zeros_like(out_acc)
        dn_acc[...] = jnp.zeros_like(dn_acc)

    win = win_ref[0, 0]
    wout = wout_ref[0, 0]
    u = dot_nn(n3[...], win)
    ga = dot_nn(g3[...], wout)
    sg = 1.0 / (1.0 + jnp.exp(-u))
    r = (u * sg).astype(BF16)
    du = (ga * (sg * (1.0 + u * (1.0 - sg)))).astype(BF16)
    out_acc[...] += dot_nt(r, wout)
    dn_acc[...] += dot_nt(du, win)
    dw_in_ref[0] = dot_nn(n3t[...], du).astype(BF16)
    dw_out_ref[0] = dot_nn(g3t[...], r).astype(BF16)

    @pl.when(step == last)
    def _():
        keep = row_valid(lens, spd, n)
        h2 = h2_ref[...]
        res_ref[...] = jnp.where(keep, h2 + out_acc[...], 0.0).astype(BF16)
        dh = jnp.where(keep, cot_ref[...].astype(F32), 0.0)
        nh, rstd = norm_parts(h2)
        dn = dn_acc[...]
        dh_ref[...] = dh + norm_back(dn, nh, rstd, gain[2:3])
        sums_ref[0:1] = jnp.sum(dn * nh, axis=0, keepdims=True)
        sums_ref[1:2] = jnp.sum(dn, axis=0, keepdims=True)


def feed(lens, h2, cot, gain, bias, wg, spd, nt):
    n, dim = h2.shape
    fc = wg.shape[3]
    block = min(512, fc)
    subs = fc // block
    dw = pl.BlockSpec((1, dim, block), lambda j, i: (j, 0, i))
    return pl.pallas_call(
        functools.partial(feed_kernel, spd),
        grid=(nt, subs),
        in_specs=[
            SMEM,
            whole((n, dim)),
            whole((n, dim)),
            whole(gain.shape),
            whole(bias.shape),
            pl.BlockSpec((1, 1, dim, block), lambda j, i: (j, 2, 0, i)),
            pl.BlockSpec((1, 1, dim, block), lambda j, i: (j, 3, 0, i)),
        ],
        out_specs=[whole((n, dim)), whole((n, dim)), whole((2, dim)), dw, dw],
        out_shape=[
            jax.ShapeDtypeStruct((n, dim), BF16),
            jax.ShapeDtypeStruct((n, dim), F32),
            jax.ShapeDtypeStruct((2, dim), F32),
            jax.ShapeDtypeStruct((nt, dim, fc), BF16),
            jax.ShapeDtypeStruct((nt, dim, fc), BF16),
        ],
        scratch_shapes=[
            pltpu.VMEM((n, dim), BF16),
            pltpu.VMEM((dim, n), BF16),
            pltpu.VMEM((n, dim), BF16),
            pltpu.VMEM((dim, n), BF16),
            pltpu.VMEM((n, dim), F32),
            pltpu.VMEM((n, dim), F32),
        ],
        compiler_params=params(2),
        name="feed_forward",
    )(lens, h2, cot, gain, bias, wg, wg)


def cross_bwd_kernel(
    spd,
    lens,
    dh2_ref,
    h1_ref,
    n2_ref,
    ed_ref,
    gain,
    q_ref,
    k_ref,
    v_ref,
    o_ref,
    w_ref,
    ded_ref,
    dh1_ref,
    sums_ref,
    dw_ref,
    g2,
    g2t,
    n2t,
    edt,
    dn_acc,
    ded_acc,
    dq,
    dk,
    dv,
):
    j = pl.program_id(0)
    n = h1_ref.shape[0]
    seq = n // spd
    enc = ed_ref.shape[0] // spd
    hc = q_ref.shape[2]

    @pl.when(j == 0)
    def _():
        dh = dh2_ref[...]
        g2[...] = dh.astype(BF16)
        g2t[...] = dh.T.astype(BF16)
        n2t[...] = n2_ref[...].T
        edt[...] = ed_ref[...].T
        dn_acc[...] = jnp.zeros_like(dn_acc)
        ded_acc[...] = jnp.zeros_like(ded_acc)

    w = w_ref.at[0, 0]
    do = dot_nn(g2[...], w[:, 3 * hc :]).astype(BF16)
    for i in range(spd):
        rows = slice(i * seq, (i + 1) * seq)
        keys = slice(i * enc, (i + 1) * enc)
        a, b, c = attn_bwd(
            q_ref[0, rows], k_ref[0, keys], v_ref[0, keys], do[rows], lens[i], False
        )
        dq[rows] = a
        dk[keys] = b
        dv[keys] = c
    dn_acc[...] += dot_nt(dq[...], w[:, :hc])
    ded_acc[...] += dot_nt(dk[...], w[:, hc : 2 * hc]) + dot_nt(dv[...], w[:, 2 * hc : 3 * hc])
    dw_ref[0, :, :hc] = dot_nn(n2t[...], dq[...]).astype(BF16)
    dw_ref[0, :, hc : 2 * hc] = dot_nn(edt[...], dk[...]).astype(BF16)
    dw_ref[0, :, 2 * hc : 3 * hc] = dot_nn(edt[...], dv[...]).astype(BF16)
    dw_ref[0, :, 3 * hc :] = dot_nn(g2t[...], o_ref[0]).astype(BF16)

    @pl.when(j == pl.num_programs(0) - 1)
    def _():
        ded_ref[...] = ded_acc[...].astype(BF16)
        nh, rstd = norm_parts(h1_ref[...])
        dn = dn_acc[...]
        dh1_ref[...] = dh2_ref[...] + norm_back(dn, nh, rstd, gain[1:2])
        sums_ref[0:1] = jnp.sum(dn * nh, axis=0, keepdims=True)
        sums_ref[1:2] = jnp.sum(dn, axis=0, keepdims=True)


def cross_bwd(lens, dh2, h1, n2, ed, gain, q, k, v, o, wg, spd, nt):
    n, dim = h1.shape
    m = ed.shape[0]
    hc = wg.shape[3] // 4
    part = pl.BlockSpec((1, n, hc), lambda j: (j, 0, 0))
    keys = pl.BlockSpec((1, m, hc), lambda j: (j, 0, 0))
    return pl.pallas_call(
        functools.partial(cross_bwd_kernel, spd),
        grid=(nt,),
        in_specs=[
            SMEM,
            whole((n, dim)),
            whole((n, dim)),
            whole((n, dim)),
            whole((m, dim)),
            whole(gain.shape),
            part,
            keys,
            keys,
            part,
            pl.BlockSpec((1, 1, dim, 4 * hc), lambda j: (j, 1, 0, 0)),
        ],
        out_specs=[
            whole((m, dim)),
            whole((n, dim)),
            whole((2, dim)),
            pl.BlockSpec((1, dim, 4 * hc), lambda j: (j, 0, 0)),
        ],
        out_shape=[
            jax.ShapeDtypeStruct((m, dim), BF16),
            jax.ShapeDtypeStruct((n, dim), F32),
            jax.ShapeDtypeStruct((2, dim), F32),
            jax.ShapeDtypeStruct((nt, dim, 4 * hc), BF16),
        ],
        scratch_shapes=[
            pltpu.VMEM((n, dim), BF16),
            pltpu.VMEM((dim, n), BF16),
            pltpu.VMEM((dim, n), BF16),
            pltpu.VMEM((dim, m), BF16),
            pltpu.VMEM((n, dim), F32),
            pltpu.VMEM((m, dim), F32),
            pltpu.VMEM((n, hc), BF16),
            pltpu.VMEM((m, hc), BF16),
            pltpu.VMEM((m, hc), BF16),
        ],
        compiler_params=params(1),
        name="cross_bwd",
    )(lens, dh2, h1, n2, ed, gain, q, k, v, o, wg)


def self_bwd_kernel(
    spd,
    lens,
    dh1_ref,
    x_ref,
    n1_ref,
    gain,
    q_ref,
    k_ref,
    v_ref,
    o_ref,
    w_ref,
    dx_ref,
    sums_ref,
    dw_ref,
    g1,
    g1t,
    n1t,
    dn_acc,
    dqkv,
):
    j = pl.program_id(0)
    n = x_ref.shape[0]
    seq = n // spd
    hc = q_ref.shape[2]

    @pl.when(j == 0)
    def _():
        dh = dh1_ref[...]
        g1[...] = dh.astype(BF16)
        g1t[...] = dh.T.astype(BF16)
        n1t[...] = n1_ref[...].T
        dn_acc[...] = jnp.zeros_like(dn_acc)

    w = w_ref.at[0, 0]
    do = dot_nn(g1[...], w[:, 3 * hc :]).astype(BF16)
    for i in range(spd):
        rows = slice(i * seq, (i + 1) * seq)
        a, b, c = attn_bwd(q_ref[0, rows], k_ref[0, rows], v_ref[0, rows], do[rows], lens[i], True)
        dqkv[rows, :hc] = a
        dqkv[rows, hc : 2 * hc] = b
        dqkv[rows, 2 * hc :] = c
    dn_acc[...] += dot_nt(dqkv[...], w[:, : 3 * hc])
    dw_ref[0, :, : 3 * hc] = dot_nn(n1t[...], dqkv[...]).astype(BF16)
    dw_ref[0, :, 3 * hc :] = dot_nn(g1t[...], o_ref[0]).astype(BF16)

    @pl.when(j == pl.num_programs(0) - 1)
    def _():
        nh, rstd = norm_parts(x_ref[...].astype(F32))
        dn = dn_acc[...]
        dx_ref[...] = (dh1_ref[...] + norm_back(dn, nh, rstd, gain[0:1])).astype(BF16)
        sums_ref[0:1] = jnp.sum(dn * nh, axis=0, keepdims=True)
        sums_ref[1:2] = jnp.sum(dn, axis=0, keepdims=True)


def self_bwd(lens, dh1, x, n1, gain, q, k, v, o, wg, spd, nt):
    n, dim = x.shape
    hc = wg.shape[3] // 4
    part = pl.BlockSpec((1, n, hc), lambda j: (j, 0, 0))
    return pl.pallas_call(
        functools.partial(self_bwd_kernel, spd),
        grid=(nt,),
        in_specs=[
            SMEM,
            whole((n, dim)),
            whole((n, dim)),
            whole((n, dim)),
            whole(gain.shape),
            part,
            part,
            part,
            part,
            pl.BlockSpec((1, 1, dim, 4 * hc), lambda j: (j, 0, 0, 0)),
        ],
        out_specs=[
            whole((n, dim)),
            whole((2, dim)),
            pl.BlockSpec((1, dim, 4 * hc), lambda j: (j, 0, 0)),
        ],
        out_shape=[
            jax.ShapeDtypeStruct((n, dim), BF16),
            jax.ShapeDtypeStruct((2, dim), F32),
            jax.ShapeDtypeStruct((nt, dim, 4 * hc), BF16),
        ],
        scratch_shapes=[
            pltpu.VMEM((n, dim), BF16),
            pltpu.VMEM((dim, n), BF16),
            pltpu.VMEM((dim, n), BF16),
            pltpu.VMEM((n, dim), F32),
            pltpu.VMEM((n, 3 * hc), BF16),
        ],
        compiler_params=params(1),
        name="self_bwd",
    )(lens, dh1, x, n1, gain, q, k, v, o, wg)


def flip(index, mask):
    out = index
    bit = 1
    while bit <= mask:
        if mask & bit:
            out = out + bit - 2 * bit * lax.rem(lax.div(index, bit), 2)
        bit *= 2
    return out


def greet(peers):
    barrier = pltpu.get_barrier_semaphore()
    for peer in peers:
        pl.semaphore_signal(barrier, inc=1, device_id=peer, device_id_type=MESH)
    pl.semaphore_wait(barrier, len(peers))


def gather_kernel(ndp, nt, own_ref, out_ref, own_sem, send_sems, recv_sems):
    d = lax.axis_index("dp")
    t = lax.axis_index("tensor")
    groups = own_ref.shape[0]
    half = own_ref.shape[2] // 2
    bits = ndp.bit_length() - 1
    chip_bits = [1 << b for b in range(1, bits)]
    orders = (chip_bits, chip_bits[::-1])

    def dp_peer(bit):
        return (flip(d, bit), t)

    def t_peer(j):
        return (d, flip(t, j))

    greet([dp_peer(1 << b) for b in range(bits)] + [t_peer(j) for j in range(1, nt)])
    own = pltpu.make_async_copy(own_ref, out_ref.at[0], own_sem)
    own.start()

    chunks = [(g, j) for g in range(groups) for j in range(1, nt)]
    started = []

    def send(c, slot, src, dst, peer):
        copy = pltpu.make_async_remote_copy(
            src_ref=src,
            dst_ref=dst,
            send_sem=send_sems.at[c, slot],
            recv_sem=recv_sems.at[c, slot],
            device_id=peer,
            device_id_type=MESH,
        )
        copy.start()
        started.append(copy)
        return copy

    first = [
        send(c, 0, own_ref.at[g, d], out_ref.at[j, g, d], t_peer(j))
        for c, (g, j) in enumerate(chunks)
    ]
    pending = {}

    def spread(c, level):
        g, j = chunks[c]
        if level == 0:
            first[c].wait_recv()
        else:
            for copy in pending.pop((c, level)):
                copy.wait_recv()
        slot = 1 + 2 * ((1 << level) - 1)
        copies = []
        if level < len(chip_bits):
            for side, order in enumerate(orders):
                held = [0]
                for bit in order[:level]:
                    held += [e ^ bit for e in held]
                rows = pl.ds(side * half, half)
                for e in held:
                    at = out_ref.at[j, g, flip(d, e), rows]
                    copies.append(send(c, slot, at, at, dp_peer(order[level])))
                    slot += 1
        else:
            for e in range(0, ndp, 2):
                at = out_ref.at[j, g, flip(d, e)]
                copies.append(send(c, slot, at, at, dp_peer(1)))
                slot += 1
        pending[(c, level + 1)] = copies

    levels = len(chip_bits) + 1
    for tick in range(len(chunks) + levels - 1):
        for level in range(levels):
            c = tick - level
            if 0 <= c < len(chunks):
                spread(c, level)
    for copies in pending.values():
        for copy in copies:
            copy.wait_recv()
    for copy in started:
        copy.wait_send()
    own.wait()


def gather_weights(own, ndp, nt):
    groups, dim, width = own.shape
    rows = dim // ndp
    count = groups * (nt - 1)
    slots = 1 + 2 * (ndp // 2 - 1) + ndp // 2
    out = pl.pallas_call(
        functools.partial(gather_kernel, ndp, nt),
        in_specs=[pl.BlockSpec(memory_space=pl.ANY)],
        out_specs=pl.BlockSpec(memory_space=pl.ANY),
        out_shape=jax.ShapeDtypeStruct((nt, groups, ndp, rows, width), BF16),
        scratch_shapes=[
            pltpu.SemaphoreType.DMA,
            pltpu.SemaphoreType.DMA((count, slots)),
            pltpu.SemaphoreType.DMA((count, slots)),
        ],
        compiler_params=pltpu.CompilerParams(
            collective_id=0, has_side_effects=True, vmem_limit_bytes=VMEM_LIMIT
        ),
        name="gather_weights",
    )(own.reshape(groups, ndp, rows, width))
    return out.reshape(nt, groups, dim, width)


def reduce_kernel(
    ndp,
    nt,
    dws_ref,
    dwc_ref,
    dwi_ref,
    dwo_ref,
    sums_ref,
    out_ref,
    norm_ref,
    got_core,
    got_chip,
    got_z,
    got_sum,
    mine,
    work,
    final,
    total,
    load_sems,
    send_sems,
    recv_sems,
    z_send,
    z_recv,
    sum_send,
    sum_recv,
):
    d = lax.axis_index("dp")
    t = lax.axis_index("tensor")
    bits = ndp.bit_length() - 1
    tbits = nt.bit_length() - 1
    chips = ndp // 2
    rows, width = out_ref.shape[1], out_ref.shape[2]
    half = rows // 2
    core = lax.rem(d, 2)
    chip = lax.div(d, 2)
    chip_bits = [1 << b for b in range(bits - 1)]
    orders = (chip_bits, chip_bits[::-1])
    levels = len(chip_bits)

    def dp_peer(bit):
        return (flip(d, bit), t)

    def t_peer(j):
        return (d, flip(t, j))

    greet([dp_peer(1 << b) for b in range(bits)] + [t_peer(j) for j in range(1, nt)])

    sources = [dwo_ref, dwi_ref, dwc_ref, dws_ref]
    target = [3, 2, 1, 0]
    chunks = [(s, j) for s in range(4) for j in list(range(1, nt)) + [0]]
    started = []

    def send(src, dst, ssem, rsem, peer):
        copy = pltpu.make_async_remote_copy(
            src_ref=src,
            dst_ref=dst,
            send_sem=ssem,
            recv_sem=rsem,
            device_id=peer,
            device_id_type=MESH,
        )
        copy.start()
        started.append(copy)
        return copy

    state = {}

    def core_send(c):
        s, j = chunks[c]
        src = sources[s].at[j, :, 1 - core]
        return send(src, got_core.at[c], send_sems.at[c, 0], recv_sems.at[c, 0], dp_peer(1))

    def core_load(c):
        s, j = chunks[c]
        copy = pltpu.make_async_copy(
            sources[s].at[j, :, core], mine.at[c % 2], load_sems.at[c % 2]
        )
        copy.start()
        return copy

    def core_add(c):
        core_copies[c].wait_recv()
        load_copies[c].wait()
        slot = c % levels
        if c >= levels:
            for copy in state.pop(("busy", c - levels)):
                copy.wait_send()
                started[:] = [one for one in started if one is not copy]

        def body(e, carry):
            a = mine[c % 2, e].astype(F32) + got_core[c, e].astype(F32)
            work[slot, e] = a.astype(BF16)
            return carry

        lax.fori_loop(0, chips, body, 0)
        if c + 2 < len(chunks):
            load_copies[c + 2] = core_load(c + 2)
        state[("busy", c)] = []
        chip_step(c, 0)

    def chip_step(c, level):
        slot = 1 + 2 * ((chips - (chips >> level)))
        base = 2 * (chips - (chips >> level))
        copies = []
        for side, order in enumerate(orders):
            rest = [0]
            for bit in order[level + 1 :]:
                rest += [e ^ bit for e in rest]
            for e in rest:
                far = flip(chip, order[level] ^ e)
                copies.append(
                    send(
                        work.at[c % levels, far, pl.ds(side * half, half)],
                        got_chip.at[c, base + len(copies)],
                        send_sems.at[c, slot + len(copies)],
                        recv_sems.at[c, slot + len(copies)],
                        dp_peer(2 * order[level]),
                    )
                )
        state[("busy", c)] += copies
        state[(c, level)] = copies

    def chip_add(c, level):
        base = 2 * (chips - (chips >> level))
        at = 0
        for copy in state[(c, level)]:
            copy.wait_recv()
        last = level == len(chip_bits) - 1
        s, j = chunks[c]
        for side, order in enumerate(orders):
            rest = [0]
            for bit in order[level + 1 :]:
                rest += [e ^ bit for e in rest]
            span = pl.ds(side * half, half)
            for e in rest:
                near = flip(chip, e)
                a = work[c % levels, near, span].astype(F32) + got_chip[c, base + at].astype(F32)
                at += 1
                if last:
                    final[c, span] = a.astype(BF16)
                else:
                    work[c % levels, near, span] = a.astype(BF16)
        if last:
            if j:
                state[("z", s, j)] = send(
                    final.at[c],
                    got_z.at[s, j - 1],
                    z_send.at[s, j - 1],
                    z_recv.at[s, j - 1],
                    t_peer(j),
                )
        else:
            chip_step(c, level + 1)

    def finish(s):
        c = chunks.index((s, 0))
        a = final[c].astype(F32)
        for j in range(1, nt):
            state[("z", s, j)].wait_recv()
            a = a + got_z[s, j - 1].astype(F32)
        out_ref[target[s]] = a

    sum_peers = [dp_peer(1 << b) for b in range(bits)] + [t_peer(1 << b) for b in range(tbits)]
    sum_copies = {}

    def sum_start(i):
        sum_copies[i] = send(
            total.at[i], got_sum.at[i], sum_send.at[i], sum_recv.at[i], sum_peers[i]
        )

    def sum_finish(i):
        sum_copies[i].wait_recv()
        total[i + 1] = total[i] + got_sum[i]

    total[0] = sums_ref[...]
    core_copies = [core_send(c) for c in range(len(chunks))]
    load_copies = {c: core_load(c) for c in range(2)}
    ticks = len(chunks) + levels
    for tick in range(ticks + 1):
        if tick < len(sum_peers):
            sum_start(tick)
        for stage in range(levels, -1, -1):
            c = tick - stage
            if 0 <= c < len(chunks):
                if stage == 0:
                    core_add(c)
                else:
                    chip_add(c, stage - 1)
        if tick < len(sum_peers):
            sum_finish(tick)
        c = tick - levels - 1
        if 0 <= c < len(chunks) and chunks[c][1] == 0:
            finish(chunks[c][0])
    norm_ref[...] = total[len(sum_peers)]
    for copy in started:
        copy.wait_send()


def reduce_grads(dws, dwc, dwi, dwo, sums, ndp, nt):
    dim, width = dws.shape[1:]
    rows, chips = dim // ndp, ndp // 2
    levels = chips.bit_length() - 1
    count = 4 * nt
    steps = (ndp.bit_length() - 1) + (nt.bit_length() - 1)
    view = (nt, chips, 2, rows, width)
    any_space = pl.BlockSpec(memory_space=pl.ANY)
    vmem = pl.BlockSpec(memory_space=pltpu.VMEM)
    slots = 1 + 2 * (chips - 1)
    return pl.pallas_call(
        functools.partial(reduce_kernel, ndp, nt),
        in_specs=[any_space] * 4 + [vmem],
        out_specs=[vmem, vmem],
        out_shape=[
            jax.ShapeDtypeStruct((4, rows, width), F32),
            jax.ShapeDtypeStruct(sums.shape, F32),
        ],
        scratch_shapes=[
            pltpu.VMEM((count, chips, rows, width), BF16),
            pltpu.VMEM((count, 2 * (chips - 1), rows // 2, width), BF16),
            pltpu.VMEM((4, nt - 1, rows, width), BF16),
            pltpu.VMEM((steps,) + sums.shape, F32),
            pltpu.VMEM((2, chips, rows, width), BF16),
            pltpu.VMEM((levels, chips, rows, width), BF16),
            pltpu.VMEM((count, rows, width), BF16),
            pltpu.VMEM((steps + 1,) + sums.shape, F32),
            pltpu.SemaphoreType.DMA((2,)),
            pltpu.SemaphoreType.DMA((count, slots)),
            pltpu.SemaphoreType.DMA((count, slots)),
            pltpu.SemaphoreType.DMA((4, nt - 1)),
            pltpu.SemaphoreType.DMA((4, nt - 1)),
            pltpu.SemaphoreType.DMA((steps,)),
            pltpu.SemaphoreType.DMA((steps,)),
        ],
        compiler_params=pltpu.CompilerParams(
            collective_id=1, has_side_effects=True, vmem_limit_bytes=VMEM_LIMIT
        ),
        name="reduce_grads",
    )(dws.reshape(view), dwc.reshape(view), dwi.reshape(view), dwo.reshape(view), sums)


def select_rows(lookup, positions):
    matches = positions[:, None] == jnp.arange(lookup.shape[0], dtype=jnp.int32)[None, :]
    return jnp.sum(jnp.where(matches, lookup[None, :], 0), axis=1)


def route_rows(selector, value_entries):
    return jnp.einsum(
        "kj,jrd->krd", selector, value_entries, preferred_element_type=F32
    ).astype(BF16)


def swap_dp(selector_out, selector_in, a):
    sent = lax.all_to_all(
        route_rows(selector_out, a), "dp", split_axis=0, concat_axis=0, tiled=True
    )
    return route_rows(selector_in, sent)


def to_sequences(a):
    return lax.all_to_all(a, "tensor", split_axis=0, concat_axis=1, tiled=True)


def to_positions(a):
    return lax.all_to_all(a, "tensor", split_axis=1, concat_axis=0, tiled=True)


def per_device(
    ndp,
    nt,
    tokens,
    enc_states,
    cotangent,
    tok_len,
    enc_len,
    deal,
    w_q_self,
    w_k_self,
    w_v_self,
    w_o_self,
    w_q_cross,
    w_k_cross,
    w_v_cross,
    w_o_cross,
    w_in,
    w_out,
    gain,
    bias,
):
    d = lax.axis_index("dp")
    t = lax.axis_index("tensor")
    seqs, _, dim = tokens.shape
    spd = seqs // nt
    hc = w_q_self.shape[1]
    slots = d * seqs + jnp.arange(seqs, dtype=jnp.int32)
    sources = select_rows(deal, slots)
    every = jnp.arange(deal.shape[0], dtype=jnp.int32)
    targets = jnp.sum(jnp.where(deal[None, :] == slots[:, None], every[None, :], 0), axis=1)
    peers = jnp.arange(ndp, dtype=jnp.int32)
    outward = (targets[None, :] // seqs == peers[:, None]).astype(BF16)
    inward = (sources[:, None] // seqs == peers[None, :]).astype(BF16)
    tok_lens = lax.dynamic_slice(select_rows(tok_len, sources), (t * spd,), (spd,))
    enc_lens = lax.dynamic_slice(select_rows(enc_len, sources), (t * spd,), (spd,))

    x = to_sequences(swap_dp(outward, inward, tokens)).reshape(-1, dim)
    ed = to_sequences(swap_dp(outward, inward, enc_states)).reshape(-1, dim)
    cot = to_sequences(cotangent).reshape(-1, dim)

    own = jnp.stack(
        [
            jnp.concatenate([w_q_self, w_k_self, w_v_self, w_o_self.T], axis=1),
            jnp.concatenate([w_q_cross, w_k_cross, w_v_cross, w_o_cross.T], axis=1),
            w_in,
            w_out.T,
        ]
    )
    wg = gather_weights(own, ndp, nt)

    n1, q1, k1, v1, o1, h1 = self_fwd(tok_lens, x, gain, bias, wg, spd, nt)
    n2, q2, k2, v2, o2, h2 = cross_fwd(enc_lens, h1, ed, gain, bias, wg, spd, nt)
    res, dh2, sums3, dwi, dwo = feed(tok_lens, h2, cot, gain, bias, wg, spd, nt)
    ded, dh1, sums2, dwc = cross_bwd(
        enc_lens, dh2, h1, n2, ed, gain, q2, k2, v2, o2, wg, spd, nt
    )
    dx, sums1, dws = self_bwd(tok_lens, dh1, x, n1, gain, q1, k1, v1, o1, wg, spd, nt)

    sums = jnp.concatenate(
        [sums1[:1], sums2[:1], sums3[:1], sums1[1:], sums2[1:], sums3[1:], jnp.zeros((2, dim), F32)]
    )
    grads, norm = reduce_grads(dws, dwc, dwi, dwo, sums, ndp, nt)

    def back(a):
        return swap_dp(inward.T, outward.T, to_positions(a.reshape(spd, -1, dim)))

    def attention(g):
        return (g[:, :hc], g[:, hc : 2 * hc], g[:, 2 * hc : 3 * hc], g[:, 3 * hc :].T)

    return (
        to_positions(res.reshape(spd, -1, dim)),
        back(dx),
        back(ded),
        *attention(grads[0]),
        *attention(grads[1]),
        grads[2],
        grads[3].T,
        norm[0:3],
        norm[3:6],
    )


def solution(mesh):
    ndp, nt = mesh.shape["dp"], mesh.shape["tensor"]
    rows = P("dp", "tensor", None)
    columns = P(None, "tensor")
    split = P("tensor", None)
    grad = P("dp", "tensor")
    turned = P("tensor", "dp")
    return jax.shard_map(
        functools.partial(per_device, ndp, nt),
        mesh=mesh,
        in_specs=(
            (rows,) * 3
            + (P(),) * 3
            + (columns, columns, columns, split) * 2
            + (columns, split, P(), P())
        ),
        out_specs=(
            (rows,) * 3 + (grad, grad, grad, turned) * 2 + (grad, turned) + (P(), P())
        ),
        check_vma=False,
    )
```

time: 1690 us -> 714 us (0.42)
  waiting for transfers between devices: 1140 us -> 82.9 us
  Pallas kernels: 0 us -> 508 us
  matrix products: 201 us -> 5.77 us
  local copies, waits for them, and re-layouts: 177 us -> 49 us
  other arithmetic: 62.4 us -> 11.2 us
  blocking collectives: 60.8 us -> 14.7 us
  starting transfers between devices: 15.9 us -> 35.1 us
    reduce_scatter x14 -> x0, waiting for transfers between devices: 782 us -> none  [the longest x4 362 us: narrow_grads(): lax.psum_scatter(value_entries, 'tensor', scatter_dimension=1, tiled=True)]
    pallas_call x0 -> x7, Pallas kernels: none -> 508 us  [the longest x1 261 us: gather_weights(): pl.pallas_call(functools.partial(gather_kernel, ndp, nt), in_specs=[pl.Bl...]
    all_gather x7 -> x0, waiting for transfers between devices: 288 us -> none  [the longest x4 196 us: widen_rows(): return lax.all_gather(value_entries, 'tensor', axis=1, tiled=True)]
    dot_general x142 -> x0, matrix products: 193 us -> none  [the longest x10 57.4 us: project(): jnp.einsum('nrw,wk->nrk', value_entries, weight_matrix, preferred_element...]
    dynamic_slice x144 -> x2, local copies, waits for them, and re-layouts: 97.5 us -> 1.17 us  [the longest x1 0.59 us: per_device(): lax.dynamic_slice(select_rows(tok_len, sources), (t * spd,), (spd,))]
    all_to_all x3 -> x9, waiting for transfers between devices: 9.61 us -> 82.9 us  [the longest x3 47.1 us: to_positions(): return lax.all_to_all(a, 'tensor', split_axis=1, concat_axis=0, tiled=True)]
    unnamed x27 -> x0, waiting for transfers between devices: 62.1 us -> none
    psum x1 -> x0, blocking collectives: 42 us -> none  [per_device(): lax.psum((jnp.stack([gain_one, gain_two, gain_three]), jnp.stack([bias_on...]
  transfers between devices with their start and end apart: 27 -> 9, of which waited for: 23 -> 7; matrix products, arithmetic and copies ran while one was open for 12% -> 8% of each run, Pallas kernels for 0% -> 62%
where the time goes in v1:
time: 714 us; the launch traced here: 708 us
  Pallas kernels  508 us (71%)
  waiting for transfers between devices  82.9 us (12%)
  local copies, waits for them, and re-layouts  49 us (7%)
  starting transfers between devices  35.1 us (5%)
  blocking collectives  14.7 us (2%)
  other arithmetic  11.2 us (2%)
    pallas_call x1, Pallas kernels, gather_weights(): pl.pallas_call(functools.partial(gather_kernel, ndp, nt), in_specs=[pl.Bl...  261 us
    pallas_call x1, Pallas kernels, reduce_grads(): pl.pallas_call(functools.partial(reduce_kernel, ndp, nt), in_specs=[any_s...  168 us
    all_to_all x3, waiting for transfers between devices, to_positions(): return lax.all_to_all(a, 'tensor', split_axis=1, concat_axis=0, tiled=True)  47.1 us
    pallas_call x1, Pallas kernels, feed(): pl.pallas_call(functools.partial(feed_kernel, spd), grid=(nt, subs), in_s...  22.5 us
    pallas_call x1, Pallas kernels, cross_bwd(): pl.pallas_call(functools.partial(cross_bwd_kernel, spd), grid=(nt,), in_s...  19.9 us
    all_to_all x3, waiting for transfers between devices, swap_dp(): lax.all_to_all(route_rows(selector_out, a), 'dp', split_axis=0, concat_ax...  18.8 us
    all_to_all x3, waiting for transfers between devices, to_sequences(): return lax.all_to_all(a, 'tensor', split_axis=0, concat_axis=1, tiled=True)  17 us
    unnamed x45, local copies, waits for them, and re-layouts  16.5 us
  transfers between devices with their start and end apart: 9, of which 7 were waited for; matrix products, arithmetic and copies ran while one was open for 8% of the time, Pallas kernels for 62%

profile of v1, /device:TPU:0, one launch (start us, length us, event | category | flops | bytes accessed | tf_op | source)
XLA Modules:
  0.0 708.1 jit_solution(1781881897422232207)
XLA Ops:
  0.7 0.9 select_reduce_fusion
  1.6 1.5 convolution_convert_fusion.7
  3.5 14.7 %all_to_all.119 = bf16[8,32,1024]{2,1,0:T(8,128)(2,1)S(1)} all-to-all(bf16[8,32,1024]{2,1,0:T(8,128)(2,1)S(1)} %copy.142), channel_id=1, replica_groups=mesh['dp'=8,'tensor'=4] {'dp'}, dimensions={0} | all-to-all | bytes 1048576 | tf_op jit(solution)/shard_map/all_to_all | solution.py:920
  18.2 4.9 all-to-all-start.4
  23.1 0.8 convolution_convert_fusion.3
  23.9 1.5 copy.158
  25.5 11.5 %all-to-all-done.4 = bf16[8,32,1024]{2,1,0:T(8,128)(2,1)S(1)} async-done(((bf16[8,32,1024]{2,1,0:T(8,128)(2,1)}), bf16[8,32,1024]{2,1,0:T(8,128)(2,1)S(1)}, u32[]{:S(2)}, u32[]{:S(2)}) %all-to-all-start.4) | async-done | bytes 524320 | tf_op jit(solution)/shard_map/all_to_all | solution.py:927
  36.9 3.6 all-to-all-start.2
  40.9 1.1 copy.145
  42.0 13.8 %all-to-all-done.2 = bf16[8,64,1024]{2,1,0:T(8,128)(2,1)S(1)} async-done(((bf16[8,64,1024]{2,1,0:T(8,128)(2,1)}), bf16[8,64,1024]{2,1,0:T(8,128)(2,1)S(1)}, u32[]{:S(2)}, u32[]{:S(2)}) %all-to-all-start.2) | async-done | bytes 1048608 | tf_op jit(solution)/shard_map/all_to_all | solution.py:920
  55.8 3.5 all-to-all-start.1
  59.3 1.0 copy.147
  60.3 1.0 copy.148
  61.3 2.0 copy.149
  63.4 0.7 convolution_convert_fusion.2
  64.1 1.6 copy.161
  65.7 5.5 all-to-all-done.1
  71.2 3.7 all-to-all-start.3
  74.9 1.7 pad_maximum_fusion.1
  76.6 2.6 copy.150
  79.2 2.0 copy.151
  81.2 2.0 copy.152
  83.3 2.0 copy.153
  85.3 1.7 pad_maximum_fusion.2
  87.0 2.6 copy.154
  89.6 4.1 copy.155
  93.7 6.7 pad_maximum_fusion.own_ref
  100.3 261.5 %gather_weights.1 = bf16[4,4,8,128,1024]{4,3,2,1,0:T(8,128)(2,1)} custom-call(bf16[4,8,128,1024]{3,2,1,0:T(8,128)(2,1)} %pad_maximum_fusion.own_ref), custom_call_target="tpu_custom_call" | custom-call | tf_op jit(solution)/shard_map/gather_weights/pallas_call | solution.py:650
  362.0 0.6 dynamic_slice.6.lens
  363.2 0.9 copy.163
  364.0 0.8 copy.146
  364.9 9.6 %self_fwd.1 = (bf16[256,1024]{1,0:T(8,128)(2,1)}, bf16[4,256,256]{2,1,0:T(8,128)(2,1)}, bf16[4,256,256]{2,1,0:T(8,128)(2,1)}, bf16[4,256,256]{2,1,0:T(8,128)(2,1...) custom-call(s32[2]{0:T(128)} %dynamic_slice.6.lens, bf16[256,1024]{1,0:T(8,128)(2,1)} %bitcast.84, f32[3,1024]{1,0:T(4,128)} %gain.9, ...), custom_call_target="tpu_custom_call" | custom-call | tf_op jit(solution)/shard_map/self_fwd/pallas_call | solution.py:133
  374.5 1.0 copy.162
  375.6 11.0 %cross_fwd.1 = (bf16[256,1024]{1,0:T(8,128)(2,1)}, bf16[4,256,256]{2,1,0:T(8,128)(2,1)}, bf16[4,512,256]{2,1,0:T(8,128)(2,1)}, bf16[4,512,256]{2,1,0:T(8,128)(2,...) custom-call(s32[2]{0:T(128)} %dynamic_slice.7.lens, f32[256,1024]{1,0:T(8,128)} %get-tuple-element.41.h1_ref, ...), custom_call_target="tpu_custom_call" | custom-call | tf_op jit(solution)/shard_map/cross_fwd/pallas_call | solution.py:194
  386.6 22.5 %feed_forward.1 = (bf16[256,1024]{1,0:T(8,128)(2,1)}, f32[256,1024]{1,0:T(8,128)}, f32[2,1024]{1,0:T(2,128)}, bf16[4,1024,1024]{2,1,0:T(8,128)(2,1)}, bf16[4,1024,1024]{2,1,0:T(8,128)(2,1)}) custom-call(s32[2]{0:T(128)} %dynamic_slice.6.lens, f32[256,1024]{1,0:T(8,128)} %get-tuple-element.42.h2_ref, bf16[256,1024]{1,0:T(8,128)(2,1)} %bitcast.89, ...), custom_call_target="tpu_custom_call" | custom-call | tf_op jit(solution)/shard_map/feed_forward/pallas_call | solution.py:297
  409.0 19.9 %cross_bwd.1 = (bf16[512,1024]{1,0:T(8,128)(2,1)}, f32[256,1024]{1,0:T(8,128)}, f32[2,1024]{1,0:T(2,128)}, bf16[4,1024,1024]{2,1,0:T(8,128)(2,1)}) custom-call(s32[2]{0:T(128)} %dynamic_slice.7.lens, f32[256,1024]{1,0:T(8,128)} %get-tuple-element.44.dh2_ref, f32[256,1024]{1,0:T(8,128)} %get-tuple-element.41.h1_ref, ...), custom_call_target="tpu_custom_call" | custom-call | tf_op jit(solution)/shard_map/cross_bwd/pallas_call | solution.py:407
  428.9 15.7 %self_bwd.1 = (bf16[256,1024]{1,0:T(8,128)(2,1)}, f32[2,1024]{1,0:T(2,128)}, bf16[4,1024,1024]{2,1,0:T(8,128)(2,1)}) custom-call(s32[2]{0:T(128)} %dynamic_slice.6.lens, f32[256,1024]{1,0:T(8,128)} %get-tuple-element.50.dh1_ref, bf16[256,1024]{1,0:T(8,128)(2,1)} %bitcast.85, bf16[256,1024]{1,0:T(8,128)(2,1)} %get-tuple-element.51.n1_ref, f32[3,1024]{1,0:T(4,128)} %gain.9, ...), custom_call_target="tpu_custom_call" | custom-call | tf_op jit(solution)/shard_map/self_bwd/pallas_call | solution.py:510
  444.7 2.5 copy.166
  447.1 4.8 all-to-all-start.6
  452.0 1.3 copy.164
  453.3 12.0 %all-to-all-done.6 = bf16[2,128,1024]{2,0,1:T(2,128)(2,1)S(1)} async-done(((bf16[2,128,1024]{2,0,1:T(2,128)(2,1)}), bf16[2,128,1024]{2,0,1:T(2,128)(2,1)S(1)}, u32[]{:S(2)}, u32[]{:S(2)}) %all-to-all-start.6) | async-done | bytes 524320 | tf_op jit(solution)/shard_map/all_to_all | solution.py:931
  465.3 3.5 all-to-all-start.5
  468.8 2.0 copy.172
  470.8 11.7 %all-to-all-done.5 = bf16[2,128,1024]{2,0,1:T(2,128)(2,1)S(1)} async-done(((bf16[2,128,1024]{2,0,1:T(2,128)(2,1)}), bf16[2,128,1024]{2,0,1:T(2,128)(2,1)S(1)}, u32[]{:S(2)}, u32[]{:S(2)}) %all-to-all-start.5) | async-done | bytes 524320 | tf_op jit(solution)/shard_map/all_to_all | solution.py:931
  482.5 3.5 all-to-all-start.8
  486.6 1.1 copy.170
  487.7 23.5 %all-to-all-done.8 = bf16[2,256,1024]{2,0,1:T(2,128)(2,1)S(1)} async-done(((bf16[2,256,1024]{2,0,1:T(2,128)(2,1)}), bf16[2,256,1024]{2,0,1:T(2,128)(2,1)S(1)}, u32[]{:S(2)}, u32[]{:S(2)}) %all-to-all-start.8) | async-done | bytes 1048608 | tf_op jit(solution)/shard_map/all_to_all | solution.py:931
  511.2 4.1 all-to-all-start.7
  515.4 0.7 concatenate.12.sums_ref
  516.1 168.0 %reduce_grads.1 = (f32[4,128,1024]{2,1,0:T(8,128)}, f32[8,1024]{1,0:T(8,128)}) custom-call(bf16[4,4,2,128,1024]{4,3,2,1,0:T(8,128)(2,1)} %bitcast.80, bf16[4,4,2,128,1024]{4,3,2,1,0:T(8,128)(2,1)} %bitcast.79, bf16[4,4,2,128,1024]{4,3,2,1,0:T(8,128)(2,1)} %bitcast.77, bf16[4,4,2,128,1024]{4,3,2,1,0:T(8,128)(2,1)} %bitcast.78, f32[8,1024]{1,0:T(8,128)} %concatenate.12.sums_ref), custom_call_target="tpu_custom_call" | custom-call | tf_op jit(solution)/shard_map/reduce_grads/pallas_call | solution.py:876
  684.4 0.7 convolution_convert_fusion.1
  685.1 1.6 copy.176
  686.7 3.6 all-to-all-start.9
  690.3 2.7 slice_bitcast_fusion
  693.0 0.9 slice_bitcast_fusion.4
  693.9 0.8 copy.180
  694.6 0.8 copy.181
  695.4 2.1 copy.182
  697.5 0.6 fusion.26
  698.1 0.9 copy.165
  699.5 1.1 copy.178
  700.6 5.0 all-to-all-done.9
  705.6 0.7 convolution_convert_fusion
  706.3 1.6 copy.179
  (53 shorter events, 3.0 us)
Async XLA Ops:
  0.6 22.4 %copy-start = (bf16[8,64,1024]{2,1,0:T(8,128)(2,1)S(1)}, bf16[8,64,1024]{2,1,0:T(8,128)(2,1)}, u32[]{:S(2)}) copy-start(bf16[8,64,1024]{2,1,0:T(8,128)(2,1)} %param.19) | copy-start | bytes 3145732
  18.2 18.7 %all-to-all-start.4 = ((bf16[8,32,1024]{2,1,0:T(8,128)(2,1)}), bf16[8,32,1024]{2,1,0:T(8,128)(2,1)S(1)}, u32[]{:S(2)}, u32[]{:S(2)}) async-start(bf16[8,32,1024]{2,1,0:T(8,128)(2,1)} %param.20), calls=%async_computation.4 | async-start | bytes 1048576 | tf_op jit(solution)/shard_map/all_to_all | solution.py:927
  23.9 35.4 %copy-start.8 = (bf16[1024,256]{1,0:T(8,128)(2,1)S(1)}, bf16[1024,256]{1,0:T(8,128)(2,1)}, u32[]{:S(2)}) copy-start(bf16[1024,256]{1,0:T(8,128)(2,1)} %param.24) | copy-start | bytes 1572868
  23.9 36.4 %copy-start.9 = (bf16[1024,256]{1,0:T(8,128)(2,1)S(1)}, bf16[1024,256]{1,0:T(8,128)(2,1)}, u32[]{:S(2)}) copy-start(bf16[1024,256]{1,0:T(8,128)(2,1)} %param.25) | copy-start | bytes 1572868
  36.9 26.5 %copy-start.3 = (bf16[8,32,1024]{2,1,0:T(8,128)(2,1)}, bf16[8,32,1024]{2,1,0:T(8,128)(2,1)S(1)}, u32[]{:S(2)}) copy-start(bf16[8,32,1024]{2,1,0:T(8,128)(2,1)S(1)} %all-to-all-done.4) | copy-start | bytes 1572868
  36.9 18.9 %all-to-all-start.2 = ((bf16[8,64,1024]{2,1,0:T(8,128)(2,1)}), bf16[8,64,1024]{2,1,0:T(8,128)(2,1)S(1)}, u32[]{:S(2)}, u32[]{:S(2)}) async-start(bf16[8,64,1024]{2,1,0:T(8,128)(2,1)} %copy.158), calls=%async_computation.2 | async-start | bytes 2097152 | tf_op jit(solution)/shard_map/all_to_all | solution.py:920
  55.8 15.4 %all-to-all-start.1 = ((bf16[8,32,1024]{2,1,0:T(8,128)(2,1)}), bf16[8,32,1024]{2,1,0:T(8,128)(2,1)S(1)}, u32[]{:S(2)}, u32[]{:S(2)}) async-start(bf16[8,32,1024]{2,1,0:T(8,128)(2,1)} %copy.145), calls=%async_computation.1 | async-start | bytes 1048576 | tf_op jit(solution)/shard_map/all_to_all | solution.py:927
  71.2 3.7 copy-start.5
  71.2 303.4 %all-to-all-start.3 = ((bf16[8,64,1024]{2,1,0:T(8,128)(2,1)}), bf16[8,64,1024]{2,1,0:T(8,128)(2,1)S(1)}, u32[]{:S(2)}, u32[]{:S(2)}) async-start(bf16[8,64,1024]{2,1,0:T(8,128)(2,1)} %copy.161), calls=%async_computation.3 | async-start | bytes 2097152 | tf_op jit(solution)/shard_map/all_to_all | solution.py:927
  89.6 4.1 copy-start.2
  100.3 261.5 %copy-start.15 = (s32[64]{0:T(128)S(1)}, s32[64]{0:T(128)}, u32[]{:S(2)}) copy-start(s32[64]{0:T(128)} %param.22) | copy-start | bytes 772
  100.3 261.5 %copy-start.16 = (s32[64]{0:T(128)S(1)}, s32[64]{0:T(128)}, u32[]{:S(2)}) copy-start(s32[64]{0:T(128)} %param.21) | copy-start | bytes 772
  100.3 262.9 %copy-start.4 = (bf16[8,32,1024]{2,1,0:T(8,128)(2,1)S(1)}, bf16[8,32,1024]{2,1,0:T(8,128)(2,1)}, u32[]{:S(2)}) copy-start(bf16[8,32,1024]{2,1,0:T(8,128)(2,1)} %copy-done.3) | copy-start | bytes 1572868
  100.3 263.7 %copy-start.6 = (bf16[8,32,1024]{2,1,0:T(8,128)(2,1)S(1)}, bf16[8,32,1024]{2,1,0:T(8,128)(2,1)}, u32[]{:S(2)}) copy-start(bf16[8,32,1024]{2,1,0:T(8,128)(2,1)} %copy-done.5) | copy-start | bytes 1572868
  428.9 23.1 %copy-start.10 = (bf16[256,1024]{1,0:T(8,128)(2,1)S(1)}, bf16[256,1024]{1,0:T(8,128)(2,1)}, u32[]{:S(2)}) copy-start(bf16[256,1024]{1,0:T(8,128)(2,1)} %get-tuple-element.43) | copy-start | bytes 1572868
  444.6 24.1 %copy-start.7 = (bf16[512,1024]{1,0:T(8,128)(2,1)S(1)}, bf16[512,1024]{1,0:T(8,128)(2,1)}, u32[]{:S(2)}) copy-start(bf16[512,1024]{1,0:T(8,128)(2,1)} %get-tuple-element.57) | copy-start | bytes 3145732
  444.6 41.4 %copy-start.14 = (f32[2,1024]{1,0:T(2,128)S(1)}, f32[2,1024]{1,0:T(2,128)}, u32[]{:S(2)}) copy-start(f32[2,1024]{1,0:T(2,128)} %get-tuple-element.62) | copy-start | bytes 24580
  444.6 41.4 %copy-start.13 = (f32[2,1024]{1,0:T(2,128)S(1)}, f32[2,1024]{1,0:T(2,128)}, u32[]{:S(2)}) copy-start(f32[2,1024]{1,0:T(2,128)} %get-tuple-element.63) | copy-start | bytes 24580
  447.1 18.2 %all-to-all-start.6 = ((bf16[2,128,1024]{2,0,1:T(2,128)(2,1)}), bf16[2,128,1024]{2,0,1:T(2,128)(2,1)S(1)}, u32[]{:S(2)}, u32[]{:S(2)}) async-start(bf16[2,128,1024]{2,0,1:T(2,128)(2,1)} %copy.166), calls=%async_computation.6 | async-start | bytes 1048576 | tf_op jit(solution)/shard_map/all_to_all | solution.py:931
  465.3 17.2 %all-to-all-start.5 = ((bf16[2,128,1024]{2,0,1:T(2,128)(2,1)}), bf16[2,128,1024]{2,0,1:T(2,128)(2,1)S(1)}, u32[]{:S(2)}, u32[]{:S(2)}) async-start(bf16[2,128,1024]{2,0,1:T(2,128)(2,1)} %copy.164), calls=%async_computation.5 | async-start | bytes 1048576 | tf_op jit(solution)/shard_map/all_to_all | solution.py:931
  470.8 44.6 %copy-start.12 = (f32[2,1024]{1,0:T(2,128)S(1)}, f32[2,1024]{1,0:T(2,128)}, u32[]{:S(2)}) copy-start(f32[2,1024]{1,0:T(2,128)} %get-tuple-element.64) | copy-start | bytes 24580
  482.5 28.7 %all-to-all-start.8 = ((bf16[2,256,1024]{2,0,1:T(2,128)(2,1)}), bf16[2,256,1024]{2,0,1:T(2,128)(2,1)S(1)}, u32[]{:S(2)}, u32[]{:S(2)}) async-start(bf16[2,256,1024]{2,0,1:T(2,128)(2,1)} %copy.172), calls=%async_computation.8 | async-start | bytes 2097152 | tf_op jit(solution)/shard_map/all_to_all | solution.py:931
  511.2 175.5 %all-to-all-start.7 = ((bf16[8,32,1024]{2,1,0:T(8,128)(2,1)}), bf16[8,32,1024]{2,1,0:T(8,128)(2,1)S(1)}, u32[]{:S(2)}, u32[]{:S(2)}) async-start(bf16[8,32,1024]{2,1,0:T(8,128)(2,1)} %copy.170), calls=%async_computation.7 | async-start | bytes 1048576 | tf_op jit(solution)/shard_map/all_to_all | solution.py:920
  686.7 18.9 %all-to-all-start.9 = ((bf16[8,64,1024]{2,1,0:T(8,128)(2,1)}), bf16[8,64,1024]{2,1,0:T(8,128)(2,1)S(1)}, u32[]{:S(2)}, u32[]{:S(2)}) async-start(bf16[8,64,1024]{2,1,0:T(8,128)(2,1)} %copy.176), calls=%async_computation.9 | async-start | bytes 2097152 | tf_op jit(solution)/shard_map/all_to_all | solution.py:920
  690.3 7.3 %copy-start.11 = (f32[8,1024]{1,0:T(8,128)S(1)}, f32[8,1024]{1,0:T(8,128)}, u32[]{:S(2)}) copy-start(f32[8,1024]{1,0:T(8,128)} %get-tuple-element.66) | copy-start | bytes 98308
  695.4 12.5 %copy-start.1 = (bf16[8,64,1024]{2,1,0:T(8,128)(2,1)S(1)}, bf16[8,64,1024]{2,1,0:T(8,128)(2,1)}, u32[]{:S(2)}) copy-start(bf16[8,64,1024]{2,1,0:T(8,128)(2,1)} %param.19) | copy-start | bytes 3145732

commit v2 on v1

--- a/solution.py
+++ b/solution.py
@@ -98,122 +98,6 @@
 
 
 SMEM = pl.BlockSpec(memory_space=pltpu.SMEM)
-
-
-def self_fwd_kernel(spd, lens, x_ref, gain, bias, w_ref, n1_ref, q_ref, k_ref, v_ref, o_ref, h_ref):
-    j = pl.program_id(0)
-    seq = x_ref.shape[0] // spd
-    hc = q_ref.shape[2]
-
-    @pl.when(j == 0)
-    def _():
-        x = x_ref[...].astype(F32)
-        nh, _ = norm_parts(x)
-        n1_ref[...] = (nh * gain[0:1] + bias[0:1]).astype(BF16)
-        h_ref[...] = x
-
-    w = w_ref.at[0, 0]
-    qkv = dot_nn(n1_ref[...], w[:, : 3 * hc]).astype(BF16)
-    q_ref[0] = qkv[:, :hc]
-    k_ref[0] = qkv[:, hc : 2 * hc]
-    v_ref[0] = qkv[:, 2 * hc :]
-    for i in range(spd):
-        rows = slice(i * seq, (i + 1) * seq)
-        o_ref[0, rows] = attn_fwd(
-            q_ref[0, rows], k_ref[0, rows], v_ref[0, rows], lens[i], True
-        )
-    h_ref[...] += dot_nt(o_ref[0], w[:, 3 * hc :])
-
-
-def self_fwd(lens, x, gain, bias, wg, spd, nt):
-    n, dim = x.shape
-    hc = wg.shape[3] // 4
-    part = pl.BlockSpec((1, n, hc), lambda j: (j, 0, 0))
-    shaped = jax.ShapeDtypeStruct((nt, n, hc), BF16)
-    return pl.pallas_call(
-        functools.partial(self_fwd_kernel, spd),
-        grid=(nt,),
-        in_specs=[
-            SMEM,
-            whole((n, dim)),
-            whole(gain.shape),
-            whole(bias.shape),
-            pl.BlockSpec((1, 1, dim, 4 * hc), lambda j: (j, 0, 0, 0)),
-        ],
-        out_specs=[whole((n, dim)), part, part, part, part, whole((n, dim))],
-        out_shape=[
-            jax.ShapeDtypeStruct((n, dim), BF16),
-            shaped,
-            shaped,
-            shaped,
-            shaped,
-            jax.ShapeDtypeStruct((n, dim), F32),
-        ],
-        compiler_params=params(1),
-        name="self_fwd",
-    )(lens, x, gain, bias, wg)
-
-
-def cross_fwd_kernel(
-    spd, lens, h1_ref, ed_ref, gain, bias, w_ref, n2_ref, q_ref, k_ref, v_ref, o_ref, h_ref
-):
-    j = pl.program_id(0)
-    seq = h1_ref.shape[0] // spd
-    enc = ed_ref.shape[0] // spd
-    hc = q_ref.shape[2]
-
-    @pl.when(j == 0)
-    def _():
-        h = h1_ref[...]
-        nh, _ = norm_parts(h)
-        n2_ref[...] = (nh * gain[1:2] + bias[1:2]).astype(BF16)
-        h_ref[...] = h
-
-    w = w_ref.at[0, 0]
-    q_ref[0] = dot_nn(n2_ref[...], w[:, :hc]).astype(BF16)
-    kv = dot_nn(ed_ref[...], w[:, hc : 3 * hc]).astype(BF16)
-    k_ref[0] = kv[:, :hc]
-    v_ref[0] = kv[:, hc:]
-    for i in range(spd):
-        rows = slice(i * seq, (i + 1) * seq)
-        keys = slice(i * enc, (i + 1) * enc)
-        o_ref[0, rows] = attn_fwd(
-            q_ref[0, rows], k_ref[0, keys], v_ref[0, keys], lens[i], False
-        )
-    h_ref[...] += dot_nt(o_ref[0], w[:, 3 * hc :])
-
-
-def cross_fwd(lens, h1, ed, gain, bias, wg, spd, nt):
-    n, dim = h1.shape
-    m = ed.shape[0]
-    hc = wg.shape[3] // 4
-    part = pl.BlockSpec((1, n, hc), lambda j: (j, 0, 0))
-    keys = pl.BlockSpec((1, m, hc), lambda j: (j, 0, 0))
-    shaped = jax.ShapeDtypeStruct((nt, n, hc), BF16)
-    long = jax.ShapeDtypeStruct((nt, m, hc), BF16)
-    return pl.pallas_call(
-        functools.partial(cross_fwd_kernel, spd),
-        grid=(nt,),
-        in_specs=[
-            SMEM,
-            whole((n, dim)),
-            whole((m, dim)),
-            whole(gain.shape),
-            whole(bias.shape),
-            pl.BlockSpec((1, 1, dim, 4 * hc), lambda j: (j, 1, 0, 0)),
-        ],
-        out_specs=[whole((n, dim)), part, keys, keys, part, whole((n, dim))],
-        out_shape=[
-            jax.ShapeDtypeStruct((n, dim), BF16),
-            shaped,
-            long,
-            long,
-            shaped,
-            jax.ShapeDtypeStruct((n, dim), F32),
-        ],
-        compiler_params=params(1),
-        name="cross_fwd",
-    )(lens, h1, ed, gain, bias, wg)
 
 
 def row_valid(lens, spd, n):
@@ -554,6 +438,15 @@
     return out
 
 
+def xor_of(a, b, size):
+    out = 0
+    bit = 1
+    while bit < size:
+        out = out + bit * lax.rem(lax.div(a, bit) + lax.div(b, bit), 2)
+        bit *= 2
+    return out
+
+
 def greet(peers):
     barrier = pltpu.get_barrier_semaphore()
     for peer in peers:
@@ -561,14 +454,76 @@
     pl.semaphore_wait(barrier, len(peers))
 
 
-def gather_kernel(ndp, nt, own_ref, out_ref, own_sem, send_sems, recv_sems):
+def front_kernel(
+    ndp,
+    nt,
+    spd,
+    tok_lens,
+    enc_lens,
+    in_peer,
+    tok_blocks,
+    enc_blocks,
+    cot_ref,
+    w_refs,
+    gain,
+    bias,
+    wg,
+    x_ref,
+    ed_ref,
+    cots_ref,
+    n1_ref,
+    q1_ref,
+    k1_ref,
+    v1_ref,
+    o1_ref,
+    h1_ref,
+    n2_ref,
+    q2_ref,
+    k2_ref,
+    v2_ref,
+    o2_ref,
+    h2_ref,
+    rx_tok,
+    rx_enc,
+    zs_tok,
+    zs_enc,
+    own,
+    raw_o,
+    raw_out,
+    wbuf,
+    load_sems,
+    own_sem,
+    wbuf_sems,
+    tok_send,
+    tok_recv,
+    enc_send,
+    enc_recv,
+    zt_send,
+    zt_recv,
+    ze_send,
+    ze_recv,
+    zc_send,
+    zc_recv,
+    line_send,
+    pass_send,
+    send_sems,
+    recv_sems,
+):
     d = lax.axis_index("dp")
     t = lax.axis_index("tensor")
-    groups = own_ref.shape[0]
-    half = own_ref.shape[2] // 2
+    dim, width = own.shape[1:]
+    hc = width // 4
+    rows_each = dim // ndp
+    half = rows_each // 2
     bits = ndp.bit_length() - 1
     chip_bits = [1 << b for b in range(1, bits)]
     orders = (chip_bits, chip_bits[::-1])
+    levels = len(chip_bits)
+    seqs, lr = cot_ref.shape[0], cot_ref.shape[1]
+    le = enc_blocks.shape[1]
+    seq, enc = nt * lr, nt * le
+    n, m = spd * seq, spd * enc
+    waits = []
 
     def dp_peer(bit):
         return (flip(d, bit), t)
@@ -576,93 +531,356 @@
     def t_peer(j):
         return (d, flip(t, j))
 
-    greet([dp_peer(1 << b) for b in range(bits)] + [t_peer(j) for j in range(1, nt)])
-    own = pltpu.make_async_copy(own_ref, out_ref.at[0], own_sem)
-    own.start()
-
-    chunks = [(g, j) for g in range(groups) for j in range(1, nt)]
-    started = []
-
-    def send(c, slot, src, dst, peer):
-        copy = pltpu.make_async_remote_copy(
+    def slab(index, side=None):
+        if side is None:
+            return pl.ds(pl.multiple_of(index * rows_each, rows_each), rows_each)
+        return pl.ds(pl.multiple_of(index * rows_each + side * half, half), half)
+
+    def remote(src, dst, ssem, rsem, peer):
+        return pltpu.make_async_remote_copy(
             src_ref=src,
             dst_ref=dst,
-            send_sem=send_sems.at[c, slot],
-            recv_sem=recv_sems.at[c, slot],
+            send_sem=ssem,
+            recv_sem=rsem,
             device_id=peer,
             device_id_type=MESH,
         )
+
+    def send(*args):
+        copy = remote(*args)
         copy.start()
-        started.append(copy)
+        waits.append(copy)
         return copy
 
-    first = [
-        send(c, 0, own_ref.at[g, d], out_ref.at[j, g, d], t_peer(j))
-        for c, (g, j) in enumerate(chunks)
+    def local(src, dst, sem):
+        copy = pltpu.make_async_copy(src, dst, sem)
+        copy.start()
+        return copy
+
+    greet([dp_peer(e) for e in range(1, ndp)] + [t_peer(j) for j in range(1, nt)])
+
+    def to_peers(blocks, rx, ssem, rsem):
+        return [
+            send(blocks.at[flip(d, e)], rx.at[d], ssem.at[e], rsem.at[e], dp_peer(e))
+            for e in range(1, ndp)
+        ], local(blocks.at[d], rx.at[d], rsem.at[0])
+
+    tok_copies, tok_own = to_peers(tok_blocks, rx_tok, tok_send, tok_recv)
+
+    wq1, wk1, wv1, wo1, wq2, wk2, wv2, wo2, w_in, w_out = w_refs
+    loads = [
+        local(src, dst, load_sems.at[i])
+        for i, (src, dst) in enumerate(
+            [
+                (wo1, raw_o.at[0]),
+                (wq1, own.at[0, :, pl.ds(0, hc)]),
+                (wk1, own.at[0, :, pl.ds(hc, hc)]),
+                (wv1, own.at[0, :, pl.ds(2 * hc, hc)]),
+                (wo2, raw_o.at[1]),
+                (wq2, own.at[1, :, pl.ds(0, hc)]),
+                (wk2, own.at[1, :, pl.ds(hc, hc)]),
+                (wv2, own.at[1, :, pl.ds(2 * hc, hc)]),
+                (w_in, own.at[2]),
+                (w_out, raw_out),
+            ]
+        )
     ]
+
+    chunks = [(g, j) for g in range(4) for j in range(1, nt)]
+
+    def line_copy(g, step):
+        there = t + step
+        j = xor_of(t, there, nt)
+        return remote(
+            own.at[g, slab(d)],
+            wg.at[j, g, slab(d)],
+            line_send.at[g, (step + 1) // 2],
+            recv_sems.at[g * (nt - 1) + j - 1, 0],
+            (d, there),
+        )
+
+    def pass_copy(c, step):
+        g, j = chunks[c]
+        there = t + step
+        j_there = xor_of(flip(t, j), there, nt)
+        return remote(
+            wg.at[j, g, slab(d)],
+            wg.at[j_there, g, slab(d)],
+            pass_send.at[c],
+            recv_sems.at[g * (nt - 1) + j_there - 1, 0],
+            (d, there),
+        )
+
+    def on_line(act, g):
+        @pl.when(t + 1 < nt)
+        def _():
+            act(line_copy(g, 1))
+
+        @pl.when(t >= 1)
+        def _():
+            act(line_copy(g, -1))
+
+    def on_pass(act, c):
+        s = flip(t, chunks[c][1])
+
+        @pl.when((s < t) & (t + 1 < nt))
+        def _():
+            act(pass_copy(c, 1))
+
+        @pl.when((s > t) & (t >= 1))
+        def _():
+            act(pass_copy(c, -1))
+
+    def start(copy):
+        copy.start()
+
+    def arrived(c):
+        g, j = chunks[c]
+        at = wg.at[j, g, slab(d)]
+        remote(at, at, pass_send.at[c], recv_sems.at[c, 0], t_peer(j)).wait_recv()
+        on_pass(start, c)
+
     pending = {}
 
     def spread(c, level):
         g, j = chunks[c]
         if level == 0:
-            first[c].wait_recv()
+            arrived(c)
         else:
             for copy in pending.pop((c, level)):
                 copy.wait_recv()
         slot = 1 + 2 * ((1 << level) - 1)
         copies = []
-        if level < len(chip_bits):
+        if level < levels:
             for side, order in enumerate(orders):
                 held = [0]
                 for bit in order[:level]:
                     held += [e ^ bit for e in held]
-                rows = pl.ds(side * half, half)
                 for e in held:
-                    at = out_ref.at[j, g, flip(d, e), rows]
-                    copies.append(send(c, slot, at, at, dp_peer(order[level])))
+                    at = wg.at[j, g, slab(flip(d, e), side)]
+                    copies.append(
+                        send(
+                            at,
+                            at,
+                            send_sems.at[c, slot],
+                            recv_sems.at[c, slot],
+                            dp_peer(order[level]),
+                        )
+                    )
                     slot += 1
-        else:
+        elif level == levels:
             for e in range(0, ndp, 2):
-                at = out_ref.at[j, g, flip(d, e)]
-                copies.append(send(c, slot, at, at, dp_peer(1)))
+                at = wg.at[j, g, slab(flip(d, e))]
+                copies.append(
+                    send(at, at, send_sems.at[c, slot], recv_sems.at[c, slot], dp_peer(1))
+                )
                 slot += 1
-        pending[(c, level + 1)] = copies
-
-    levels = len(chip_bits) + 1
-    for tick in range(len(chunks) + levels - 1):
-        for level in range(levels):
-            c = tick - level
-            if 0 <= c < len(chunks):
-                spread(c, level)
-    for copies in pending.values():
+        elif g < 2:
+            fills[c] = local(wg.at[j, g], wbuf.at[c % 2], wbuf_sems.at[c % 2])
+        if copies:
+            pending[(c, level + 1)] = copies
+
+    fills = {}
+
+    def to_sequences(src, dst, rows, ssem, rsem):
+        for j in range(1, nt):
+            there = flip(t, j)
+            send(
+                src.at[pl.ds(there * spd, spd)],
+                dst.at[:, pl.ds(pl.multiple_of(t * rows, rows), rows)],
+                ssem.at[j],
+                rsem.at[j],
+                t_peer(j),
+            )
+        return local(
+            src.at[pl.ds(t * spd, spd)],
+            dst.at[:, pl.ds(pl.multiple_of(t * rows, rows), rows)],
+            rsem.at[0],
+        )
+
+    def sequences_here(own_copy, src, dst, rows, ssem, rsem):
+        own_copy.wait()
+        for j in range(1, nt):
+            there = flip(t, j)
+            remote(
+                src.at[pl.ds(t * spd, spd)],
+                dst.at[:, pl.ds(pl.multiple_of(there * rows, rows), rows)],
+                ssem.at[j],
+                rsem.at[j],
+                t_peer(j),
+            ).wait_recv()
+
+    def blocks_here(copies, own_copy, rx, zs):
+        own_copy.wait()
         for copy in copies:
             copy.wait_recv()
-    for copy in started:
+        for i in range(seqs):
+            zs[i] = rx[in_peer[i]]
+
+    def self_norm():
+        x = x_ref[...].reshape(n, dim).astype(F32)
+        nh, _ = norm_parts(x)
+        n1_ref[...] = (nh * gain[0:1] + bias[0:1]).astype(BF16)
+        h1_ref[...] = x
+
+    def self_part(j, w):
+        qkv = dot_nn(n1_ref[...], w[:, : 3 * hc]).astype(BF16)
+        q1_ref[j] = qkv[:, :hc]
+        k1_ref[j] = qkv[:, hc : 2 * hc]
+        v1_ref[j] = qkv[:, 2 * hc :]
+        for i in range(spd):
+            rows = slice(i * seq, (i + 1) * seq)
+            o1_ref[j, rows] = attn_fwd(
+                q1_ref[j, rows], k1_ref[j, rows], v1_ref[j, rows], tok_lens[i], True
+            )
+        h1_ref[...] += dot_nt(o1_ref[j], w[:, 3 * hc :])
+
+    def cross_norm():
+        h = h1_ref[...]
+        nh, _ = norm_parts(h)
+        n2_ref[...] = (nh * gain[1:2] + bias[1:2]).astype(BF16)
+        h2_ref[...] = h
+
+    def cross_part(j, w):
+        q2_ref[j] = dot_nn(n2_ref[...], w[:, :hc]).astype(BF16)
+        kv = dot_nn(ed_ref[...].reshape(m, dim), w[:, hc : 3 * hc]).astype(BF16)
+        k2_ref[j] = kv[:, :hc]
+        v2_ref[j] = kv[:, hc:]
+        for i in range(spd):
+            rows = slice(i * seq, (i + 1) * seq)
+            keys = slice(i * enc, (i + 1) * enc)
+            o2_ref[j, rows] = attn_fwd(
+                q2_ref[j, rows], k2_ref[j, keys], v2_ref[j, keys], enc_lens[i], False
+            )
+        h2_ref[...] += dot_nt(o2_ref[j], w[:, 3 * hc :])
+
+    for i in range(4):
+        loads[i].wait()
+    own[0, :, 3 * hc :] = raw_o[0].T
+    on_line(start, 0)
+    blocks_here(tok_copies, tok_own, rx_tok, zs_tok)
+    own_x = to_sequences(zs_tok, x_ref, lr, zt_send, zt_recv)
+    enc_copies, enc_own = to_peers(enc_blocks, rx_enc, enc_send, enc_recv)
+    for i in range(4, 10):
+        loads[i].wait()
+    own[1, :, 3 * hc :] = raw_o[1].T
+    block = min(256, width)
+    for at in range(0, width, block):
+        own[3, :, at : at + block] = raw_out[at : at + block].T
+    own_copy = local(own, wg.at[0], own_sem)
+
+    state = {}
+    ready = levels + 1
+    count = len(chunks)
+    per = nt - 1
+    for tick in range(count + ready):
+        for level in range(ready + 1):
+            c = tick - level
+            if 0 <= c < count:
+                spread(c, level)
+                if level == 0 and c % per == 0 and c // per + 1 < 4:
+                    on_line(start, c // per + 1)
+        if tick == 0:
+            blocks_here(enc_copies, enc_own, rx_enc, zs_enc)
+            own_ed = to_sequences(zs_enc, ed_ref, le, ze_send, ze_recv)
+        if tick == 2:
+            sequences_here(own_x, zs_tok, x_ref, lr, zt_send, zt_recv)
+            self_norm()
+            self_part(0, own.at[0])
+        c = tick - ready - 1
+        if 0 <= c < 2 * per:
+            g, j = chunks[c]
+            fills[c].wait()
+            (self_part if g == 0 else cross_part)(j, wbuf.at[c % 2])
+            if c == per - 1:
+                sequences_here(own_ed, zs_enc, ed_ref, le, ze_send, ze_recv)
+                own_cot = to_sequences(cot_ref, cots_ref, lr, zc_send, zc_recv)
+                cross_norm()
+                cross_part(0, own.at[1])
+
+    sequences_here(own_cot, cot_ref, cots_ref, lr, zc_send, zc_recv)
+    own_copy.wait()
+    for g in range(4):
+        on_line(lambda copy: copy.wait_send(), g)
+    for c in range(count):
+        on_pass(lambda copy: copy.wait_send(), c)
+    for copy in waits:
         copy.wait_send()
-    own.wait()
-
-
-def gather_weights(own, ndp, nt):
-    groups, dim, width = own.shape
-    rows = dim // ndp
-    count = groups * (nt - 1)
+
+
+def front(ndp, nt, spd, tok_lens, enc_lens, in_peer, tok_blocks, enc_blocks, cot, weights, gain, bias):
+    seqs, lr, dim = cot.shape
+    le = enc_blocks.shape[1]
+    seq, enc = nt * lr, nt * le
+    n, m = spd * seq, spd * enc
+    hc = weights[0].shape[1]
+    width = 4 * hc
+    count = 4 * (nt - 1)
     slots = 1 + 2 * (ndp // 2 - 1) + ndp // 2
-    out = pl.pallas_call(
-        functools.partial(gather_kernel, ndp, nt),
-        in_specs=[pl.BlockSpec(memory_space=pl.ANY)],
-        out_specs=pl.BlockSpec(memory_space=pl.ANY),
-        out_shape=jax.ShapeDtypeStruct((nt, groups, ndp, rows, width), BF16),
+    smem = pl.BlockSpec(memory_space=pltpu.SMEM)
+    vmem = pl.BlockSpec(memory_space=pltpu.VMEM)
+    any_space = pl.BlockSpec(memory_space=pl.ANY)
+    dma = pltpu.SemaphoreType.DMA
+    shape = jax.ShapeDtypeStruct
+    part, keys = shape((nt, n, hc), BF16), shape((nt, m, hc), BF16)
+
+    def body(*refs):
+        front_kernel(ndp, nt, spd, *refs[:6], refs[6:16], *refs[16:])
+
+    return pl.pallas_call(
+        body,
+        in_specs=[smem] * 3 + [any_space] * 13 + [vmem] * 2,
+        out_specs=[any_space, vmem, vmem, any_space] + [vmem] * 12,
+        out_shape=[
+            shape((nt, 4, dim, width), BF16),
+            shape((spd, seq, dim), BF16),
+            shape((spd, enc, dim), BF16),
+            shape((spd, seq, dim), BF16),
+            shape((n, dim), BF16),
+            part,
+            part,
+            part,
+            part,
+            shape((n, dim), F32),
+            shape((n, dim), BF16),
+            part,
+            keys,
+            keys,
+            part,
+            shape((n, dim), F32),
+        ],
         scratch_shapes=[
-            pltpu.SemaphoreType.DMA,
-            pltpu.SemaphoreType.DMA((count, slots)),
-            pltpu.SemaphoreType.DMA((count, slots)),
+            pltpu.VMEM((ndp, lr, dim), BF16),
+            pltpu.VMEM((ndp, le, dim), BF16),
+            pltpu.VMEM((seqs, lr, dim), BF16),
+            pltpu.VMEM((seqs, le, dim), BF16),
+            pltpu.VMEM((4, dim, width), BF16),
+            pltpu.VMEM((2, hc, dim), BF16),
+            pltpu.VMEM((width, dim), BF16),
+            pltpu.VMEM((2, dim, width), BF16),
+            dma((10,)),
+            dma,
+            dma((2,)),
+            dma((ndp,)),
+            dma((ndp,)),
+            dma((ndp,)),
+            dma((ndp,)),
+            dma((nt,)),
+            dma((nt,)),
+            dma((nt,)),
+            dma((nt,)),
+            dma((nt,)),
+            dma((nt,)),
+            dma((4, 2)),
+            dma((count,)),
+            dma((count, slots)),
+            dma((count, slots)),
         ],
         compiler_params=pltpu.CompilerParams(
             collective_id=0, has_side_effects=True, vmem_limit_bytes=VMEM_LIMIT
         ),
-        name="gather_weights",
-    )(own.reshape(groups, ndp, rows, width))
-    return out.reshape(nt, groups, dim, width)
+        name="front",
+    )(tok_lens, enc_lens, in_peer, tok_blocks, enc_blocks, cot, *weights, gain, bias)
 
 
 def reduce_kernel(
@@ -923,10 +1141,6 @@
     return route_rows(selector_in, sent)
 
 
-def to_sequences(a):
-    return lax.all_to_all(a, "tensor", split_axis=0, concat_axis=1, tiled=True)
-
-
 def to_positions(a):
     return lax.all_to_all(a, "tensor", split_axis=1, concat_axis=0, tiled=True)
 
@@ -968,22 +1182,33 @@
     tok_lens = lax.dynamic_slice(select_rows(tok_len, sources), (t * spd,), (spd,))
     enc_lens = lax.dynamic_slice(select_rows(enc_len, sources), (t * spd,), (spd,))
 
-    x = to_sequences(swap_dp(outward, inward, tokens)).reshape(-1, dim)
-    ed = to_sequences(swap_dp(outward, inward, enc_states)).reshape(-1, dim)
-    cot = to_sequences(cotangent).reshape(-1, dim)
-
-    own = jnp.stack(
-        [
-            jnp.concatenate([w_q_self, w_k_self, w_v_self, w_o_self.T], axis=1),
-            jnp.concatenate([w_q_cross, w_k_cross, w_v_cross, w_o_cross.T], axis=1),
-            w_in,
-            w_out.T,
-        ]
+    weights = (
+        w_q_self,
+        w_k_self,
+        w_v_self,
+        w_o_self,
+        w_q_cross,
+        w_k_cross,
+        w_v_cross,
+        w_o_cross,
+        w_in,
+        w_out,
     )
-    wg = gather_weights(own, ndp, nt)
-
-    n1, q1, k1, v1, o1, h1 = self_fwd(tok_lens, x, gain, bias, wg, spd, nt)
-    n2, q2, k2, v2, o2, h2 = cross_fwd(enc_lens, h1, ed, gain, bias, wg, spd, nt)
+    wg, x, ed, cot, n1, q1, k1, v1, o1, h1, n2, q2, k2, v2, o2, h2 = front(
+        ndp,
+        nt,
+        spd,
+        tok_lens,
+        enc_lens,
+        sources // seqs,
+        route_rows(outward, tokens),
+        route_rows(outward, enc_states),
+        cotangent,
+        weights,
+        gain,
+        bias,
+    )
+    x, ed, cot = x.reshape(-1, dim), ed.reshape(-1, dim), cot.reshape(-1, dim)
     res, dh2, sums3, dwi, dwo = feed(tok_lens, h2, cot, gain, bias, wg, spd, nt)
     ded, dh1, sums2, dwc = cross_bwd(
         enc_lens, dh2, h1, n2, ed, gain, q2, k2, v2, o2, wg, spd, nt

time: 714 us -> 490 us (0.69)
  Pallas kernels: 508 us -> 394 us
  waiting for transfers between devices: 82.9 us -> 39.9 us
  local copies, waits for them, and re-layouts: 49 us -> 24.4 us
  starting transfers between devices: 35.1 us -> 18.8 us
  blocking collectives: 14.7 us -> 0 us
  other arithmetic: 11.2 us -> 2.36 us
    pallas_call x3 -> x1, Pallas kernels: 282 us -> 168 us  [front(): pl.pallas_call(body, in_specs=[smem] * 3 + [any_space] * 13 + [vmem] * 2,...]
    all_to_all x3, waiting for transfers between devices: 47.1 us -> 27 us  [to_positions(): return lax.all_to_all(a, 'tensor', split_axis=1, concat_axis=0, tiled=True)]
    all_to_all x3 -> x0, waiting for transfers between devices: 17 us -> none  [to_sequences(): return lax.all_to_all(a, 'tensor', split_axis=0, concat_axis=1, tiled=True)]
    all_to_all x1 -> x0, blocking collectives: 14.7 us -> none  [swap_dp(): lax.all_to_all(route_rows(selector_out, a), 'dp', split_axis=0, concat_ax...]
    all_to_all x3 -> x0, starting transfers between devices: 12 us -> none  [to_sequences(): return lax.all_to_all(a, 'tensor', split_axis=0, concat_axis=1, tiled=True)]
    unnamed x45 -> x37, local copies, waits for them, and re-layouts: 16.5 us -> 6.48 us
    all_to_all x3 -> x2, waiting for transfers between devices: 18.8 us -> 12.9 us  [swap_dp(): lax.all_to_all(route_rows(selector_out, a), 'dp', split_axis=0, concat_ax...]
  transfers between devices with their start and end apart: 9 -> 5, of which waited for: 7 -> 4; matrix products, arithmetic and copies ran while one was open for 8% -> 4% of each run, Pallas kernels for 62% -> 35%
where the time goes in v2:
time: 490 us; the launch traced here: 486 us
  Pallas kernels  394 us (80%)
  waiting for transfers between devices  39.9 us (8%)
  local copies, waits for them, and re-layouts  24.4 us (5%)
  starting transfers between devices  18.8 us (4%)
    pallas_call x1, Pallas kernels, reduce_grads(): pl.pallas_call(functools.partial(reduce_kernel, ndp, nt), in_specs=[any_s...  169 us
    pallas_call x1, Pallas kernels, front(): pl.pallas_call(body, in_specs=[smem] * 3 + [any_space] * 13 + [vmem] * 2,...  168 us
    all_to_all x3, waiting for transfers between devices, to_positions(): return lax.all_to_all(a, 'tensor', split_axis=1, concat_axis=0, tiled=True)  27 us
    pallas_call x1, Pallas kernels, feed(): pl.pallas_call(functools.partial(feed_kernel, spd), grid=(nt, subs), in_s...  22.1 us
    pallas_call x1, Pallas kernels, cross_bwd(): pl.pallas_call(functools.partial(cross_bwd_kernel, spd), grid=(nt,), in_s...  19.9 us
    pallas_call x1, Pallas kernels, self_bwd(): pl.pallas_call(functools.partial(self_bwd_kernel, spd), grid=(nt,), in_sp...  15.7 us
    all_to_all x2, waiting for transfers between devices, swap_dp(): lax.all_to_all(route_rows(selector_out, a), 'dp', split_axis=0, concat_ax...  12.9 us
    all_to_all x3, starting transfers between devices, to_positions(): return lax.all_to_all(a, 'tensor', split_axis=1, concat_axis=0, tiled=True)  10.9 us
  transfers between devices with their start and end apart: 5, of which 4 were waited for; matrix products, arithmetic and copies ran while one was open for 4% of the time, Pallas kernels for 35%

profile of v2, /device:TPU:0, one launch (start us, length us, event | category | flops | bytes accessed | tf_op | source)
XLA Modules:
  0.0 485.7 jit_solution(12387360490336905058)
XLA Ops:
  0.6 0.0 copy-start
  0.7 0.9 select_reduce_fusion
  1.6 0.9 select_reduce_fusion.1
  2.5 0.6 dynamic_slice.6.refs_0_.lens
  3.1 0.6 dynamic_slice.7.refs_1_.lens
  3.7 0.5 and_select_fusion
  4.2 0.0 copy-done
  4.2 0.8 fusion.2
  5.0 1.6 copy.141.refs_4_
  6.6 0.0 copy-done.10
  6.6 0.5 fusion.6
  7.1 1.1 copy.142.refs_3_
  8.2 167.9 %front.1 = (bf16[4,4,1024,1024]{3,2,1,0:T(8,128)(2,1)}, bf16[2,128,1024]{2,1,0:T(8,128)(2,1)}, bf16[2,256,1024]{2,1,0:T(8,128)(2,1)}, bf16[2,128,1024]{2,1,0:T(8...) custom-call(s32[2]{0:T(128)} %dynamic_slice.6.refs_0_.lens, ...), custom_call_target="tpu_custom_call" | custom-call | tf_op jit(solution)/shard_map/front/pallas_call | solution.py:830
  176.1 22.1 %feed_forward.1 = (bf16[256,1024]{1,0:T(8,128)(2,1)}, f32[256,1024]{1,0:T(8,128)}, f32[2,1024]{1,0:T(2,128)}, bf16[4,1024,1024]{2,1,0:T(8,128)(2,1)}, bf16[4,1024,1024]{2,1,0:T(8,128)(2,1)}) custom-call(s32[2]{0:T(128)} %dynamic_slice.6.refs_0_.lens, f32[256,1024]{1,0:T(8,128)} %get-tuple-element.45.h2_ref, bf16[256,1024]{1,0:T(8,128)(2,1)} %bitcast.60, ...), custom_call_target="tpu_custom_call" | custom-call | tf_op jit(solution)/shard_map/feed_forward/pallas_call | solution.py:181
  198.1 19.9 %cross_bwd.1 = (bf16[512,1024]{1,0:T(8,128)(2,1)}, f32[256,1024]{1,0:T(8,128)}, f32[2,1024]{1,0:T(2,128)}, bf16[4,1024,1024]{2,1,0:T(8,128)(2,1)}) custom-call(s32[2]{0:T(128)} %dynamic_slice.7.refs_1_.lens, f32[256,1024]{1,0:T(8,128)} %get-tuple-element.49.dh2_ref, f32[256,1024]{1,0:T(8,128)} %get-tuple-element.50.h1_ref, ...), custom_call_target="tpu_custom_call" | custom-call | tf_op jit(solution)/shard_map/cross_bwd/pallas_call | solution.py:291
  218.0 15.7 %self_bwd.1 = (bf16[256,1024]{1,0:T(8,128)(2,1)}, f32[2,1024]{1,0:T(2,128)}, bf16[4,1024,1024]{2,1,0:T(8,128)(2,1)}) custom-call(s32[2]{0:T(128)} %dynamic_slice.6.refs_0_.lens, f32[256,1024]{1,0:T(8,128)} %get-tuple-element.57.dh1_ref, bf16[256,1024]{1,0:T(8,128)(2,1)} %bitcast.59, bf16[256,1024]{1,0:T(8,128)(2,1)} %get-tuple-element.59.n1_ref, ...), custom_call_target="tpu_custom_call" | custom-call | tf_op jit(solution)/shard_map/self_bwd/pallas_call | solution.py:394
  233.7 0.0 copy-start.8
  233.7 2.5 copy.106
  236.2 3.7 all-to-all-start.1
  239.9 0.0 copy-done.9
  239.9 1.3 copy.104
  241.2 14.3 %all-to-all-done.1 = bf16[2,128,1024]{2,0,1:T(2,128)(2,1)S(1)} async-done(((bf16[2,128,1024]{2,0,1:T(2,128)(2,1)}), bf16[2,128,1024]{2,0,1:T(2,128)(2,1)S(1)}, u32[]{:S(2)}, u32[]{:S(2)}) %all-to-all-start.1) | async-done | bytes 524320 | tf_op jit(solution)/shard_map/all_to_all | solution.py:1145
  255.5 3.5 all-to-all-start
  259.0 0.0 copy-start.15
  259.0 0.0 copy-start.14
  259.1 0.0 copy-start.13
  259.1 2.0 copy.112
  261.1 12.7 %all-to-all-done = bf16[2,128,1024]{2,0,1:T(2,128)(2,1)S(1)} async-done(((bf16[2,128,1024]{2,0,1:T(2,128)(2,1)}), bf16[2,128,1024]{2,0,1:T(2,128)(2,1)S(1)}, u32[]{:S(2)}, u32[]{:S(2)}) %all-to-all-start) | async-done | bytes 524320 | tf_op jit(solution)/shard_map/all_to_all | solution.py:1145
  273.8 0.8 copy-done.3
  274.6 3.7 all-to-all-start.3
  278.3 0.0 copy-done.14
  278.3 0.0 copy-done.13
  278.4 0.7 concatenate.3.sums_ref
  279.0 168.9 %reduce_grads.1 = (f32[4,128,1024]{2,1,0:T(8,128)}, f32[8,1024]{1,0:T(8,128)}) custom-call(bf16[4,4,2,128,1024]{4,3,2,1,0:T(8,128)(2,1)} %bitcast.51, bf16[4,4,2,128,1024]{4,3,2,1,0:T(8,128)(2,1)} %bitcast.50, bf16[4,4,2,128,1024]{4,3,2,1,0:T(8,128)(2,1)} %bitcast.48, bf16[4,4,2,128,1024]{4,3,2,1,0:T(8,128)(2,1)} %bitcast.49, f32[8,1024]{1,0:T(8,128)} %concatenate.3.sums_ref), custom_call_target="tpu_custom_call" | custom-call | tf_op jit(solution)/shard_map/reduce_grads/pallas_call | solution.py:1094
  448.0 0.0 copy-start.12
  448.0 0.1 copy.107
  448.1 0.0 copy-start.2
  448.1 0.5 copy-done.12
  448.6 0.4 convolution_convert_fusion.3
  449.0 1.1 copy.110
  450.1 0.0 all-to-all-done.3
  450.1 4.1 all-to-all-start.2
  454.3 1.4 slice_bitcast_fusion
  455.6 0.3 copy.113
  455.9 0.1 copy.114
  456.0 0.7 convolution_convert_fusion.1
  456.7 1.5 copy.116
  458.3 5.7 %all-to-all-done.2 = bf16[8,32,1024]{2,1,0:T(8,128)(2,1)} async-done(((bf16[8,32,1024]{2,1,0:T(8,128)(2,1)}), bf16[8,32,1024]{2,1,0:T(8,128)(2,1)}, u32[]{:S(2)}, u32[]{:S(2)}) %all-to-all-start.2) | async-done | bytes 524320 | tf_op jit(solution)/shard_map/all_to_all | solution.py:1138
  464.0 3.8 all-to-all-start.4
  467.8 0.0 copy-start.11
  467.8 0.0 copy-start.4
  467.8 0.8 slice_bitcast_fusion.5
  468.6 0.8 copy.120
  469.3 0.8 slice_bitcast_fusion.4
  470.1 0.8 copy.121
  470.8 1.0 copy.122
  471.8 0.6 fusion.22
  472.5 0.9 copy.105
  473.4 1.5 convolution_convert_fusion.2
  474.9 0.0 copy-start.1
  474.9 1.1 copy.118
  476.0 7.2 %all-to-all-done.4 = bf16[8,64,1024]{2,1,0:T(8,128)(2,1)S(1)} async-done(((bf16[8,64,1024]{2,1,0:T(8,128)(2,1)}), bf16[8,64,1024]{2,1,0:T(8,128)(2,1)S(1)}, u32[]{:S(2)}, u32[]{:S(2)}) %all-to-all-start.4) | async-done | bytes 1048608 | tf_op jit(solution)/shard_map/all_to_all | solution.py:1138
  483.1 0.7 convolution_convert_fusion
  483.9 1.6 copy.119
  (21 shorter events, 0.1 us)
Async XLA Ops:
  0.6 3.6 copy-start
  4.2 2.4 copy-start.10
  233.7 6.2 %copy-start.9 = (bf16[256,1024]{1,0:T(8,128)(2,1)S(1)}, bf16[256,1024]{1,0:T(8,128)(2,1)}, u32[]{:S(2)}) copy-start(bf16[256,1024]{1,0:T(8,128)(2,1)} %get-tuple-element.48) | copy-start | bytes 1572868
  233.7 25.4 %copy-start.8 = (bf16[512,1024]{1,0:T(8,128)(2,1)S(1)}, bf16[512,1024]{1,0:T(8,128)(2,1)}, u32[]{:S(2)}) copy-start(bf16[512,1024]{1,0:T(8,128)(2,1)} %get-tuple-element.65) | copy-start | bytes 3145732
  236.2 19.4 %all-to-all-start.1 = ((bf16[2,128,1024]{2,0,1:T(2,128)(2,1)}), bf16[2,128,1024]{2,0,1:T(2,128)(2,1)S(1)}, u32[]{:S(2)}, u32[]{:S(2)}) async-start(bf16[2,128,1024]{2,0,1:T(2,128)(2,1)} %copy.106), calls=%async_computation.1 | async-start | bytes 1048576 | tf_op jit(solution)/shard_map/all_to_all | solution.py:1145
  255.5 18.3 %all-to-all-start = ((bf16[2,128,1024]{2,0,1:T(2,128)(2,1)}), bf16[2,128,1024]{2,0,1:T(2,128)(2,1)S(1)}, u32[]{:S(2)}, u32[]{:S(2)}) async-start(bf16[2,128,1024]{2,0,1:T(2,128)(2,1)} %copy.104), calls=%async_computation | async-start | bytes 1048576 | tf_op jit(solution)/shard_map/all_to_all | solution.py:1145
  259.0 19.3 %copy-start.15 = (f32[2,1024]{1,0:T(2,128)S(1)}, f32[2,1024]{1,0:T(2,128)}, u32[]{:S(2)}) copy-start(f32[2,1024]{1,0:T(2,128)} %get-tuple-element.70) | copy-start | bytes 24580
  259.0 19.3 %copy-start.14 = (f32[2,1024]{1,0:T(2,128)S(1)}, f32[2,1024]{1,0:T(2,128)}, u32[]{:S(2)}) copy-start(f32[2,1024]{1,0:T(2,128)} %get-tuple-element.71) | copy-start | bytes 24580
  259.1 19.3 %copy-start.13 = (f32[2,1024]{1,0:T(2,128)S(1)}, f32[2,1024]{1,0:T(2,128)}, u32[]{:S(2)}) copy-start(f32[2,1024]{1,0:T(2,128)} %get-tuple-element.72) | copy-start | bytes 24580
  273.8 0.8 copy-start.3
  274.6 175.5 %all-to-all-start.3 = ((bf16[2,256,1024]{2,0,1:T(2,128)(2,1)}), bf16[2,256,1024]{2,0,1:T(2,128)(2,1)S(1)}, u32[]{:S(2)}, u32[]{:S(2)}) async-start(bf16[2,256,1024]{2,0,1:T(2,128)(2,1)} %copy.112), calls=%async_computation.3 | async-start | bytes 2097152 | tf_op jit(solution)/shard_map/all_to_all | solution.py:1145
  448.0 0.7 copy-start.12
  448.1 6.2 %copy-start.2 = (f32[4,128,1024]{2,1,0:T(8,128)S(1)}, f32[4,128,1024]{2,1,0:T(8,128)}, u32[]{:S(2)}) copy-start(f32[4,128,1024]{2,1,0:T(8,128)} %get-tuple-element.73) | copy-start | bytes 6291460
  450.1 13.9 %all-to-all-start.2 = ((bf16[8,32,1024]{2,1,0:T(8,128)(2,1)}), bf16[8,32,1024]{2,1,0:T(8,128)(2,1)}, u32[]{:S(2)}, u32[]{:S(2)}) async-start(bf16[8,32,1024]{2,1,0:T(8,128)(2,1)} %copy.110), calls=%async_computation.2 | async-start | bytes 1048576 | tf_op jit(solution)/shard_map/all_to_all | solution.py:1138
  456.7 11.1 %copy-start.7 = (f32[128,1024]{1,0:T(8,128)S(1)}, f32[128,1024]{1,0:T(8,128)}, u32[]{:S(2)}) copy-start(f32[128,1024]{1,0:T(8,128)} %get-tuple-element.157) | copy-start | bytes 1572868
  458.3 11.1 %copy-start.6 = (f32[128,1024]{1,0:T(8,128)S(1)}, f32[128,1024]{1,0:T(8,128)}, u32[]{:S(2)}) copy-start(f32[128,1024]{1,0:T(8,128)} %get-tuple-element.156) | copy-start | bytes 1572868
  458.3 12.6 %copy-start.5 = (f32[1024,128]{0,1:T(8,128)S(1)}, f32[1024,128]{0,1:T(8,128)}, u32[]{:S(2)}) copy-start(f32[1024,128]{0,1:T(8,128)} %get-tuple-element.154) | copy-start | bytes 1572868
  464.0 19.1 %all-to-all-start.4 = ((bf16[8,64,1024]{2,1,0:T(8,128)(2,1)}), bf16[8,64,1024]{2,1,0:T(8,128)(2,1)S(1)}, u32[]{:S(2)}, u32[]{:S(2)}) async-start(bf16[8,64,1024]{2,1,0:T(8,128)(2,1)} %copy.116), calls=%async_computation.4 | async-start | bytes 2097152 | tf_op jit(solution)/shard_map/all_to_all | solution.py:1138
  467.8 4.0 copy-start.11
  467.8 4.7 copy-start.4
  474.9 10.6 %copy-start.1 = (bf16[8,64,1024]{2,1,0:T(8,128)(2,1)S(1)}, bf16[8,64,1024]{2,1,0:T(8,128)(2,1)}, u32[]{:S(2)}) copy-start(bf16[8,64,1024]{2,1,0:T(8,128)(2,1)} %param.19) | copy-start | bytes 3145732

commit v3 on v2

--- a/solution.py
+++ b/solution.py
@@ -87,19 +87,6 @@
     return dq, dk, dv
 
 
-def params(steps):
-    return pltpu.CompilerParams(
-        dimension_semantics=("arbitrary",) * steps, vmem_limit_bytes=VMEM_LIMIT
-    )
-
-
-def whole(shape):
-    return pl.BlockSpec(shape, lambda *_: (0,) * len(shape))
-
-
-SMEM = pl.BlockSpec(memory_space=pltpu.SMEM)
-
-
 def row_valid(lens, spd, n):
     row = lax.broadcasted_iota(jnp.int32, (n, 1), 0)
     seq = n // spd
@@ -107,325 +94,6 @@
     for i in range(1, spd):
         end = jnp.where(row >= i * seq, i * seq + lens[i], end)
     return row < end
-
-
-def feed_kernel(
-    spd,
-    lens,
-    h2_ref,
-    cot_ref,
-    gain,
-    bias,
-    win_ref,
-    wout_ref,
-    res_ref,
-    dh_ref,
-    sums_ref,
-    dw_in_ref,
-    dw_out_ref,
-    n3,
-    n3t,
-    g3,
-    g3t,
-    out_acc,
-    dn_acc,
-):
-    step = pl.program_id(0) * pl.num_programs(1) + pl.program_id(1)
-    last = pl.num_programs(0) * pl.num_programs(1) - 1
-    n = h2_ref.shape[0]
-
-    @pl.when(step == 0)
-    def _():
-        nh, _ = norm_parts(h2_ref[...])
-        low = nh * gain[2:3] + bias[2:3]
-        n3[...] = low.astype(BF16)
-        n3t[...] = low.T.astype(BF16)
-        keep = row_valid(lens, spd, n)
-        dh = jnp.where(keep, cot_ref[...].astype(F32), 0.0)
-        g3[...] = dh.astype(BF16)
-        g3t[...] = dh.T.astype(BF16)
-        out_acc[...] = jnp.zeros_like(out_acc)
-        dn_acc[...] = jnp.zeros_like(dn_acc)
-
-    win = win_ref[0, 0]
-    wout = wout_ref[0, 0]
-    u = dot_nn(n3[...], win)
-    ga = dot_nn(g3[...], wout)
-    sg = 1.0 / (1.0 + jnp.exp(-u))
-    r = (u * sg).astype(BF16)
-    du = (ga * (sg * (1.0 + u * (1.0 - sg)))).astype(BF16)
-    out_acc[...] += dot_nt(r, wout)
-    dn_acc[...] += dot_nt(du, win)
-    dw_in_ref[0] = dot_nn(n3t[...], du).astype(BF16)
-    dw_out_ref[0] = dot_nn(g3t[...], r).astype(BF16)
-
-    @pl.when(step == last)
-    def _():
-        keep = row_valid(lens, spd, n)
-        h2 = h2_ref[...]
-        res_ref[...] = jnp.where(keep, h2 + out_acc[...], 0.0).astype(BF16)
-        dh = jnp.where(keep, cot_ref[...].astype(F32), 0.0)
-        nh, rstd = norm_parts(h2)
-        dn = dn_acc[...]
-        dh_ref[...] = dh + norm_back(dn, nh, rstd, gain[2:3])
-        sums_ref[0:1] = jnp.sum(dn * nh, axis=0, keepdims=True)
-        sums_ref[1:2] = jnp.sum(dn, axis=0, keepdims=True)
-
-
-def feed(lens, h2, cot, gain, bias, wg, spd, nt):
-    n, dim = h2.shape
-    fc = wg.shape[3]
-    block = min(512, fc)
-    subs = fc // block
-    dw = pl.BlockSpec((1, dim, block), lambda j, i: (j, 0, i))
-    return pl.pallas_call(
-        functools.partial(feed_kernel, spd),
-        grid=(nt, subs),
-        in_specs=[
-            SMEM,
-            whole((n, dim)),
-            whole((n, dim)),
-            whole(gain.shape),
-            whole(bias.shape),
-            pl.BlockSpec((1, 1, dim, block), lambda j, i: (j, 2, 0, i)),
-            pl.BlockSpec((1, 1, dim, block), lambda j, i: (j, 3, 0, i)),
-        ],
-        out_specs=[whole((n, dim)), whole((n, dim)), whole((2, dim)), dw, dw],
-        out_shape=[
-            jax.ShapeDtypeStruct((n, dim), BF16),
-            jax.ShapeDtypeStruct((n, dim), F32),
-            jax.ShapeDtypeStruct((2, dim), F32),
-            jax.ShapeDtypeStruct((nt, dim, fc), BF16),
-            jax.ShapeDtypeStruct((nt, dim, fc), BF16),
-        ],
-        scratch_shapes=[
-            pltpu.VMEM((n, dim), BF16),
-            pltpu.VMEM((dim, n), BF16),
-            pltpu.VMEM((n, dim), BF16),
-            pltpu.VMEM((dim, n), BF16),
-            pltpu.VMEM((n, dim), F32),
-            pltpu.VMEM((n, dim), F32),
-        ],
-        compiler_params=params(2),
-        name="feed_forward",
-    )(lens, h2, cot, gain, bias, wg, wg)
-
-
-def cross_bwd_kernel(
-    spd,
-    lens,
-    dh2_ref,
-    h1_ref,
-    n2_ref,
-    ed_ref,
-    gain,
-    q_ref,
-    k_ref,
-    v_ref,
-    o_ref,
-    w_ref,
-    ded_ref,
-    dh1_ref,
-    sums_ref,
-    dw_ref,
-    g2,
-    g2t,
-    n2t,
-    edt,
-    dn_acc,
-    ded_acc,
-    dq,
-    dk,
-    dv,
-):
-    j = pl.program_id(0)
-    n = h1_ref.shape[0]
-    seq = n // spd
-    enc = ed_ref.shape[0] // spd
-    hc = q_ref.shape[2]
-
-    @pl.when(j == 0)
-    def _():
-        dh = dh2_ref[...]
-        g2[...] = dh.astype(BF16)
-        g2t[...] = dh.T.astype(BF16)
-        n2t[...] = n2_ref[...].T
-        edt[...] = ed_ref[...].T
-        dn_acc[...] = jnp.zeros_like(dn_acc)
-        ded_acc[...] = jnp.zeros_like(ded_acc)
-
-    w = w_ref.at[0, 0]
-    do = dot_nn(g2[...], w[:, 3 * hc :]).astype(BF16)
-    for i in range(spd):
-        rows = slice(i * seq, (i + 1) * seq)
-        keys = slice(i * enc, (i + 1) * enc)
-        a, b, c = attn_bwd(
-            q_ref[0, rows], k_ref[0, keys], v_ref[0, keys], do[rows], lens[i], False
-        )
-        dq[rows] = a
-        dk[keys] = b
-        dv[keys] = c
-    dn_acc[...] += dot_nt(dq[...], w[:, :hc])
-    ded_acc[...] += dot_nt(dk[...], w[:, hc : 2 * hc]) + dot_nt(dv[...], w[:, 2 * hc : 3 * hc])
-    dw_ref[0, :, :hc] = dot_nn(n2t[...], dq[...]).astype(BF16)
-    dw_ref[0, :, hc : 2 * hc] = dot_nn(edt[...], dk[...]).astype(BF16)
-    dw_ref[0, :, 2 * hc : 3 * hc] = dot_nn(edt[...], dv[...]).astype(BF16)
-    dw_ref[0, :, 3 * hc :] = dot_nn(g2t[...], o_ref[0]).astype(BF16)
-
-    @pl.when(j == pl.num_programs(0) - 1)
-    def _():
-        ded_ref[...] = ded_acc[...].astype(BF16)
-        nh, rstd = norm_parts(h1_ref[...])
-        dn = dn_acc[...]
-        dh1_ref[...] = dh2_ref[...] + norm_back(dn, nh, rstd, gain[1:2])
-        sums_ref[0:1] = jnp.sum(dn * nh, axis=0, keepdims=True)
-        sums_ref[1:2] = jnp.sum(dn, axis=0, keepdims=True)
-
-
-def cross_bwd(lens, dh2, h1, n2, ed, gain, q, k, v, o, wg, spd, nt):
-    n, dim = h1.shape
-    m = ed.shape[0]
-    hc = wg.shape[3] // 4
-    part = pl.BlockSpec((1, n, hc), lambda j: (j, 0, 0))
-    keys = pl.BlockSpec((1, m, hc), lambda j: (j, 0, 0))
-    return pl.pallas_call(
-        functools.partial(cross_bwd_kernel, spd),
-        grid=(nt,),
-        in_specs=[
-            SMEM,
-            whole((n, dim)),
-            whole((n, dim)),
-            whole((n, dim)),
-            whole((m, dim)),
-            whole(gain.shape),
-            part,
-            keys,
-            keys,
-            part,
-            pl.BlockSpec((1, 1, dim, 4 * hc), lambda j: (j, 1, 0, 0)),
-        ],
-        out_specs=[
-            whole((m, dim)),
-            whole((n, dim)),
-            whole((2, dim)),
-            pl.BlockSpec((1, dim, 4 * hc), lambda j: (j, 0, 0)),
-        ],
-        out_shape=[
-            jax.ShapeDtypeStruct((m, dim), BF16),
-            jax.ShapeDtypeStruct((n, dim), F32),
-            jax.ShapeDtypeStruct((2, dim), F32),
-            jax.ShapeDtypeStruct((nt, dim, 4 * hc), BF16),
-        ],
-        scratch_shapes=[
-            pltpu.VMEM((n, dim), BF16),
-            pltpu.VMEM((dim, n), BF16),
-            pltpu.VMEM((dim, n), BF16),
-            pltpu.VMEM((dim, m), BF16),
-            pltpu.VMEM((n, dim), F32),
-            pltpu.VMEM((m, dim), F32),
-            pltpu.VMEM((n, hc), BF16),
-            pltpu.VMEM((m, hc), BF16),
-            pltpu.VMEM((m, hc), BF16),
-        ],
-        compiler_params=params(1),
-        name="cross_bwd",
-    )(lens, dh2, h1, n2, ed, gain, q, k, v, o, wg)
-
-
-def self_bwd_kernel(
-    spd,
-    lens,
-    dh1_ref,
-    x_ref,
-    n1_ref,
-    gain,
-    q_ref,
-    k_ref,
-    v_ref,
-    o_ref,
-    w_ref,
-    dx_ref,
-    sums_ref,
-    dw_ref,
-    g1,
-    g1t,
-    n1t,
-    dn_acc,
-    dqkv,
-):
-    j = pl.program_id(0)
-    n = x_ref.shape[0]
-    seq = n // spd
-    hc = q_ref.shape[2]
-
-    @pl.when(j == 0)
-    def _():
-        dh = dh1_ref[...]
-        g1[...] = dh.astype(BF16)
-        g1t[...] = dh.T.astype(BF16)
-        n1t[...] = n1_ref[...].T
-        dn_acc[...] = jnp.zeros_like(dn_acc)
-
-    w = w_ref.at[0, 0]
-    do = dot_nn(g1[...], w[:, 3 * hc :]).astype(BF16)
-    for i in range(spd):
-        rows = slice(i * seq, (i + 1) * seq)
-        a, b, c = attn_bwd(q_ref[0, rows], k_ref[0, rows], v_ref[0, rows], do[rows], lens[i], True)
-        dqkv[rows, :hc] = a
-        dqkv[rows, hc : 2 * hc] = b
-        dqkv[rows, 2 * hc :] = c
-    dn_acc[...] += dot_nt(dqkv[...], w[:, : 3 * hc])
-    dw_ref[0, :, : 3 * hc] = dot_nn(n1t[...], dqkv[...]).astype(BF16)
-    dw_ref[0, :, 3 * hc :] = dot_nn(g1t[...], o_ref[0]).astype(BF16)
-
-    @pl.when(j == pl.num_programs(0) - 1)
-    def _():
-        nh, rstd = norm_parts(x_ref[...].astype(F32))
-        dn = dn_acc[...]
-        dx_ref[...] = (dh1_ref[...] + norm_back(dn, nh, rstd, gain[0:1])).astype(BF16)
-        sums_ref[0:1] = jnp.sum(dn * nh, axis=0, keepdims=True)
-        sums_ref[1:2] = jnp.sum(dn, axis=0, keepdims=True)
-
-
-def self_bwd(lens, dh1, x, n1, gain, q, k, v, o, wg, spd, nt):
-    n, dim = x.shape
-    hc = wg.shape[3] // 4
-    part = pl.BlockSpec((1, n, hc), lambda j: (j, 0, 0))
-    return pl.pallas_call(
-        functools.partial(self_bwd_kernel, spd),
-        grid=(nt,),
-        in_specs=[
-            SMEM,
-            whole((n, dim)),
-            whole((n, dim)),
-            whole((n, dim)),
-            whole(gain.shape),
-            part,
-            part,
-            part,
-            part,
-            pl.BlockSpec((1, 1, dim, 4 * hc), lambda j: (j, 0, 0, 0)),
-        ],
-        out_specs=[
-            whole((n, dim)),
-            whole((2, dim)),
-            pl.BlockSpec((1, dim, 4 * hc), lambda j: (j, 0, 0)),
-        ],
-        out_shape=[
-            jax.ShapeDtypeStruct((n, dim), BF16),
-            jax.ShapeDtypeStruct((2, dim), F32),
-            jax.ShapeDtypeStruct((nt, dim, 4 * hc), BF16),
-        ],
-        scratch_shapes=[
-            pltpu.VMEM((n, dim), BF16),
-            pltpu.VMEM((dim, n), BF16),
-            pltpu.VMEM((dim, n), BF16),
-            pltpu.VMEM((n, dim), F32),
-            pltpu.VMEM((n, 3 * hc), BF16),
-        ],
-        compiler_params=params(1),
-        name="self_bwd",
-    )(lens, dh1, x, n1, gain, q, k, v, o, wg)
 
 
 def flip(index, mask):
@@ -883,44 +551,126 @@
     )(tok_lens, enc_lens, in_peer, tok_blocks, enc_blocks, cot, *weights, gain, bias)
 
 
-def reduce_kernel(
+CORE_SLOTS = 4
+CHIP_SLOTS = 4
+DW_SLOTS = 3
+Z_SLOTS = 4
+SPACING = 2
+
+
+def back_kernel(
     ndp,
     nt,
-    dws_ref,
-    dwc_ref,
-    dwi_ref,
-    dwo_ref,
-    sums_ref,
-    out_ref,
+    spd,
+    tok_lens,
+    enc_lens,
+    back_slot,
+    wg,
+    x_hbm,
+    ed_hbm,
+    cot_hbm,
+    n1_hbm,
+    q1_hbm,
+    k1_hbm,
+    v1_hbm,
+    o1_hbm,
+    h1_hbm,
+    n2_hbm,
+    q2_hbm,
+    k2_hbm,
+    v2_hbm,
+    o2_hbm,
+    h2_hbm,
+    gain,
+    res_out,
+    rx_tok,
+    rx_enc,
+    grad_ref,
     norm_ref,
+    h2_ref,
+    cot_ref,
+    h1_ref,
+    n2_ref,
+    ed_ref,
+    q2_ref,
+    k2_ref,
+    v2_ref,
+    o2_ref,
+    x_ref,
+    n1_ref,
+    q1_ref,
+    k1_ref,
+    v1_ref,
+    o1_ref,
+    low,
+    low_t,
+    grad_low,
+    grad_low_t,
+    edt,
+    out_acc,
+    dn_acc,
+    ded_acc,
+    dh_ref,
+    res_ref,
+    dx_ref,
+    ded_ref,
+    dq,
+    dk,
+    dv,
+    panels,
+    zrx_tok,
+    zrx_enc,
+    sb_tok,
+    sb_enc,
+    dw,
     got_core,
     got_chip,
     got_z,
-    got_sum,
-    mine,
     work,
     final,
     total,
+    got_sum,
     load_sems,
+    panel_sems,
     send_sems,
     recv_sems,
     z_send,
     z_recv,
     sum_send,
     sum_recv,
+    zr_send,
+    zr_recv,
+    zt_send,
+    zt_recv,
+    ze_send,
+    ze_recv,
+    tok_send,
+    tok_recv,
+    enc_send,
+    enc_recv,
+    core_credit,
+    chip_credit,
 ):
     d = lax.axis_index("dp")
     t = lax.axis_index("tensor")
     bits = ndp.bit_length() - 1
     tbits = nt.bit_length() - 1
     chips = ndp // 2
-    rows, width = out_ref.shape[1], out_ref.shape[2]
-    half = rows // 2
+    rows_each, width = grad_ref.shape[1], grad_ref.shape[2]
+    dim = wg.shape[2]
+    hc = width // 4
+    half = rows_each // 2
     core = lax.rem(d, 2)
     chip = lax.div(d, 2)
     chip_bits = [1 << b for b in range(bits - 1)]
     orders = (chip_bits, chip_bits[::-1])
     levels = len(chip_bits)
+    work_slots = work.shape[0]
+    seqs, lr = res_out.shape[0], res_out.shape[1]
+    le = rx_enc.shape[1]
+    seq, enc = nt * lr, nt * le
+    n, m = spd * seq, spd * enc
+    started = []
 
     def dp_peer(bit):
         return (flip(d, bit), t)
@@ -928,15 +678,8 @@
     def t_peer(j):
         return (d, flip(t, j))
 
-    greet([dp_peer(1 << b) for b in range(bits)] + [t_peer(j) for j in range(1, nt)])
-
-    sources = [dwo_ref, dwi_ref, dwc_ref, dws_ref]
-    target = [3, 2, 1, 0]
-    chunks = [(s, j) for s in range(4) for j in list(range(1, nt)) + [0]]
-    started = []
-
-    def send(src, dst, ssem, rsem, peer):
-        copy = pltpu.make_async_remote_copy(
+    def remote(src, dst, ssem, rsem, peer):
+        return pltpu.make_async_remote_copy(
             src_ref=src,
             dst_ref=dst,
             send_sem=ssem,
@@ -944,106 +687,359 @@
             device_id=peer,
             device_id_type=MESH,
         )
+
+    def send(*args):
+        copy = remote(*args)
         copy.start()
         started.append(copy)
         return copy
 
-    state = {}
-
-    def core_send(c):
-        s, j = chunks[c]
-        src = sources[s].at[j, :, 1 - core]
-        return send(src, got_core.at[c], send_sems.at[c, 0], recv_sems.at[c, 0], dp_peer(1))
-
-    def core_load(c):
-        s, j = chunks[c]
-        copy = pltpu.make_async_copy(
-            sources[s].at[j, :, core], mine.at[c % 2], load_sems.at[c % 2]
-        )
+    def sent(copy):
+        copy.wait_send()
+        started[:] = [one for one in started if one is not copy]
+
+    def local(src, dst, sem):
+        copy = pltpu.make_async_copy(src, dst, sem)
         copy.start()
         return copy
 
+    loads = [
+        local(src, dst, load_sems.at[i])
+        for i, (src, dst) in enumerate(
+            [
+                (h2_hbm, h2_ref),
+                (cot_hbm, cot_ref),
+                (n2_hbm, n2_ref),
+                (ed_hbm, ed_ref),
+                (q2_hbm, q2_ref),
+                (k2_hbm, k2_ref),
+                (v2_hbm, v2_ref),
+                (o2_hbm, o2_ref),
+                (h1_hbm, h1_ref),
+                (n1_hbm, n1_ref),
+                (q1_hbm, q1_ref),
+                (k1_hbm, k1_ref),
+                (v1_hbm, v1_ref),
+                (o1_hbm, o1_ref),
+                (x_hbm, x_ref),
+            ]
+        )
+    ]
+
+    def loaded(first, last):
+        for i in range(first, last):
+            loads[i].wait()
+
+    shards = list(range(1, nt)) + [0]
+    units = [("feed", j) for j in shards] + [("cross", j) for j in shards]
+    units += [("self", j) for j in shards]
+    made = {"feed": (3, 2), "cross": (1,), "self": (0,)}
+    chunks = []
+    unit_at = {}
+    for u, (kind, j) in enumerate(units):
+        unit_at[len(chunks)] = u
+        chunks += [(g, j) for g in made[kind]]
+    count = len(chunks)
+    fetched = {}
+
+    def fetch(u):
+        if u < len(units):
+            kind, j = units[u]
+            fetched[u] = [
+                local(wg.at[j, g], panels.at[2 * (u % 2) + i], panel_sems.at[2 * (u % 2) + i])
+                for i, g in enumerate(made[kind])
+            ]
+
+    fetch(0)
+    greet([dp_peer(e) for e in range(1, ndp)] + [t_peer(j) for j in range(1, nt)])
+
+    def put(c, column, a, b):
+        cols = b.shape[1]
+        for e in range(chips):
+            part = dot_nn(a[2 * e * rows_each : 2 * (e + 1) * rows_each], b)
+            dw[c % DW_SLOTS, e, :, :, column : column + cols] = part.astype(BF16).reshape(
+                2, rows_each, cols
+            )
+
+    def feed_init():
+        loaded(0, 2)
+        nh, _ = norm_parts(h2_ref[...])
+        v = nh * gain[2:3] + gain[5:6]
+        low[...] = v.astype(BF16)
+        low_t[...] = v.T.astype(BF16)
+        keep = row_valid(tok_lens, spd, n)
+        dh = jnp.where(keep, cot_ref[...].reshape(n, dim).astype(F32), 0.0)
+        grad_low[...] = dh.astype(BF16)
+        grad_low_t[...] = dh.T.astype(BF16)
+        out_acc[...] = jnp.zeros_like(out_acc)
+        dn_acc[...] = jnp.zeros_like(dn_acc)
+
+    def feed_part(c, wout_ref, win_ref):
+        block = min(512, width)
+        for at in range(0, width, block):
+            win = win_ref[:, at : at + block]
+            wout = wout_ref[:, at : at + block]
+            u = dot_nn(low[...], win)
+            ga = dot_nn(grad_low[...], wout)
+            sg = 1.0 / (1.0 + jnp.exp(-u))
+            r = (u * sg).astype(BF16)
+            du = (ga * (sg * (1.0 + u * (1.0 - sg)))).astype(BF16)
+            out_acc[...] += dot_nt(r, wout)
+            dn_acc[...] += dot_nt(du, win)
+            put(c, at, grad_low_t, r)
+            put(c + 1, at, low_t, du)
+
+    def norm_grads(row, v, gain_row):
+        nh, rstd = norm_parts(v)
+        dn = dn_acc[...]
+        total[0, row : row + 1] = jnp.sum(dn * nh, axis=0, keepdims=True)
+        total[0, 3 + row : 4 + row] = jnp.sum(dn, axis=0, keepdims=True)
+        return norm_back(dn, nh, rstd, gain_row)
+
+    def feed_end():
+        keep = row_valid(tok_lens, spd, n)
+        h2 = h2_ref[...]
+        res = jnp.where(keep, h2 + out_acc[...], 0.0).astype(BF16)
+        res_ref[...] = res.reshape(spd, seq, dim)
+        dh = jnp.where(keep, cot_ref[...].reshape(n, dim).astype(F32), 0.0)
+        dh_ref[...] = dh + norm_grads(2, h2, gain[2:3])
+
+    def branch_init(kept):
+        dh = dh_ref[...]
+        grad_low[...] = dh.astype(BF16)
+        grad_low_t[...] = dh.T.astype(BF16)
+        low_t[...] = kept[...].T
+        dn_acc[...] = jnp.zeros_like(dn_acc)
+
+    def cross_init():
+        loaded(2, 9)
+        branch_init(n2_ref)
+        edt[...] = ed_ref[...].reshape(m, dim).T
+        ded_acc[...] = jnp.zeros_like(ded_acc)
+
+    def cross_part(c, j, w):
+        do = dot_nn(grad_low[...], w[:, 3 * hc :]).astype(BF16)
+        for i in range(spd):
+            rows = slice(i * seq, (i + 1) * seq)
+            keys = slice(i * enc, (i + 1) * enc)
+            dq[rows, :hc], dk[keys], dv[keys] = attn_bwd(
+                q2_ref[j, rows], k2_ref[j, keys], v2_ref[j, keys], do[rows], enc_lens[i], False
+            )
+        dn_acc[...] += dot_nt(dq[:, :hc], w[:, :hc])
+        ded_acc[...] += dot_nt(dk[...], w[:, hc : 2 * hc]) + dot_nt(dv[...], w[:, 2 * hc : 3 * hc])
+        put(c, 0, low_t, dq[:, :hc])
+        put(c, hc, edt, dk[...])
+        put(c, 2 * hc, edt, dv[...])
+        put(c, 3 * hc, grad_low_t, o2_ref[j])
+
+    def cross_end():
+        ded_ref[...] = ded_acc[...].astype(BF16).reshape(spd, enc, dim)
+        dh_ref[...] += norm_grads(1, h1_ref[...], gain[1:2])
+
+    def self_init():
+        loaded(9, 15)
+        branch_init(n1_ref)
+
+    def self_part(c, j, w):
+        do = dot_nn(grad_low[...], w[:, 3 * hc :]).astype(BF16)
+        for i in range(spd):
+            rows = slice(i * seq, (i + 1) * seq)
+            dq[rows, :hc], dq[rows, hc : 2 * hc], dq[rows, 2 * hc :] = attn_bwd(
+                q1_ref[j, rows], k1_ref[j, rows], v1_ref[j, rows], do[rows], tok_lens[i], True
+            )
+        dn_acc[...] += dot_nt(dq[...], w[:, : 3 * hc])
+        put(c, 0, low_t, dq[...])
+        put(c, 3 * hc, grad_low_t, o1_ref[j])
+
+    def self_end():
+        x = x_ref[...].reshape(n, dim).astype(F32)
+        dx = dh_ref[...] + norm_grads(0, x, gain[0:1])
+        dx_ref[...] = dx.astype(BF16).reshape(spd, seq, dim)
+
+    def run_unit(c):
+        u = unit_at[c]
+        kind, j = units[u]
+        for i in range(len(made[kind])):
+            if c + i >= DW_SLOTS:
+                sent(core_copies[c + i - DW_SLOTS])
+        for copy in fetched.pop(u):
+            copy.wait()
+        fetch(u + 1)
+        slot = 2 * (u % 2)
+        first, last = j == shards[0], j == shards[-1]
+        if kind == "feed":
+            if first:
+                feed_init()
+            feed_part(c, panels.at[slot], panels.at[slot + 1])
+            if last:
+                feed_end()
+        elif kind == "cross":
+            if first:
+                cross_init()
+            cross_part(c, j, panels.at[slot])
+            if last:
+                cross_end()
+        else:
+            if first:
+                self_init()
+            self_part(c, j, panels.at[slot])
+            if last:
+                self_end()
+
+    core_copies = {}
+    chip_copies = {}
+    z_copies = {}
+
+    def core_send(c):
+        if c >= CORE_SLOTS:
+            pl.semaphore_wait(core_credit, 1)
+        core_copies[c] = send(
+            dw.at[c % DW_SLOTS, :, 1 - core],
+            got_core.at[c % CORE_SLOTS],
+            send_sems.at[c, 0],
+            recv_sems.at[c, 0],
+            dp_peer(1),
+        )
+
     def core_add(c):
         core_copies[c].wait_recv()
-        load_copies[c].wait()
-        slot = c % levels
-        if c >= levels:
-            for copy in state.pop(("busy", c - levels)):
-                copy.wait_send()
-                started[:] = [one for one in started if one is not copy]
+        if c >= work_slots:
+            for level in range(levels):
+                for copy in chip_copies.pop((c - work_slots, level)):
+                    sent(copy)
 
         def body(e, carry):
-            a = mine[c % 2, e].astype(F32) + got_core[c, e].astype(F32)
-            work[slot, e] = a.astype(BF16)
+            a = dw[c % DW_SLOTS, e, core] + got_core[c % CORE_SLOTS, e]
+            work[c % work_slots, e] = a
             return carry
 
         lax.fori_loop(0, chips, body, 0)
-        if c + 2 < len(chunks):
-            load_copies[c + 2] = core_load(c + 2)
-        state[("busy", c)] = []
-        chip_step(c, 0)
-
-    def chip_step(c, level):
-        slot = 1 + 2 * ((chips - (chips >> level)))
+        if c + CORE_SLOTS < count:
+            pl.semaphore_signal(core_credit, inc=1, device_id=dp_peer(1), device_id_type=MESH)
+        chip_send(c, 0)
+
+    def rest_of(order, level):
+        rest = [0]
+        for bit in order[level + 1 :]:
+            rest += [e ^ bit for e in rest]
+        return rest
+
+    def chip_send(c, level):
         base = 2 * (chips - (chips >> level))
         copies = []
         for side, order in enumerate(orders):
-            rest = [0]
-            for bit in order[level + 1 :]:
-                rest += [e ^ bit for e in rest]
-            for e in rest:
-                far = flip(chip, order[level] ^ e)
+            if c >= CHIP_SLOTS:
+                pl.semaphore_wait(chip_credit.at[level, side], 1)
+            for e in rest_of(order, level):
+                at = base + len(copies)
                 copies.append(
                     send(
-                        work.at[c % levels, far, pl.ds(side * half, half)],
-                        got_chip.at[c, base + len(copies)],
-                        send_sems.at[c, slot + len(copies)],
-                        recv_sems.at[c, slot + len(copies)],
+                        work.at[
+                            c % work_slots,
+                            flip(chip, order[level] ^ e),
+                            pl.ds(side * half, half),
+                        ],
+                        got_chip.at[c % CHIP_SLOTS, at],
+                        send_sems.at[c, 1 + at],
+                        recv_sems.at[c, 1 + at],
                         dp_peer(2 * order[level]),
                     )
                 )
-        state[("busy", c)] += copies
-        state[(c, level)] = copies
+        chip_copies[(c, level)] = copies
 
     def chip_add(c, level):
-        base = 2 * (chips - (chips >> level))
-        at = 0
-        for copy in state[(c, level)]:
+        at = 2 * (chips - (chips >> level))
+        g, j = chunks[c]
+        copies = iter(chip_copies[(c, level)])
+        last = level == levels - 1
+        if last and j:
+            zs = (c - c // len(shards)) % Z_SLOTS
+            key = [k for k, v in z_copies.items() if v[1] == zs and not v[2]]
+            for k in key:
+                sent(z_copies[k][0])
+                z_copies[k] = (z_copies[k][0], zs, True)
+        for side, order in enumerate(orders):
+            span = pl.ds(side * half, half)
+            for e in rest_of(order, level):
+                next(copies).wait_recv()
+                near = flip(chip, e)
+                a = work[c % work_slots, near, span]
+                b = got_chip[c % CHIP_SLOTS, at]
+                at += 1
+                if not last:
+                    work[c % work_slots, near, span] = a + b
+                elif j:
+                    final[zs, span] = a + b
+                else:
+                    grad_ref[g, span] = a.astype(F32) + b.astype(F32)
+            if c + CHIP_SLOTS < count:
+                pl.semaphore_signal(
+                    chip_credit.at[level, side],
+                    inc=1,
+                    device_id=dp_peer(2 * order[level]),
+                    device_id_type=MESH,
+                )
+        if not last:
+            chip_send(c, level + 1)
+        elif j:
+            copy = send(
+                final.at[zs],
+                got_z.at[g, j - 1],
+                z_send.at[g, j - 1],
+                z_recv.at[g, j - 1],
+                t_peer(j),
+            )
+            z_copies[(g, j)] = (copy, zs, False)
+
+    def finish(c):
+        g, j = chunks[c]
+        if j == 0:
+            a = grad_ref[g]
+            for i in range(1, nt):
+                z_copies[(g, i)][0].wait_recv()
+                a = a + got_z[g, i - 1].astype(F32)
+            grad_ref[g] = a
+
+    def to_positions(src, dst, rows, ssem, rsem):
+        for j in range(1, nt):
+            there = flip(t, j)
+            send(
+                src.at[:, pl.ds(pl.multiple_of(there * rows, rows), rows)],
+                dst.at[pl.ds(t * spd, spd)],
+                ssem.at[j],
+                rsem.at[j],
+                t_peer(j),
+            )
+        return local(
+            src.at[:, pl.ds(pl.multiple_of(t * rows, rows), rows)],
+            dst.at[pl.ds(t * spd, spd)],
+            rsem.at[0],
+        )
+
+    def positions_here(own_copy, src, dst, rows, ssem, rsem):
+        own_copy.wait()
+        for j in range(1, nt):
+            remote(
+                src.at[:, pl.ds(pl.multiple_of(t * rows, rows), rows)],
+                dst.at[pl.ds(flip(t, j) * spd, spd)],
+                ssem.at[j],
+                rsem.at[j],
+                t_peer(j),
+            ).wait_recv()
+
+    def to_inputs(zrx, sb, rx, ssem, rsem):
+        for k in range(ndp):
+            sb[k] = zrx[back_slot[k]]
+        copies = [
+            send(sb.at[flip(d, e)], rx.at[d], ssem.at[e], rsem.at[e], dp_peer(e))
+            for e in range(1, ndp)
+        ]
+        return copies + [local(sb.at[d], rx.at[d], rsem.at[0])]
+
+    def inputs_here(copies):
+        for copy in copies[:-1]:
             copy.wait_recv()
-        last = level == len(chip_bits) - 1
-        s, j = chunks[c]
-        for side, order in enumerate(orders):
-            rest = [0]
-            for bit in order[level + 1 :]:
-                rest += [e ^ bit for e in rest]
-            span = pl.ds(side * half, half)
-            for e in rest:
-                near = flip(chip, e)
-                a = work[c % levels, near, span].astype(F32) + got_chip[c, base + at].astype(F32)
-                at += 1
-                if last:
-                    final[c, span] = a.astype(BF16)
-                else:
-                    work[c % levels, near, span] = a.astype(BF16)
-        if last:
-            if j:
-                state[("z", s, j)] = send(
-                    final.at[c],
-                    got_z.at[s, j - 1],
-                    z_send.at[s, j - 1],
-                    z_recv.at[s, j - 1],
-                    t_peer(j),
-                )
-        else:
-            chip_step(c, level + 1)
-
-    def finish(s):
-        c = chunks.index((s, 0))
-        a = final[c].astype(F32)
-        for j in range(1, nt):
-            state[("z", s, j)].wait_recv()
-            a = a + got_z[s, j - 1].astype(F32)
-        out_ref[target[s]] = a
+        copies[-1].wait()
 
     sum_peers = [dp_peer(1 << b) for b in range(bits)] + [t_peer(1 << b) for b in range(tbits)]
     sum_copies = {}
@@ -1057,70 +1053,155 @@
         sum_copies[i].wait_recv()
         total[i + 1] = total[i] + got_sum[i]
 
-    total[0] = sums_ref[...]
-    core_copies = [core_send(c) for c in range(len(chunks))]
-    load_copies = {c: core_load(c) for c in range(2)}
-    ticks = len(chunks) + levels
-    for tick in range(ticks + 1):
-        if tick < len(sum_peers):
-            sum_start(tick)
-        for stage in range(levels, -1, -1):
-            c = tick - stage
-            if 0 <= c < len(chunks):
-                if stage == 0:
-                    core_add(c)
-                else:
-                    chip_add(c, stage - 1)
-        if tick < len(sum_peers):
-            sum_finish(tick)
-        c = tick - levels - 1
-        if 0 <= c < len(chunks) and chunks[c][1] == 0:
-            finish(chunks[c][0])
+    total[0] = jnp.zeros_like(total[0])
+    depth = SPACING * (levels + 1) + 2
+    feed_last = count // 2 - 2
+    cross_last = 3 * count // 4 - 1
+    state = {}
+    for tick in range(count + max(depth, len(sum_peers) + 3)):
+        c = tick - depth
+        if 0 <= c < count:
+            finish(c)
+        for level in range(levels - 1, -1, -1):
+            c = tick - SPACING * (level + 2)
+            if 0 <= c < count:
+                chip_add(c, level)
+        c = tick - SPACING
+        if 0 <= c < count:
+            core_add(c)
+        if tick in unit_at:
+            run_unit(tick)
+        if tick < count:
+            core_send(tick)
+        if tick == feed_last:
+            state["res"] = to_positions(res_ref, res_out, lr, zr_send, zr_recv)
+        if tick == cross_last:
+            state["ded"] = to_positions(ded_ref, zrx_enc, le, ze_send, ze_recv)
+        if tick == cross_last + 2:
+            positions_here(state["ded"], ded_ref, zrx_enc, le, ze_send, ze_recv)
+            state["enc"] = to_inputs(zrx_enc, sb_enc, rx_enc, enc_send, enc_recv)
+        if tick == count - 1:
+            state["dx"] = to_positions(dx_ref, zrx_tok, lr, zt_send, zt_recv)
+        if tick == count + 1:
+            positions_here(state["dx"], dx_ref, zrx_tok, lr, zt_send, zt_recv)
+            state["tok"] = to_inputs(zrx_tok, sb_tok, rx_tok, tok_send, tok_recv)
+        i = tick - count
+        if 0 <= i - 1 < len(sum_peers):
+            sum_finish(i - 1)
+        if 0 <= i < len(sum_peers):
+            sum_start(i)
     norm_ref[...] = total[len(sum_peers)]
+    positions_here(state["res"], res_ref, res_out, lr, zr_send, zr_recv)
+    inputs_here(state["enc"])
+    inputs_here(state["tok"])
     for copy in started:
         copy.wait_send()
 
 
-def reduce_grads(dws, dwc, dwi, dwo, sums, ndp, nt):
-    dim, width = dws.shape[1:]
+def back(ndp, nt, spd, tok_lens, enc_lens, back_slot, wg, kept, norms):
+    x, ed, cot, n1, q1, k1, v1, o1, h1, n2, q2, k2, v2, o2, h2 = kept
+    _, _, dim, width = wg.shape
+    _, seq, _ = x.shape
+    enc = ed.shape[1]
+    lr, le = seq // nt, enc // nt
+    seqs = spd * nt
+    n, m = spd * seq, spd * enc
+    hc = width // 4
     rows, chips = dim // ndp, ndp // 2
+    half = rows // 2
     levels = chips.bit_length() - 1
     count = 4 * nt
     steps = (ndp.bit_length() - 1) + (nt.bit_length() - 1)
-    view = (nt, chips, 2, rows, width)
+    slots = 1 + 2 * (chips - 1)
+    smem = pl.BlockSpec(memory_space=pltpu.SMEM)
+    vmem = pl.BlockSpec(memory_space=pltpu.VMEM)
     any_space = pl.BlockSpec(memory_space=pl.ANY)
-    vmem = pl.BlockSpec(memory_space=pltpu.VMEM)
-    slots = 1 + 2 * (chips - 1)
+    dma = pltpu.SemaphoreType.DMA
+    shape = jax.ShapeDtypeStruct
+
+    def like(a):
+        return pltpu.VMEM(a.shape, a.dtype)
+
     return pl.pallas_call(
-        functools.partial(reduce_kernel, ndp, nt),
-        in_specs=[any_space] * 4 + [vmem],
-        out_specs=[vmem, vmem],
+        functools.partial(back_kernel, ndp, nt, spd),
+        in_specs=[smem] * 3 + [any_space] * 16 + [vmem],
+        out_specs=[any_space] * 3 + [vmem] * 2,
         out_shape=[
-            jax.ShapeDtypeStruct((4, rows, width), F32),
-            jax.ShapeDtypeStruct(sums.shape, F32),
+            shape((seqs, lr, dim), BF16),
+            shape((ndp, lr, dim), BF16),
+            shape((ndp, le, dim), BF16),
+            shape((4, rows, width), F32),
+            shape((8, dim), F32),
         ],
         scratch_shapes=[
-            pltpu.VMEM((count, chips, rows, width), BF16),
-            pltpu.VMEM((count, 2 * (chips - 1), rows // 2, width), BF16),
+            *[like(a) for a in (h2, cot, h1, n2, ed, q2, k2, v2, o2, x, n1, q1, k1, v1, o1)],
+            pltpu.VMEM((n, dim), BF16),
+            pltpu.VMEM((dim, n), BF16),
+            pltpu.VMEM((n, dim), BF16),
+            pltpu.VMEM((dim, n), BF16),
+            pltpu.VMEM((dim, m), BF16),
+            pltpu.VMEM((n, dim), F32),
+            pltpu.VMEM((n, dim), F32),
+            pltpu.VMEM((m, dim), F32),
+            pltpu.VMEM((n, dim), F32),
+            pltpu.VMEM((spd, seq, dim), BF16),
+            pltpu.VMEM((spd, seq, dim), BF16),
+            pltpu.VMEM((spd, enc, dim), BF16),
+            pltpu.VMEM((n, 3 * hc), BF16),
+            pltpu.VMEM((m, hc), BF16),
+            pltpu.VMEM((m, hc), BF16),
+            pltpu.VMEM((4, dim, width), BF16),
+            pltpu.VMEM((seqs, lr, dim), BF16),
+            pltpu.VMEM((seqs, le, dim), BF16),
+            pltpu.VMEM((ndp, lr, dim), BF16),
+            pltpu.VMEM((ndp, le, dim), BF16),
+            pltpu.VMEM((DW_SLOTS, chips, 2, rows, width), BF16),
+            pltpu.VMEM((CORE_SLOTS, chips, rows, width), BF16),
+            pltpu.VMEM((CHIP_SLOTS, 2 * (chips - 1), half, width), BF16),
             pltpu.VMEM((4, nt - 1, rows, width), BF16),
-            pltpu.VMEM((steps,) + sums.shape, F32),
-            pltpu.VMEM((2, chips, rows, width), BF16),
-            pltpu.VMEM((levels, chips, rows, width), BF16),
-            pltpu.VMEM((count, rows, width), BF16),
-            pltpu.VMEM((steps + 1,) + sums.shape, F32),
-            pltpu.SemaphoreType.DMA((2,)),
-            pltpu.SemaphoreType.DMA((count, slots)),
-            pltpu.SemaphoreType.DMA((count, slots)),
-            pltpu.SemaphoreType.DMA((4, nt - 1)),
-            pltpu.SemaphoreType.DMA((4, nt - 1)),
-            pltpu.SemaphoreType.DMA((steps,)),
-            pltpu.SemaphoreType.DMA((steps,)),
+            pltpu.VMEM((SPACING * levels, chips, rows, width), BF16),
+            pltpu.VMEM((Z_SLOTS, rows, width), BF16),
+            pltpu.VMEM((steps + 1, 8, dim), F32),
+            pltpu.VMEM((steps, 8, dim), F32),
+            dma((15,)),
+            dma((4,)),
+            dma((count, slots)),
+            dma((count, slots)),
+            dma((4, nt - 1)),
+            dma((4, nt - 1)),
+            dma((steps,)),
+            dma((steps,)),
+            *[dma((nt,)) for _ in range(6)],
+            *[dma((ndp,)) for _ in range(4)],
+            pltpu.SemaphoreType.REGULAR,
+            pltpu.SemaphoreType.REGULAR((levels, 2)),
         ],
         compiler_params=pltpu.CompilerParams(
             collective_id=1, has_side_effects=True, vmem_limit_bytes=VMEM_LIMIT
         ),
-        name="reduce_grads",
-    )(dws.reshape(view), dwc.reshape(view), dwi.reshape(view), dwo.reshape(view), sums)
+        name="back",
+    )(
+        tok_lens,
+        enc_lens,
+        back_slot,
+        wg,
+        x,
+        ed,
+        cot,
+        n1,
+        q1,
+        k1,
+        v1,
+        o1,
+        h1,
+        n2,
+        q2,
+        k2,
+        v2,
+        o2,
+        h2,
+        norms,
+    )
 
 
 def select_rows(lookup, positions):
@@ -1132,17 +1213,6 @@
     return jnp.einsum(
         "kj,jrd->krd", selector, value_entries, preferred_element_type=F32
     ).astype(BF16)
-
-
-def swap_dp(selector_out, selector_in, a):
-    sent = lax.all_to_all(
-        route_rows(selector_out, a), "dp", split_axis=0, concat_axis=0, tiled=True
-    )
-    return route_rows(selector_in, sent)
-
-
-def to_positions(a):
-    return lax.all_to_all(a, "tensor", split_axis=1, concat_axis=0, tiled=True)
 
 
 def per_device(
@@ -1178,7 +1248,6 @@
     targets = jnp.sum(jnp.where(deal[None, :] == slots[:, None], every[None, :], 0), axis=1)
     peers = jnp.arange(ndp, dtype=jnp.int32)
     outward = (targets[None, :] // seqs == peers[:, None]).astype(BF16)
-    inward = (sources[:, None] // seqs == peers[None, :]).astype(BF16)
     tok_lens = lax.dynamic_slice(select_rows(tok_len, sources), (t * spd,), (spd,))
     enc_lens = lax.dynamic_slice(select_rows(enc_len, sources), (t * spd,), (spd,))
 
@@ -1194,7 +1263,7 @@
         w_in,
         w_out,
     )
-    wg, x, ed, cot, n1, q1, k1, v1, o1, h1, n2, q2, k2, v2, o2, h2 = front(
+    wg, *kept = front(
         ndp,
         nt,
         spd,
@@ -1208,28 +1277,26 @@
         gain,
         bias,
     )
-    x, ed, cot = x.reshape(-1, dim), ed.reshape(-1, dim), cot.reshape(-1, dim)
-    res, dh2, sums3, dwi, dwo = feed(tok_lens, h2, cot, gain, bias, wg, spd, nt)
-    ded, dh1, sums2, dwc = cross_bwd(
-        enc_lens, dh2, h1, n2, ed, gain, q2, k2, v2, o2, wg, spd, nt
+    back_slot = jnp.sum(
+        jnp.where(
+            sources[None, :] // seqs == peers[:, None],
+            jnp.arange(seqs, dtype=jnp.int32)[None, :],
+            0,
+        ),
+        axis=1,
     )
-    dx, sums1, dws = self_bwd(tok_lens, dh1, x, n1, gain, q1, k1, v1, o1, wg, spd, nt)
-
-    sums = jnp.concatenate(
-        [sums1[:1], sums2[:1], sums3[:1], sums1[1:], sums2[1:], sums3[1:], jnp.zeros((2, dim), F32)]
+    norms = jnp.concatenate([gain, bias, jnp.zeros((2, dim), F32)])
+    res, tok_grads, enc_grads, grads, norm = back(
+        ndp, nt, spd, tok_lens, enc_lens, back_slot, wg, kept, norms
     )
-    grads, norm = reduce_grads(dws, dwc, dwi, dwo, sums, ndp, nt)
-
-    def back(a):
-        return swap_dp(inward.T, outward.T, to_positions(a.reshape(spd, -1, dim)))
 
     def attention(g):
         return (g[:, :hc], g[:, hc : 2 * hc], g[:, 2 * hc : 3 * hc], g[:, 3 * hc :].T)
 
     return (
-        to_positions(res.reshape(spd, -1, dim)),
-        back(dx),
-        back(ded),
+        res,
+        route_rows(outward.T, tok_grads),
+        route_rows(outward.T, enc_grads),
         *attention(grads[0]),
         *attention(grads[1]),
         grads[2],

time: 490 us -> 387 us (0.79)
  waiting for transfers between devices: 39.9 us -> 0 us
  Pallas kernels: 394 us -> 359 us
  starting transfers between devices: 18.8 us -> 0 us
  local copies, waits for them, and re-layouts: 24.4 us -> 13.8 us
    all_to_all x5 -> x0, waiting for transfers between devices: 39.9 us -> none  [the longest x3 27 us: to_positions(): return lax.all_to_all(a, 'tensor', split_axis=1, concat_axis=0, tiled=True)]
    pallas_call x4 -> x1, Pallas kernels: 227 us -> 191 us  [back(): pl.pallas_call(functools.partial(back_kernel, ndp, nt, spd), in_specs=[sm...]
    all_to_all x5 -> x0, starting transfers between devices: 18.8 us -> none  [the longest x3 10.9 us: to_positions(): return lax.all_to_all(a, 'tensor', split_axis=1, concat_axis=0, tiled=True)]
    reshape x3 -> x0, local copies, waits for them, and re-layouts: 5.87 us -> none  [the longest x2 4.54 us: back(): return swap_dp(inward.T, outward.T, to_positions(a.reshape(spd, -1, dim)))]
  transfers between devices with their start and end apart: 5 -> 0, of which waited for: 4 -> 0; matrix products, arithmetic and copies ran while one was open for 4% -> 0% of each run, Pallas kernels for 35% -> 0%
where the time goes in v3:
time: 387 us; the launch traced here: 384 us
  Pallas kernels  359 us (93%)
  local copies, waits for them, and re-layouts  13.8 us (4%)
  matrix products  5.76 us (1%)
  other arithmetic  3.88 us (1%)
    pallas_call x1, Pallas kernels, back(): pl.pallas_call(functools.partial(back_kernel, ndp, nt, spd), in_specs=[sm...  191 us
    pallas_call x1, Pallas kernels, front(): pl.pallas_call(body, in_specs=[smem] * 3 + [any_space] * 13 + [vmem] * 2,...  168 us

profile of v3, /device:TPU:0, one launch (start us, length us, event | category | flops | bytes accessed | tf_op | source)
XLA Modules:
  0.0 383.8 jit_solution(8142360049120370666)
XLA Ops:
  0.6 0.0 copy-start
  0.7 0.1 pad.2.clone
  0.8 0.9 select_reduce_fusion
  1.7 0.0 copy-start.4
  1.7 0.6 select_reduce_fusion.1.back_slot
  2.4 0.9 select_reduce_fusion.2
  3.2 0.6 dynamic_slice.7.refs_1_.enc_lens
  3.8 0.6 dynamic_slice.6.refs_0_.tok_lens
  4.4 1.4 maximum_maximum_fusion.gain
  5.8 1.5 fusion.4
  7.4 1.1 copy.74.refs_3_
  8.5 0.0 copy-done
  8.5 0.8 fusion.1
  9.3 0.0 copy-done.4
  9.3 1.5 copy.73.refs_4_
  10.8 167.8 %front.1 = (bf16[4,4,1024,1024]{3,2,1,0:T(8,128)(2,1)}, bf16[2,128,1024]{2,1,0:T(8,128)(2,1)}, bf16[2,256,1024]{2,1,0:T(8,128)(2,1)}, bf16[2,128,1024]{2,1,0:T(8...) custom-call(s32[2]{0:T(128)} %dynamic_slice.6.refs_0_.tok_lens, ...), custom_call_target="tpu_custom_call" | custom-call | tf_op jit(solution)/shard_map/front/pallas_call | solution.py:498
  178.6 191.3 %back.1 = (bf16[8,32,1024]{2,1,0:T(8,128)(2,1)}, bf16[8,32,1024]{2,1,0:T(8,128)(2,1)}, bf16[8,64,1024]{2,1,0:T(8,128)(2,1)}, f32[4,128,1024]{2,1,0:T(8,128)}, f32[8,1024]{1,0:T(8,128)}) custom-call(s32[2]{0:T(128)} %dynamic_slice.6.refs_0_.tok_lens, s32[2]{0:T(128)} %dynamic_slice.7.refs_1_.enc_lens, s32[8]{0:T(128)} %select_reduce_fusion.1.back_slot, ...), custom_call_target="tpu_custom_call" | custom-call | tf_op jit(solution)/shard_map/back/pallas_call | solution.py:1125
  369.9 1.5 fusion.15
  371.3 1.5 convolution_convert_fusion.1
  372.8 2.0 convolution_convert_fusion
  374.8 0.0 copy-start.2
  374.8 1.5 copy.55
  376.3 1.1 copy.54
  377.4 0.0 copy-done.2
  377.4 1.0 slice_bitcast_fusion
  378.4 0.0 copy-start.3
  378.4 0.0 copy-start.1
  378.5 1.0 copy.58
  379.4 0.8 slice_bitcast_fusion.4
  380.2 0.8 copy.57
  381.0 0.8 slice_bitcast_fusion.5
  381.7 0.8 copy.56
  382.5 0.0 copy-done.3
  382.5 0.8 copy.76
  383.3 0.0 copy-done.1
  (3 shorter events, 0.0 us)
Async XLA Ops:
  0.6 7.8 %copy-start = (bf16[8,64,1024]{2,1,0:T(8,128)(2,1)S(1)}, bf16[8,64,1024]{2,1,0:T(8,128)(2,1)}, u32[]{:S(2)}) copy-start(bf16[8,64,1024]{2,1,0:T(8,128)(2,1)} %param.19) | copy-start | bytes 3145732
  1.7 7.5 %copy-start.4 = (s32[8]{0:T(128)}, s32[8]{0:T(128)S(1)}, u32[]{:S(2)}) copy-start(s32[8]{0:T(128)S(1)} %get-tuple-element.106.refs_2_) | copy-start | bytes 100
  374.8 2.6 copy-start.2
  378.4 4.0 %copy-start.3 = (bf16[8,32,1024]{2,1,0:T(8,128)(2,1)S(1)}, bf16[8,32,1024]{2,1,0:T(8,128)(2,1)}, u32[]{:S(2)}) copy-start(bf16[8,32,1024]{2,1,0:T(8,128)(2,1)} %get-tuple-element.122) | copy-start | bytes 1572868
  378.4 4.8 %copy-start.1 = (bf16[8,64,1024]{2,1,0:T(8,128)(2,1)S(1)}, bf16[8,64,1024]{2,1,0:T(8,128)(2,1)}, u32[]{:S(2)}) copy-start(bf16[8,64,1024]{2,1,0:T(8,128)(2,1)} %param.19) | copy-start | bytes 3145732

commit v4 on v3

--- a/solution.py
+++ b/solution.py
@@ -13,6 +13,8 @@
 EPSILON = 1e-05
 MESH = pl.DeviceIdType.MESH
 VMEM_LIMIT = 60 * 1024 * 1024
+SPACING = 2
+Z_LEAD = 2
 BF16 = jnp.bfloat16
 F32 = jnp.float32
 
@@ -126,11 +128,11 @@
     ndp,
     nt,
     spd,
-    tok_lens,
-    enc_lens,
-    in_peer,
-    tok_blocks,
-    enc_blocks,
+    deal_ref,
+    tok_len_ref,
+    enc_len_ref,
+    tok_ref,
+    enc_ref,
     cot_ref,
     w_refs,
     gain,
@@ -151,6 +153,8 @@
     v2_ref,
     o2_ref,
     h2_ref,
+    tx_tok,
+    tx_enc,
     rx_tok,
     rx_enc,
     zs_tok,
@@ -188,10 +192,13 @@
     orders = (chip_bits, chip_bits[::-1])
     levels = len(chip_bits)
     seqs, lr = cot_ref.shape[0], cot_ref.shape[1]
-    le = enc_blocks.shape[1]
+    le = enc_ref.shape[1]
     seq, enc = nt * lr, nt * le
     n, m = spd * seq, spd * enc
     waits = []
+    sources = [deal_ref[d * seqs + i] for i in range(seqs)]
+    tok_lens = [tok_len_ref[deal_ref[d * seqs + t * spd + i]] for i in range(spd)]
+    enc_lens = [enc_len_ref[deal_ref[d * seqs + t * spd + i]] for i in range(spd)]
 
     def dp_peer(bit):
         return (flip(d, bit), t)
@@ -225,15 +232,26 @@
         copy.start()
         return copy
 
+    tok_load = local(tok_ref, zs_tok, load_sems.at[10])
+    enc_load = local(enc_ref, zs_enc, load_sems.at[11])
+    out_slot = []
+    for k in range(ndp):
+        slot = 0
+        for i in range(seqs):
+            slot = jnp.where(deal_ref[k * seqs + i] == d * seqs + i, i, slot)
+        out_slot.append(slot)
     greet([dp_peer(e) for e in range(1, ndp)] + [t_peer(j) for j in range(1, nt)])
 
-    def to_peers(blocks, rx, ssem, rsem):
+    def to_peers(load, held, blocks, rx, ssem, rsem):
+        load.wait()
+        for k in range(ndp):
+            blocks[k] = held[out_slot[k]]
         return [
             send(blocks.at[flip(d, e)], rx.at[d], ssem.at[e], rsem.at[e], dp_peer(e))
             for e in range(1, ndp)
         ], local(blocks.at[d], rx.at[d], rsem.at[0])
 
-    tok_copies, tok_own = to_peers(tok_blocks, rx_tok, tok_send, tok_recv)
+    tok_copies, tok_own = to_peers(tok_load, zs_tok, tx_tok, rx_tok, tok_send, tok_recv)
 
     wq1, wk1, wv1, wo1, wq2, wk2, wv2, wo2, w_in, w_out = w_refs
     loads = [
@@ -312,9 +330,7 @@
 
     def spread(c, level):
         g, j = chunks[c]
-        if level == 0:
-            arrived(c)
-        else:
+        if level:
             for copy in pending.pop((c, level)):
                 copy.wait_recv()
         slot = 1 + 2 * ((1 << level) - 1)
@@ -383,7 +399,7 @@
         for copy in copies:
             copy.wait_recv()
         for i in range(seqs):
-            zs[i] = rx[in_peer[i]]
+            zs[i] = rx[lax.div(sources[i], seqs)]
 
     def self_norm():
         x = x_ref[...].reshape(n, dim).astype(F32)
@@ -428,7 +444,7 @@
     on_line(start, 0)
     blocks_here(tok_copies, tok_own, rx_tok, zs_tok)
     own_x = to_sequences(zs_tok, x_ref, lr, zt_send, zt_recv)
-    enc_copies, enc_own = to_peers(enc_blocks, rx_enc, enc_send, enc_recv)
+    enc_copies, enc_own = to_peers(enc_load, zs_enc, tx_enc, rx_enc, enc_send, enc_recv)
     for i in range(4, 10):
         loads[i].wait()
     own[1, :, 3 * hc :] = raw_o[1].T
@@ -438,24 +454,34 @@
     own_copy = local(own, wg.at[0], own_sem)
 
     state = {}
-    ready = levels + 1
     count = len(chunks)
     per = nt - 1
-    for tick in range(count + ready):
-        for level in range(ready + 1):
-            c = tick - level
+    stage_at = [SPACING * level for level in range(levels + 1)]
+    stage_at.append(stage_at[-1] + 1)
+
+    def line_stage(c):
+        arrived(c)
+        if c % per == 0 and c // per + 1 < 4:
+            on_line(start, c // per + 1)
+
+    for c in range(min(Z_LEAD, count)):
+        line_stage(c)
+    part_at = stage_at[-1] + 1
+    for tick in range(count + part_at):
+        if tick + Z_LEAD < count:
+            line_stage(tick + Z_LEAD)
+        for level in range(levels + 1, -1, -1):
+            c = tick - stage_at[level]
             if 0 <= c < count:
                 spread(c, level)
-                if level == 0 and c % per == 0 and c // per + 1 < 4:
-                    on_line(start, c // per + 1)
         if tick == 0:
             blocks_here(enc_copies, enc_own, rx_enc, zs_enc)
             own_ed = to_sequences(zs_enc, ed_ref, le, ze_send, ze_recv)
-        if tick == 2:
+        if tick == 1:
             sequences_here(own_x, zs_tok, x_ref, lr, zt_send, zt_recv)
             self_norm()
             self_part(0, own.at[0])
-        c = tick - ready - 1
+        c = tick - part_at
         if 0 <= c < 2 * per:
             g, j = chunks[c]
             fills[c].wait()
@@ -476,9 +502,9 @@
         copy.wait_send()
 
 
-def front(ndp, nt, spd, tok_lens, enc_lens, in_peer, tok_blocks, enc_blocks, cot, weights, gain, bias):
+def front(ndp, nt, spd, deal, tok_len, enc_len, tokens, enc_states, cot, weights, gain, bias):
     seqs, lr, dim = cot.shape
-    le = enc_blocks.shape[1]
+    le = enc_states.shape[1]
     seq, enc = nt * lr, nt * le
     n, m = spd * seq, spd * enc
     hc = weights[0].shape[1]
@@ -520,13 +546,15 @@
         scratch_shapes=[
             pltpu.VMEM((ndp, lr, dim), BF16),
             pltpu.VMEM((ndp, le, dim), BF16),
+            pltpu.VMEM((ndp, lr, dim), BF16),
+            pltpu.VMEM((ndp, le, dim), BF16),
             pltpu.VMEM((seqs, lr, dim), BF16),
             pltpu.VMEM((seqs, le, dim), BF16),
             pltpu.VMEM((4, dim, width), BF16),
             pltpu.VMEM((2, hc, dim), BF16),
             pltpu.VMEM((width, dim), BF16),
             pltpu.VMEM((2, dim, width), BF16),
-            dma((10,)),
+            dma((12,)),
             dma,
             dma((2,)),
             dma((ndp,)),
@@ -548,23 +576,22 @@
             collective_id=0, has_side_effects=True, vmem_limit_bytes=VMEM_LIMIT
         ),
         name="front",
-    )(tok_lens, enc_lens, in_peer, tok_blocks, enc_blocks, cot, *weights, gain, bias)
+    )(deal, tok_len, enc_len, tokens, enc_states, cot, *weights, gain, bias)
 
 
 CORE_SLOTS = 4
 CHIP_SLOTS = 4
 DW_SLOTS = 3
 Z_SLOTS = 4
-SPACING = 2
 
 
 def back_kernel(
     ndp,
     nt,
     spd,
-    tok_lens,
-    enc_lens,
-    back_slot,
+    deal_ref,
+    tok_len_ref,
+    enc_len_ref,
     wg,
     x_hbm,
     ed_hbm,
@@ -582,6 +609,7 @@
     o2_hbm,
     h2_hbm,
     gain,
+    bias,
     res_out,
     rx_tok,
     rx_enc,
@@ -671,6 +699,9 @@
     seq, enc = nt * lr, nt * le
     n, m = spd * seq, spd * enc
     started = []
+    sources = [deal_ref[d * seqs + i] for i in range(seqs)]
+    tok_lens = [tok_len_ref[deal_ref[d * seqs + t * spd + i]] for i in range(spd)]
+    enc_lens = [enc_len_ref[deal_ref[d * seqs + t * spd + i]] for i in range(spd)]
 
     def dp_peer(bit):
         return (flip(d, bit), t)
@@ -764,7 +795,7 @@
     def feed_init():
         loaded(0, 2)
         nh, _ = norm_parts(h2_ref[...])
-        v = nh * gain[2:3] + gain[5:6]
+        v = nh * gain[2:3] + bias[2:3]
         low[...] = v.astype(BF16)
         low_t[...] = v.T.astype(BF16)
         keep = row_valid(tok_lens, spd, n)
@@ -1029,7 +1060,10 @@
 
     def to_inputs(zrx, sb, rx, ssem, rsem):
         for k in range(ndp):
-            sb[k] = zrx[back_slot[k]]
+            slot = 0
+            for i in range(seqs):
+                slot = jnp.where(lax.div(sources[i], seqs) == k, i, slot)
+            sb[k] = zrx[slot]
         copies = [
             send(sb.at[flip(d, e)], rx.at[d], ssem.at[e], rsem.at[e], dp_peer(e))
             for e in range(1, ndp)
@@ -1098,7 +1132,7 @@
         copy.wait_send()
 
 
-def back(ndp, nt, spd, tok_lens, enc_lens, back_slot, wg, kept, norms):
+def back(ndp, nt, spd, deal, tok_len, enc_len, wg, kept, gain, bias):
     x, ed, cot, n1, q1, k1, v1, o1, h1, n2, q2, k2, v2, o2, h2 = kept
     _, _, dim, width = wg.shape
     _, seq, _ = x.shape
@@ -1124,7 +1158,7 @@
 
     return pl.pallas_call(
         functools.partial(back_kernel, ndp, nt, spd),
-        in_specs=[smem] * 3 + [any_space] * 16 + [vmem],
+        in_specs=[smem] * 3 + [any_space] * 16 + [vmem] * 2,
         out_specs=[any_space] * 3 + [vmem] * 2,
         out_shape=[
             shape((seqs, lr, dim), BF16),
@@ -1181,9 +1215,9 @@
         ),
         name="back",
     )(
-        tok_lens,
-        enc_lens,
-        back_slot,
+        deal,
+        tok_len,
+        enc_len,
         wg,
         x,
         ed,
@@ -1200,110 +1234,59 @@
         v2,
         o2,
         h2,
-        norms,
-    )
-
-
-def select_rows(lookup, positions):
-    matches = positions[:, None] == jnp.arange(lookup.shape[0], dtype=jnp.int32)[None, :]
-    return jnp.sum(jnp.where(matches, lookup[None, :], 0), axis=1)
-
-
-def route_rows(selector, value_entries):
-    return jnp.einsum(
-        "kj,jrd->krd", selector, value_entries, preferred_element_type=F32
-    ).astype(BF16)
-
-
-def per_device(
-    ndp,
-    nt,
-    tokens,
-    enc_states,
-    cotangent,
-    tok_len,
-    enc_len,
-    deal,
-    w_q_self,
-    w_k_self,
-    w_v_self,
-    w_o_self,
-    w_q_cross,
-    w_k_cross,
-    w_v_cross,
-    w_o_cross,
-    w_in,
-    w_out,
-    gain,
-    bias,
-):
-    d = lax.axis_index("dp")
-    t = lax.axis_index("tensor")
-    seqs, _, dim = tokens.shape
-    spd = seqs // nt
-    hc = w_q_self.shape[1]
-    slots = d * seqs + jnp.arange(seqs, dtype=jnp.int32)
-    sources = select_rows(deal, slots)
-    every = jnp.arange(deal.shape[0], dtype=jnp.int32)
-    targets = jnp.sum(jnp.where(deal[None, :] == slots[:, None], every[None, :], 0), axis=1)
-    peers = jnp.arange(ndp, dtype=jnp.int32)
-    outward = (targets[None, :] // seqs == peers[:, None]).astype(BF16)
-    tok_lens = lax.dynamic_slice(select_rows(tok_len, sources), (t * spd,), (spd,))
-    enc_lens = lax.dynamic_slice(select_rows(enc_len, sources), (t * spd,), (spd,))
-
-    weights = (
-        w_q_self,
-        w_k_self,
-        w_v_self,
-        w_o_self,
-        w_q_cross,
-        w_k_cross,
-        w_v_cross,
-        w_o_cross,
-        w_in,
-        w_out,
-    )
-    wg, *kept = front(
-        ndp,
-        nt,
-        spd,
-        tok_lens,
-        enc_lens,
-        sources // seqs,
-        route_rows(outward, tokens),
-        route_rows(outward, enc_states),
-        cotangent,
-        weights,
         gain,
         bias,
     )
-    back_slot = jnp.sum(
-        jnp.where(
-            sources[None, :] // seqs == peers[:, None],
-            jnp.arange(seqs, dtype=jnp.int32)[None, :],
-            0,
-        ),
-        axis=1,
+
+
+def tail_kernel(seqs, deal_ref, res, rx_tok, rx_enc, grads, norm, *outs):
+    d = lax.axis_index("dp")
+    result, d_tok, d_enc = outs[:3]
+    hc = outs[3].shape[1]
+    result[...] = res[...]
+    for i in range(seqs):
+        peer = 0
+        for k in range(rx_tok.shape[0]):
+            peer = jnp.where(deal_ref[k * seqs + i] == d * seqs + i, k, peer)
+        d_tok[i] = rx_tok[peer]
+        d_enc[i] = rx_enc[peer]
+    for g in range(2):
+        for i in range(3):
+            outs[3 + 4 * g + i][...] = grads[g, :, i * hc : (i + 1) * hc]
+        outs[6 + 4 * g][...] = grads[g, :, 3 * hc :].T
+    outs[11][...] = grads[2]
+    outs[12][...] = grads[3].T
+    outs[13][...] = norm[0:3]
+    outs[14][...] = norm[3:6]
+
+
+def tail(deal, res, rx_tok, rx_enc, grads, norm):
+    seqs, lr, dim = res.shape
+    le = rx_enc.shape[1]
+    rows, width = grads.shape[1:]
+    hc = width // 4
+    vmem = pl.BlockSpec(memory_space=pltpu.VMEM)
+    straight, turned = ((rows, hc), F32), ((hc, rows), F32)
+    shapes = [((seqs, lr, dim), BF16), ((seqs, lr, dim), BF16), ((seqs, le, dim), BF16)]
+    shapes += ([straight] * 3 + [turned]) * 2
+    shapes += [((rows, width), F32), ((width, rows), F32), ((3, dim), F32), ((3, dim), F32)]
+    return pl.pallas_call(
+        functools.partial(tail_kernel, seqs),
+        in_specs=[pl.BlockSpec(memory_space=pltpu.SMEM)] + [vmem] * 5,
+        out_specs=[vmem] * len(shapes),
+        out_shape=[jax.ShapeDtypeStruct(*one) for one in shapes],
+        compiler_params=pltpu.CompilerParams(vmem_limit_bytes=VMEM_LIMIT),
+        name="tail",
+    )(deal, res, rx_tok, rx_enc, grads, norm)
+
+
+def per_device(ndp, nt, tokens, enc_states, cotangent, tok_len, enc_len, deal, *rest):
+    *weights, gain, bias = rest
+    spd = tokens.shape[0] // nt
+    wg, *kept = front(
+        ndp, nt, spd, deal, tok_len, enc_len, tokens, enc_states, cotangent, weights, gain, bias
     )
-    norms = jnp.concatenate([gain, bias, jnp.zeros((2, dim), F32)])
-    res, tok_grads, enc_grads, grads, norm = back(
-        ndp, nt, spd, tok_lens, enc_lens, back_slot, wg, kept, norms
-    )
-
-    def attention(g):
-        return (g[:, :hc], g[:, hc : 2 * hc], g[:, 2 * hc : 3 * hc], g[:, 3 * hc :].T)
-
-    return (
-        res,
-        route_rows(outward.T, tok_grads),
-        route_rows(outward.T, enc_grads),
-        *attention(grads[0]),
-        *attention(grads[1]),
-        grads[2],
-        grads[3].T,
-        norm[0:3],
-        norm[3:6],
-    )
+    return tail(deal, *back(ndp, nt, spd, deal, tok_len, enc_len, wg, kept, gain, bias))
 
 
 def solution(mesh):

time: 387 us -> 397 us (1.026)
  Pallas kernels: 359 us -> 390 us
  local copies, waits for them, and re-layouts: 13.8 us -> 0 us
  matrix products: 5.76 us -> 0 us
    pallas_call x1, Pallas kernels: 168 us -> 194 us  [front(): pl.pallas_call(body, in_specs=[smem] * 3 + [any_space] * 13 + [vmem] * 2,...]
    unnamed x16 -> x0, local copies, waits for them, and re-layouts: 5.96 us -> none
    dot_general x4 -> x0, matrix products: 5.76 us -> none  [route_rows(): jnp.einsum('kj,jrd->krd', selector, value_entries, preferred_element_type...]
    pallas_call x0 -> x1, Pallas kernels: none -> 4.45 us  [tail(): pl.pallas_call(functools.partial(tail_kernel, seqs), in_specs=[pl.BlockSp...]
where the time goes in v4:
time: 397 us; the launch traced here: 391 us
  Pallas kernels  390 us (98%)
    pallas_call x1, Pallas kernels, front(): pl.pallas_call(body, in_specs=[smem] * 3 + [any_space] * 13 + [vmem] * 2,...  194 us
    pallas_call x1, Pallas kernels, back(): pl.pallas_call(functools.partial(back_kernel, ndp, nt, spd), in_specs=[sm...  192 us

profile of v4, /device:TPU:0, one launch (start us, length us, event | category | flops | bytes accessed | tf_op | source)
XLA Modules:
  0.0 391.3 jit_solution(2226474587017198428)
XLA Ops:
  0.7 194.2 %front.1 = (bf16[4,4,1024,1024]{3,2,1,0:T(8,128)(2,1)}, bf16[2,128,1024]{2,1,0:T(8,128)(2,1)}, bf16[2,256,1024]{2,1,0:T(8,128)(2,1)}, bf16[2,128,1024]{2,1,0:T(8...) custom-call(s32[64]{0:T(128)} %deal_ref.3, ...), custom_call_target="tpu_custom_call" | custom-call | tf_op jit(solution)/shard_map/front/pallas_call | solution.py:524
  194.8 191.8 %back.1 = (bf16[8,32,1024]{2,1,0:T(8,128)(2,1)}, bf16[8,32,1024]{2,1,0:T(8,128)(2,1)}, bf16[8,64,1024]{2,1,0:T(8,128)(2,1)}, f32[4,128,1024]{2,1,0:T(8,128)}, f32[8,1024]{1,0:T(8,128)}) custom-call(s32[64]{0:T(128)} %deal_ref.3, s32[64]{0:T(128)} %tok_len_ref.1, s32[64]{0:T(128)} %enc_len_ref.1, bf16[4,4,1024,1024]{3,2,1,0:T(8,128)(2,1)} %get-tuple-element.36.wg, ...), custom_call_target="tpu_custom_call" | custom-call | tf_op jit(solution)/shard_map/back/pallas_call | solution.py:1159
  386.6 4.5 %tail.1 = (bf16[8,32,1024]{2,1,0:T(8,128)(2,1)}, bf16[8,32,1024]{2,1,0:T(8,128)(2,1)}, bf16[8,64,1024]{2,1,0:T(8,128)(2,1)}, f32[128,256]{1,0:T(8,128)}, f32[128...) custom-call(s32[64]{0:T(128)} %deal_ref.3, ...), custom_call_target="tpu_custom_call" | custom-call | tf_op jit(solution)/shard_map/tail/pallas_call | solution.py:1273
